TPU v7x, 256 devices: a whole 4x4x8 slice. The times are simulated.
256 devices in a mesh: doc: 16 (over z_lo, x), head: 8 (over z_hi, y), cuts: 2 (over core).
Axes of the slice: x: 4, y: 4, z: 8 (z_hi: 2, z_lo: 4; z = z_hi * 4 + z_lo), core: 2. Of those that a mesh axis runs over, the one named last changes fastest.
Arguments:
- inputs: bfloat16 [2, 16, 256, 4096], P('cuts', 'doc'), may hold values from -9 to 9
- weight_query: bfloat16 [4096, 2048], P(None, 'head'), may hold values from -1 to 1
- weight_key: bfloat16 [4096, 2048], P(None, 'head'), may hold values from -2 to 2
- weight_value: bfloat16 [4096, 2048], P(None, 'head'), may hold values from -0.09375 to 0.09375
- grad_output: bfloat16 [2, 16, 256, 2048], P('cuts', 'doc', None, 'head'), may hold values from -24 to 24
- partner_one: int32 [2, 16], P('cuts'), may hold values from 0 to 15, each once within a row
- partner_two: int32 [2, 16], P('cuts'), may hold values from 0 to 15, each once within a row
Outputs:
- grad_key: bfloat16 [2, 16, 256, 2048], P('cuts', 'doc', None, 'head')
- grad_value: bfloat16 [2, 16, 256, 2048], P('cuts', 'doc', None, 'head')
- grad_weight_query: float32 [4096, 2048], P(('doc', 'cuts'), 'head')
- grad_weight_key: float32 [4096, 2048], P(('doc', 'cuts'), 'head')
- grad_weight_value: float32 [4096, 2048], P(('doc', 'cuts'), 'head')
- grad_input: bfloat16 [2, 16, 4096, 256], P('cuts', 'doc', 'head')
Inputs may be any that keep to these rules, and one draw needn't show every extreme that they name: `partner_one`: each row is a permutation of the documents 0 to 15 of the slice. `partner_two`: each row is a permutation of the documents 0 to 15 of the slice.
All inputs are finite; a program needn't handle non-finite values.
Results may differ from a plain program's by a relative error of at most 0.033.
Values may be sent and summed in bfloat16 or wider, within the bound.
No kernel may reach another device: no remote copies, remote signals or barrier semaphores. Data moves between devices by JAX's collectives and lax.ppermute only.
A program may use at most 128 MiB of HBM per device.

v0:
```python
import math

import jax
import jax.numpy as jnp
from jax import lax
from jax.sharding import PartitionSpec as P

HD = 128


def per_device(
    inputs, weight_query, weight_key, weight_value, grad_output, partner_one, partner_two
):
    tokens = inputs[0, 0]
    length = tokens.shape[0]
    columns = weight_query.shape[1]
    head_count = columns // HD
    factor = 1.0 / math.sqrt(HD)
    doc_peers = lax.axis_size("doc")
    block_rows = length // doc_peers
    myself = lax.axis_index("doc")
    first_partner = partner_one[0]
    second_partner = partner_two[0]
    queries = jnp.dot(tokens, weight_query, preferred_element_type=jnp.float32).astype(jnp.bfloat16)
    key_rows = jnp.dot(tokens, weight_key, preferred_element_type=jnp.float32).astype(jnp.bfloat16)
    value_rows = jnp.dot(tokens, weight_value, preferred_element_type=jnp.float32).astype(
        jnp.bfloat16
    )
    key_value = jnp.concatenate([key_rows, value_rows], axis=1)
    chosen = jnp.stack([first_partner[myself], second_partner[myself]])
    offsets = jnp.arange(length, dtype=jnp.int32)
    start_kv = jnp.zeros((2, length, 2 * columns), jnp.bfloat16)
    segment = lax.all_gather(key_value, "doc", axis=0, tiled=True)
    amount = segment.shape[0]
    slot_rows = []
    for which_one in range(2):
        positions = chosen[which_one] * length + offsets
        inside = (positions >= 0) & (positions < amount)
        picked = jnp.take(segment, jnp.clip(positions, 0, amount - 1), axis=0)
        slot_rows.append(jnp.where(inside[:, None], picked, start_kv[which_one]))
    partner_kv = jnp.stack(slot_rows)
    keys_all = jnp.concatenate(
        [key_rows, partner_kv[0, :, :columns], partner_kv[1, :, :columns]], axis=0
    )
    keys_all = keys_all.reshape(3 * length, head_count, HD)
    values_all = jnp.concatenate(
        [value_rows, partner_kv[0, :, columns:], partner_kv[1, :, columns:]], axis=0
    )
    values_all = values_all.reshape(3 * length, head_count, HD)
    query_heads = queries.reshape(length, head_count, HD)
    dout_rows = grad_output[0, 0]
    dout_heads = dout_rows.reshape(length, head_count, HD)
    scores = (
        jnp.einsum("qhe,khe->hqk", query_heads, keys_all, preferred_element_type=jnp.float32)
        * factor
    )
    row_index = lax.broadcasted_iota(jnp.int32, (length, 3 * length), 0)
    col_index = lax.broadcasted_iota(jnp.int32, (length, 3 * length), 1)
    allowed = (col_index >= length) | (col_index <= row_index)
    scores = jnp.where(allowed[None], scores, -jnp.inf)
    maximum = jnp.max(scores, axis=-1, keepdims=True)
    exponent = jnp.exp(scores - maximum)
    totals = jnp.sum(exponent, axis=-1, keepdims=True)
    probability = exponent / totals
    rounded = probability.astype(jnp.bfloat16)
    attended = jnp.einsum("hqk,khe->qhe", rounded, values_all, preferred_element_type=jnp.float32)
    row_delta = jnp.sum(dout_heads.astype(jnp.float32) * attended, axis=-1)
    prob_grad = jnp.einsum(
        "qhe,khe->hqk", dout_heads, values_all, preferred_element_type=jnp.float32
    )
    score_grad = (probability * (prob_grad - row_delta.T[:, :, None])).astype(jnp.bfloat16)
    grad_query = (
        jnp.einsum("hqk,khe->qhe", score_grad, keys_all, preferred_element_type=jnp.float32)
        * factor
    )
    grad_query = grad_query.astype(jnp.bfloat16).reshape(length, columns)
    doc_numbers = jnp.arange(doc_peers, dtype=jnp.int32)
    grad_keys = (
        jnp.einsum("hqk,qhe->khe", score_grad, query_heads, preferred_element_type=jnp.float32)
        * factor
    )
    grad_values = jnp.einsum(
        "hqk,qhe->khe", rounded, dout_heads, preferred_element_type=jnp.float32
    )
    both_grads = jnp.concatenate(
        [grad_keys.reshape(3 * length, columns), grad_values.reshape(3 * length, columns)], axis=1
    )
    own_grad = both_grads[:length]
    outbound = both_grads[length:].reshape(2, doc_peers, block_rows, 2 * columns)
    received = lax.all_to_all(
        outbound.astype(jnp.bfloat16), "doc", split_axis=1, concat_axis=1, tiled=True
    ).astype(outbound.dtype)
    chosen_one = (first_partner[:, None] == doc_numbers[None, :]).astype(jnp.float32)
    chosen_two = (second_partner[:, None] == doc_numbers[None, :]).astype(jnp.float32)
    gathered = jnp.einsum("dt,dbf->tbf", chosen_one, received[0], precision=lax.Precision.HIGHEST)
    gathered = gathered + jnp.einsum(
        "dt,dbf->tbf", chosen_two, received[1], precision=lax.Precision.HIGHEST
    )
    returned = (
        lax.all_to_all(
            gathered.astype(jnp.bfloat16), "doc", split_axis=0, concat_axis=0, tiled=True
        )
        .astype(gathered.dtype)
        .reshape(length, 2 * columns)
    )
    kv_grad = own_grad + returned
    grad_key = kv_grad[:, :columns].astype(jnp.bfloat16)
    grad_value = kv_grad[:, columns:].astype(jnp.bfloat16)
    all_grads = jnp.concatenate([grad_query, grad_key, grad_value], axis=1)
    shared = lax.psum_scatter(
        lax.dot_general(
            tokens, all_grads, (((0,), (0,)), ((), ())), preferred_element_type=jnp.float32
        ).astype(jnp.bfloat16),
        ("doc", "cuts"),
        scatter_dimension=0,
        tiled=True,
    ).astype(jnp.float32)
    numbers = (((1,), (1,)), ((), ()))
    result = lax.dot_general(weight_query, grad_query, numbers, preferred_element_type=jnp.float32)
    result = result + lax.dot_general(
        weight_key, grad_key, numbers, preferred_element_type=jnp.float32
    )
    result = result + lax.dot_general(
        weight_value, grad_value, numbers, preferred_element_type=jnp.float32
    )
    input_rows = lax.psum_scatter(
        result.astype(jnp.bfloat16), "head", scatter_dimension=0, tiled=True
    ).astype(jnp.float32)
    return (
        grad_key.reshape(1, 1, length, columns),
        grad_value.reshape(1, 1, length, columns),
        shared[:, :columns],
        shared[:, columns : 2 * columns],
        shared[:, 2 * columns :],
        input_rows.astype(jnp.bfloat16).reshape(1, 1, input_rows.shape[0], length),
    )


def solution(mesh):
    in_specs = (
        P("cuts", "doc", None, None),
        P(None, "head"),
        P(None, "head"),
        P(None, "head"),
        P("cuts", "doc", None, "head"),
        P("cuts", None),
        P("cuts", None),
    )
    out_specs = (
        P("cuts", "doc", None, "head"),
        P("cuts", "doc", None, "head"),
        P(("doc", "cuts"), "head"),
        P(("doc", "cuts"), "head"),
        P(("doc", "cuts"), "head"),
        P("cuts", "doc", "head", None),
    )
    return jax.shard_map(
        per_device, mesh=mesh, in_specs=in_specs, out_specs=out_specs, check_vma=False
    )
```

profile of v0, /device:TPU:16, one launch (start us, length us, event | category | flops | bytes accessed | tf_op | source)
XLA Modules:
  0.0 437.8 jit_solution(7440671462932104760)
XLA Ops:
  7.2 1.5 copy-done
  8.8 2.7 fusion.20
  11.5 1.0 fusion.23
  12.5 0.7 pad_maximum_fusion.3
  13.6 0.6 fusion.61
  14.2 0.7 compare_and_fusion
  14.9 0.7 compare_and_fusion.2
  15.5 0.7 compare_and_fusion.1
  16.2 0.7 compare_and_fusion.3
  16.8 0.7 compare_select_fusion
  17.5 0.7 compare_select_fusion.1
  18.3 2.5 fusion.17
  20.8 84.0 %all-gather.2.cloned.1.call-done = bf16[4096,512]{0,1:T(8,128)(2,1)} async-done(((bf16[256,512]{0,1:T(8,128)(2,1)}), bf16[4096,512]{0,1:T(8,128)(2,1)}) %all-gather.2.cloned.1.call-update) | async-done | bytes 4194320 | tf_op jit(solution)/shard_map/all_gather | solution.py:33
  104.8 6.5 %copy.57 = bf16[4096,512]{1,0:T(8,128)(2,1)} copy(bf16[4096,512]{0,1:T(8,128)(2,1)} %all-gather.2.cloned.1.call-done) | data formatting | bytes 8388608 | tf_op jit(solution)/shard_map/all_gather | solution.py:33
  111.3 3.9 gather_fusion.1
  115.3 3.9 gather_fusion
  119.5 0.8 copy.69
  120.5 0.8 copy.68
  121.8 1.9 fusion.63
  123.7 1.6 fusion.29
  125.3 1.2 fusion.65
  126.5 1.4 copy.75
  127.9 1.6 fusion.26
  129.5 1.9 fusion.12
  131.4 0.9 copy-done.5
  132.3 1.2 convolution_multiply_fusion
  133.5 2.3 copy.74
  135.8 1.1 fusion.27
  137.0 19.8 %all_to_all.10 = bf16[2,16,16,512]{3,2,0,1:T(8,128)(2,1)S(1)} all-to-all(bf16[2,16,16,512]{3,2,0,1:T(8,128)(2,1)S(1)} %copy.76), channel_id=1, replica_groups=mesh['doc'=16,'head'=8,'cuts'=2] {'doc'}, dimensions={1} | all-to-all | bytes 1048576 | tf_op jit(solution)/shard_map/all_to_all | solution.py:90
  157.4 0.9 copy.79
  158.2 3.5 all-to-all-start.1
  162.0 1.6 fusion.16
  163.6 4.3 fusion.64
  167.9 3.8 all-to-all-done.1
  171.7 1.2 fusion.32
  172.9 0.5 copy-done.1
  173.4 3.1 convolution_add_fusion.1
  176.5 2.1 fusion.3
  178.7 4.5 %fusion.1 = bf16[4096,768]{0,1:T(8,128)(2,1)} fusion(bf16[1,1,256,4096]{3,2,1,0:T(8,128)(2,1)S(1)} %copy-done, bf16[256,512]{1,0:T(8,128)(2,1)S(1)} %fusion.32, bf16[256,256]{1,0:T(8,128)(2,1)S(1)} %copy.81), kind=kOutput, calls=%fused_computation.4 | convolution fusion | flops 1614544896 | bytes 8781824 | tf_op jit(solution)/shard_map/dot_general | solution.py:111
  183.2 8.6 %copy.91 = bf16[4096,768]{1,0:T(8,128)(2,1)} copy(bf16[4096,768]{0,1:T(8,128)(2,1)} %fusion.1) | data formatting | bytes 12582912
  191.9 0.7 slice_bitcast_fusion
  192.6 81.1 %reduce-scatter.5.cloned.1.call-done = bf16[512,256]{0,1:T(8,128)(2,1)} async-done(((bf16[4096,256]{0,1:T(8,128)(2,1)}), bf16[512,256]{0,1:T(8,128)(2,1)}) %reduce-scatter.5.cloned.1.call-update) | async-done | bytes 262160 | tf_op jit(solution)/shard_map/reduce_scatter | solution.py:126
  273.7 1.8 copy.85
  275.5 152.4 %reduce-scatter.7.cloned.1.call-done = bf16[128,768]{1,0:T(8,128)(2,1)} async-done(((bf16[4096,768]{1,0:T(8,128)(2,1)}), bf16[128,768]{1,0:T(8,128)(2,1)}) %reduce-scatter.7.cloned.1.call-update) | async-done | bytes 196624
  427.9 1.1 copy.92
  429.0 0.8 copy.84
  429.8 0.8 copy.83
  430.5 0.8 copy.82
  (56 shorter events, 2.5 us)
Async XLA Ops:
  7.2 1.6 copy-start
  7.2 97.6 %all-gather.2.cloned.1.call-start = ((), (), s32[]{:S(2)}) async-start(), calls=%async_computation.4 | async-start | bytes 4456448 | tf_op jit(solution)/shard_map/all_gather | solution.py:33
  8.8 2.7 copy-start.2
  11.4 2.0 copy-start.6
  11.5 2.1 copy-start.13
  11.5 2.1 copy-start.14
  13.3 108.5 %copy-start.7 = (bf16[256,2,128]{2,0,1:T(8,128)(2,1)}, bf16[256,2,128]{2,0,1:T(8,128)(2,1)S(1)}, u32[]{:S(2)}) copy-start(bf16[256,2,128]{2,0,1:T(8,128)(2,1)S(1)} %copy.61) | copy-start | bytes 393220
  121.5 2.2 copy-start.9
  121.8 3.5 copy-start.11
  125.3 1.2 copy-start.4
  125.3 2.6 copy-start.12
  131.4 0.9 copy-start.5
  156.8 5.2 %copy-start.8 = (bf16[256,2,128]{2,0,1:T(8,128)(2,1)S(1)}, bf16[256,2,128]{2,0,1:T(8,128)(2,1)}, u32[]{:S(2)}) copy-start(bf16[256,2,128]{2,0,1:T(8,128)(2,1)} %copy-done.7) | copy-start | bytes 393220
  156.8 5.2 %copy-start.10 = (bf16[256,2,128]{2,0,1:T(8,128)(2,1)S(1)}, bf16[256,2,128]{2,0,1:T(8,128)(2,1)}, u32[]{:S(2)}) copy-start(bf16[256,2,128]{2,0,1:T(8,128)(2,1)} %copy-done.9) | copy-start | bytes 393220
  158.2 13.5 %all-to-all-start.1 = ((bf16[16,16,512]{2,1,0:T(8,128)(2,1)}), bf16[16,16,512]{2,1,0:T(8,128)(2,1)S(1)}, u32[]{:S(2)}, u32[]{:S(2)}) async-start(bf16[16,16,512]{2,1,0:T(8,128)(2,1)} %copy.79), calls=%async_computation.1 | async-start | bytes 524288 | tf_op jit(solution)/shard_map/all_to_all | solution.py:100
  161.8 111.9 %reduce-scatter.5.cloned.1.call-start = ((), (), s32[]{:S(2)}) async-start(), calls=%async_computation.5 | async-start | bytes 2359296 | tf_op jit(solution)/shard_map/reduce_scatter | solution.py:126
  171.7 1.7 copy-start.1
  173.4 3.1 copy-start.3
  178.6 249.3 %reduce-scatter.7.cloned.1.call-start = ((), (), s32[]{:S(2)}) async-start(), calls=%async_computation.6 | async-start | bytes 6488064
Sparse Core Ops, SparseCore 0:
  13.3 91.4 all-gather.1
  178.7 94.9 reduce-scatter.4
  276.4 151.4 reduce-scatter.6
where the time goes:
time: 439 us; the launch traced here: 438 us
  waiting for transfers between devices  321 us (73%)
  local copies, waits for them, and re-layouts  39.2 us (9%)
  matrix products  30 us (7%)
  blocking collectives  19.8 us (5%)
  between operations  14.2 us (3%)
  other arithmetic  9.41 us (2%)
    unnamed x4, waiting for transfers between devices  152 us
    all_gather x1, waiting for transfers between devices, per_device(): segment = lax.all_gather(key_value, 'doc', axis=0, tiled=True)  84 us
    reduce_scatter x1, waiting for transfers between devices, per_device(): lax.psum_scatter(result.astype(jnp.bfloat16), 'head', scatter_dimension=0...  81.1 us
    all_to_all x1, blocking collectives, per_device(): lax.all_to_all(outbound.astype(jnp.bfloat16), 'doc', split_axis=1, concat...  19.8 us
    unnamed x37, local copies, waits for them, and re-layouts  16.9 us
  transfers between devices with their start and end apart: 4, of which 4 were waited for; matrix products, arithmetic and copies ran while one was open for 7% of the time, Pallas kernels for 0%

commit v1 on v0

v1 whole, which is shorter than its diff:
```python
import functools
import math

import jax
import jax.numpy as jnp
from jax import lax
from jax.experimental import pallas as pl
from jax.experimental.pallas import tpu as pltpu
from jax.sharding import PartitionSpec as P

HD = 128
XS = 4
ZS = 4
YS = 4
BF = jnp.bfloat16
F32 = jnp.float32
SMALL = 16 * 1024 * 1024
LARGE = 52 * 1024 * 1024
VMEM = pl.BlockSpec(memory_space=pltpu.VMEM)
SMEM = pl.BlockSpec(memory_space=pltpu.SMEM)
ANY = pl.BlockSpec(memory_space=pl.ANY)


def _params(limit):
    return pltpu.CompilerParams(vmem_limit_bytes=limit)


def _cost(flops, nbytes, trans=0):
    return pl.CostEstimate(flops=flops, bytes_accessed=nbytes, transcendentals=trans)


def _nt(a, b):
    return lax.dot_general(a, b, (((1,), (1,)), ((), ())), preferred_element_type=F32)


def _nn(a, b):
    return lax.dot_general(a, b, (((1,), (0,)), ((), ())), preferred_element_type=F32)


def _tn(a, b):
    return lax.dot_general(a, b, (((0,), (0,)), ((), ())), preferred_element_type=F32)


PIECES = 8
HINT = 30_000_000_000


def _project_body(x_ref, wq_ref, wk_ref, wv_ref, do_ref, o_ref, *rest):
    outs, (xs, ws, acc, sems) = rest[:XS], rest[XS:]
    d, n = wq_ref.shape
    my_x = lax.rem(lax.axis_index("doc"), XS)
    width = d // (ZS * XS)
    kb = d // PIECES
    last = pltpu.make_async_copy(do_ref, o_ref.at[:, 3 * n :], sems.at[PIECES, 0])
    copies = []
    for i in range(PIECES):
        part = slice(i * kb, (i + 1) * kb)
        row = [pltpu.make_async_copy(x_ref.at[:, part], xs.at[:, part], sems.at[i, 0])]
        for j, w in enumerate((wq_ref, wk_ref, wv_ref)):
            row.append(pltpu.make_async_copy(w.at[part, :], ws.at[j, part, :], sems.at[i, j + 1]))
        for c in row:
            c.start()
        copies.append(row)
    last.start()
    for i in range(PIECES):
        part = slice(i * kb, (i + 1) * kb)
        for c in copies[i]:
            c.wait()
        x = xs[:, part]
        for j in range(3):
            cols = slice(j * n, (j + 1) * n)
            prod = _nn(x, ws[j, part, :])
            if i == 0:
                acc[:, cols] = prod
            elif i < PIECES - 1:
                acc[:, cols] += prod
            else:
                o_ref[:, cols] = (acc[:, cols] + prod).astype(BF)
    last.wait()
    for k in range(XS):
        for z in range(ZS):
            start = pl.multiple_of((z * XS + lax.rem(my_x + k, XS)) * width, width)
            outs[k][:, z * width : (z + 1) * width] = xs[:, pl.ds(start, width)]


def project(x, wq, wk, wv, do):
    t, d = x.shape
    n = wq.shape[1]
    return pl.pallas_call(
        _project_body,
        in_specs=[ANY] * 5,
        out_specs=[VMEM] * (1 + XS),
        out_shape=[jax.ShapeDtypeStruct((t, 4 * n), BF)]
        + [jax.ShapeDtypeStruct((t, d // XS), BF)] * XS,
        scratch_shapes=[
            pltpu.VMEM((t, d), BF),
            pltpu.VMEM((3, d, n), BF),
            pltpu.VMEM((t, 3 * n), F32),
            pltpu.SemaphoreType.DMA((PIECES + 1, 4)),
        ],
        compiler_params=_params(LARGE),
        cost_estimate=_cost(6 * t * d * n, 2 * (t * d + 3 * d * n)),
        name="project",
    )(x, wq, wk, wv, do)


def _stack_body(*refs):
    o_ref = refs[-1]
    for i, r in enumerate(refs[:-1]):
        o_ref[i] = r[...]


def stack(parts, flops):
    shape = (len(parts), *parts[0].shape)
    return pl.pallas_call(
        _stack_body,
        in_specs=[VMEM] * len(parts),
        out_specs=VMEM,
        out_shape=jax.ShapeDtypeStruct(shape, BF),
        compiler_params=_params(SMALL),
        cost_estimate=_cost(flops, 0),
        name="stack",
    )(*parts)


def _pick_kv_body(p1_ref, p2_ref, all_ref, *rest):
    kv_ref = rest[-1]
    n = all_ref.shape[2] // 4

    def one(d, carry):
        for slot, p_ref in enumerate((p1_ref, p2_ref)):
            kv_ref[d, slot] = all_ref[p_ref[d], :, n : 3 * n]
        return carry

    lax.fori_loop(0, all_ref.shape[0], one, 0)


def _pick_qdo_body(p1_ref, p2_ref, all_ref, *rest):
    qdo_ref = rest[-1]
    n = all_ref.shape[2] // 4

    def one(d, carry):
        for slot, p_ref in enumerate((p1_ref, p2_ref)):
            p = p_ref[d]
            qdo_ref[p, slot, :, :n] = all_ref[d, :, :n]
            qdo_ref[p, slot, :, n:] = all_ref[d, :, 3 * n :]
        return carry

    lax.fori_loop(0, all_ref.shape[0], one, 0)


def pick(body, p1, p2, blocks, after):
    docs, rows, n = blocks.shape
    n = n // 4
    return pl.pallas_call(
        body,
        in_specs=[SMEM, SMEM, VMEM] + [VMEM] * len(after),
        out_specs=VMEM,
        out_shape=jax.ShapeDtypeStruct((docs, 2, rows, 2 * n), BF),
        compiler_params=_params(SMALL),
        cost_estimate=_cost(0, 2 * docs * rows * n * 8),
        name="pick",
    )(p1, p2, blocks, *after)


def _attend_body(factor, qkv_ref, kv_ref, *rest):
    gq_ref, st_ref = rest[-2:]
    t, n = gq_ref.shape
    st_ref[...] = jnp.zeros_like(st_ref)
    for h in range(n // HD):
        c = slice(h * HD, (h + 1) * HD)
        q = qkv_ref[:, c]
        k = qkv_ref[:, n + h * HD : n + (h + 1) * HD]
        v = qkv_ref[:, 2 * n + h * HD : 2 * n + (h + 1) * HD]
        do = qkv_ref[:, 3 * n + h * HD : 3 * n + (h + 1) * HD]
        keys, values = [k], [v]
        for s in range(2):
            keys.append(kv_ref[:, s, :, c].reshape(t, HD))
            values.append(kv_ref[:, s, :, n + h * HD : n + (h + 1) * HD].reshape(t, HD))
        sc = [_nt(kk, q) * factor for kk in keys]
        key_at = lax.broadcasted_iota(jnp.int32, (t, t), 0)
        query_at = lax.broadcasted_iota(jnp.int32, (t, t), 1)
        sc[0] = jnp.where(key_at <= query_at, sc[0], -jnp.inf)
        m = functools.reduce(jnp.maximum, [jnp.max(x, axis=0, keepdims=True) for x in sc])
        e = [jnp.exp(x - m) for x in sc]
        il = 1.0 / sum(jnp.sum(x, axis=0, keepdims=True) for x in e)
        p = [x * il for x in e]
        low = [x.astype(BF) for x in p]
        dp = [_nt(vv, do) for vv in values]
        delta = sum(
            jnp.sum(a.astype(F32) * b, axis=0, keepdims=True) for a, b in zip(low, dp)
        )
        ds = [(a * (b - delta)).astype(BF) for a, b in zip(p, dp)]
        gq = sum(_tn(a, kk) for a, kk in zip(ds, keys)) * factor
        gq_ref[:, c] = gq.astype(BF)
        st_ref[3 * h : 3 * h + 1, :] = m
        st_ref[3 * h + 1 : 3 * h + 2, :] = il
        st_ref[3 * h + 2 : 3 * h + 3, :] = delta


def attend(factor, qkv, kv, after):
    t, n = qkv.shape
    n = n // 4
    return pl.pallas_call(
        functools.partial(_attend_body, factor),
        in_specs=[VMEM] * 2 + [ANY] * len(after),
        out_specs=[VMEM] * 2,
        out_shape=[
            jax.ShapeDtypeStruct((t, n), BF),
            jax.ShapeDtypeStruct((8, t), F32),
        ],
        compiler_params=_params(SMALL),
        cost_estimate=_cost(2 * 11 * t * t * n, 4 * t * n * 10, 3 * t * t * n // HD),
        name="attend",
    )(qkv, kv, *after)


def _settle_body(factor, p1_ref, p2_ref, qkv_ref, qdo_ref, *rest):
    gk_ref, gv_ref, both_ref = rest[-3:]
    st_refs = rest[:ZS]
    t, n = gk_ref.shape
    me = lax.axis_index("doc")
    names = [
        sum(jnp.where(p[d] == me, d, 0) for d in range(p1_ref.shape[0]))
        for p in (p1_ref, p2_ref)
    ]
    steps_z = [lax.rem(me // XS - d // XS + ZS, ZS) for d in names]
    steps_x = [lax.rem(lax.rem(me, XS) - lax.rem(d, XS) + XS, XS) for d in names]
    for h in range(n // HD):
        c = slice(h * HD, (h + 1) * HD)
        k = qkv_ref[:, n + h * HD : n + (h + 1) * HD]
        v = qkv_ref[:, 2 * n + h * HD : 2 * n + (h + 1) * HD]
        dk = dv = 0.0
        for s in range(3):
            if s == 2:
                st = st_refs[0][0]
                q, do = qkv_ref[:, c], qkv_ref[:, 3 * n + h * HD : 3 * n + (h + 1) * HD]
            else:
                st = st_refs[0][steps_x[s]]
                for j in range(1, ZS):
                    st = jnp.where(steps_z[s] == j, st_refs[j][steps_x[s]], st)
                q = qdo_ref[:, s, :, c].reshape(t, HD)
                do = qdo_ref[:, s, :, n + h * HD : n + (h + 1) * HD].reshape(t, HD)
            m, il, delta = (st[3 * h + i : 3 * h + i + 1, :] for i in range(3))
            sc = _nt(k, q) * factor
            if s == 2:
                key_at = lax.broadcasted_iota(jnp.int32, (t, t), 0)
                query_at = lax.broadcasted_iota(jnp.int32, (t, t), 1)
                sc = jnp.where(key_at <= query_at, sc, -jnp.inf)
            p = jnp.exp(sc - m) * il
            dp = _nt(v, do)
            ds = (p * (dp - delta)).astype(BF)
            dk = dk + _nn(ds, q) * factor
            dv = dv + _nn(p.astype(BF), do)
        gk, gv = dk.astype(BF), dv.astype(BF)
        gk_ref[:, c] = gk
        gv_ref[:, c] = gv
        both_ref[:, c] = gk
        both_ref[:, n + h * HD : n + (h + 1) * HD] = gv


def settle(factor, p1, p2, qkv, qdo, stats, after):
    t, n = qkv.shape
    n = n // 4
    return pl.pallas_call(
        functools.partial(_settle_body, factor),
        in_specs=[SMEM] * 2 + [VMEM] * (2 + ZS + len(after)),
        out_specs=[VMEM] * 3,
        out_shape=[
            jax.ShapeDtypeStruct((t, n), BF),
            jax.ShapeDtypeStruct((t, n), BF),
            jax.ShapeDtypeStruct((t, 2 * n), BF),
        ],
        compiler_params=_params(SMALL),
        cost_estimate=_cost(2 * 12 * t * t * n, 4 * t * n * 8, 3 * t * t * n // HD),
        name="settle",
    )(p1, p2, qkv, qdo, *stats, *after)


def _wgrad_body(near_ref, far_ref, *refs):
    gq, gkv = refs[0:XS], refs[XS : 2 * XS]
    xs = (near_ref.at[0], near_ref.at[1], far_ref.at[0], near_ref.at[2])
    keep_ref, send_ref = refs[-2:]
    first = lax.axis_index("cuts") == 0
    half, n = keep_ref.shape[1], gq[0].shape[1]
    for z in range(ZS):
        for cols, gs in ((slice(0, n), gq), (slice(n, 3 * n), gkv)):
            acc = None
            for x, g in zip(xs, gs):
                part = _tn(x[:, z * 2 * half : (z + 1) * 2 * half], g[...])
                acc = part if acc is None else acc + part
            top, low = acc[:half], acc[half:]
            keep_ref[z, :, cols] = jnp.where(first, top, low)
            send_ref[z, :, cols] = jnp.where(first, low, top).astype(BF)


def wgrad(near, far, gq, gkv):
    _, t, rows = near.shape
    n = gq[0].shape[1]
    shape = (ZS, rows // (2 * ZS), 3 * n)
    return pl.pallas_call(
        _wgrad_body,
        in_specs=[VMEM] * (2 + 2 * XS),
        out_specs=[VMEM, VMEM],
        out_shape=[jax.ShapeDtypeStruct(shape, F32), jax.ShapeDtypeStruct(shape, BF)],
        compiler_params=_params(SMALL),
        cost_estimate=_cost(2 * XS * t * rows * 3 * n, 2 * XS * t * (rows + 3 * n) + 6 * rows * n),
        name="wgrad",
    )(near, far, *gq, *gkv)


def _xgrad_body(wq_ref, wk_ref, wv_ref, gq_ref, gkv_ref, *rest):
    o_ref = rest[-1]
    n = gq_ref.shape[1]
    block = o_ref.shape[2]
    rb = 256
    for y in range(YS):
        for half in range(2):
            for r in range(block // rb):
                at = (half * YS + y) * block + r * rb
                rows = slice(at, at + rb)
                acc = (
                    _nt(wq_ref[rows], gq_ref[...])
                    + _nt(wk_ref[rows], gkv_ref[:, :n])
                    + _nt(wv_ref[rows], gkv_ref[:, n:])
                )
                o_ref[y, half, r * rb : (r + 1) * rb] = acc.astype(BF)


def xgrad(wq, wk, wv, gq, gkv, after):
    d, n = wq.shape
    t = gq.shape[0]
    return pl.pallas_call(
        _xgrad_body,
        in_specs=[VMEM] * (5 + len(after)),
        out_specs=VMEM,
        out_shape=jax.ShapeDtypeStruct((YS, 2, d // (2 * YS), t), BF),
        compiler_params=_params(SMALL),
        cost_estimate=_cost(6 * t * d * n, 6 * d * n + 8 * t * n + 2 * d * t),
        name="xgrad",
    )(wq, wk, wv, gq, gkv, *after)


def shift_x(v, k):
    pairs = [(z * XS + x, z * XS + (x + k) % XS) for z in range(ZS) for x in range(XS)]
    return lax.ppermute(v, "doc", pairs)


def shift_z(v, k):
    pairs = [(z * XS + x, ((z + k) % ZS) * XS + x) for z in range(ZS) for x in range(XS)]
    return lax.ppermute(v, "doc", pairs)


def shift_y(v, k):
    pairs = [(a * YS + y, a * YS + (y + k) % YS) for a in range(2) for y in range(YS)]
    return lax.ppermute(v, "head", pairs)


def swap_halves(v):
    pairs = [(a * YS + y, (1 - a) * YS + y) for a in range(2) for y in range(YS)]
    return lax.ppermute(v, "head", pairs)


def swap_cores(v):
    return lax.ppermute(v, "cuts", [(0, 1), (1, 0)])


ORDER = (1, 3, 2)


def per_device(
    inputs, weight_query, weight_key, weight_value, grad_output, partner_one, partner_two
):
    x = inputs[0, 0]
    do = grad_output[0, 0]
    t, d = x.shape
    n = weight_query.shape[1]
    factor = 1.0 / math.sqrt(HD)
    docs = lax.axis_size("doc")
    rows = t // docs
    p1, p2 = partner_one[0], partner_two[0]
    me = lax.axis_index("doc")
    my_z = me // XS
    def spread(v):
        return lax.all_to_all(v, "doc", split_axis=0, concat_axis=0, tiled=True)

    qkvd, *cuts = project(x, weight_query, weight_key, weight_value, do)
    blocks = spread(qkvd.reshape(docs, rows, 4 * n))

    near = stack([cuts[0], shift_x(cuts[1], 1), shift_x(cuts[3], 3)], HINT)
    far = stack([shift_x(cuts[2], 2)], HINT)

    kv = spread(pick(_pick_kv_body, p1, p2, blocks, [near]))
    qdo = spread(pick(_pick_qdo_body, p1, p2, blocks, [far]))
    gq, stats = attend(factor, qkvd, kv, [])
    weights = [weight_query, weight_key, weight_value]
    row = jnp.stack([shift_x(stats, k) if k else stats for k in range(XS)])
    all_stats = [shift_z(row, k) if k else row for k in range(ZS)]
    gq_x = {0: gq, **{k: shift_x(gq, k) for k in ORDER}}
    gk, gv, gkv = settle(factor, p1, p2, qkvd, qdo, all_stats, weights)
    gkv_x = {0: gkv, **{k: shift_x(gkv, k) for k in ORDER}}

    terms = xgrad(*weights, gq, gkv, [gq_x[k] for k in ORDER])
    groups = [[a * YS + y for y in range(YS)] for a in range(2)]
    terms = lax.all_to_all(
        terms, "head", split_axis=0, concat_axis=0, tiled=True, axis_index_groups=groups
    )
    mine, theirs = wgrad(
        near,
        far,
        [gq_x[k] for k in range(XS)],
        [gkv_x[k] for k in range(XS)],
    )
    pair = (mine + swap_cores(theirs).astype(F32)).astype(BF)
    total = lax.dynamic_index_in_dim(pair, my_z, axis=0, keepdims=False).astype(F32)
    for k in range(1, ZS):
        out = lax.dynamic_index_in_dim(pair, (my_z + k) % ZS, axis=0, keepdims=False)
        total = total + shift_z(out, k).astype(F32)
    sums = jnp.sum(terms.astype(F32), axis=0)
    my_half = lax.axis_index("head") // YS
    keep = lax.dynamic_index_in_dim(sums, my_half, axis=0, keepdims=False)
    send = lax.dynamic_index_in_dim(sums, 1 - my_half, axis=0, keepdims=False)
    features = (keep + swap_halves(send.astype(BF)).astype(F32)).astype(BF)
    return (
        gk.reshape(1, 1, t, n),
        gv.reshape(1, 1, t, n),
        total[:, :n],
        total[:, n : 2 * n],
        total[:, 2 * n :],
        features.reshape(1, 1, features.shape[0], t),
    )


def solution(mesh):
    in_specs = (
        P("cuts", "doc", None, None),
        P(None, "head"),
        P(None, "head"),
        P(None, "head"),
        P("cuts", "doc", None, "head"),
        P("cuts", None),
        P("cuts", None),
    )
    out_specs = (
        P("cuts", "doc", None, "head"),
        P("cuts", "doc", None, "head"),
        P(("doc", "cuts"), "head"),
        P(("doc", "cuts"), "head"),
        P(("doc", "cuts"), "head"),
        P("cuts", "doc", "head", None),
    )
    return jax.shard_map(
        per_device, mesh=mesh, in_specs=in_specs, out_specs=out_specs, check_vma=False
    )
```

time: 439 us -> 158 us (0.36)
  the two profiles are of different devices: /device:TPU:16 before, /device:TPU:72 now
where the time goes in v1:
time: 158 us
  starting transfers between devices  60 us (38%)
  waiting for transfers between devices  57.6 us (36%)
  Pallas kernels  21.6 us (14%)
  local copies, waits for them, and re-layouts  14.6 us (9%)
  other arithmetic  3.06 us (2%)
    ppermute x6, waiting for transfers between devices, shift_z(): return lax.ppermute(v, 'doc', pairs)  26.3 us
    all_to_all x3, starting transfers between devices, spread(): return lax.all_to_all(v, 'doc', split_axis=0, concat_axis=0, tiled=True)  22.1 us
    all_to_all x3, waiting for transfers between devices, spread(): return lax.all_to_all(v, 'doc', split_axis=0, concat_axis=0, tiled=True)  21.4 us
    ppermute x12, starting transfers between devices, shift_x(): return lax.ppermute(v, 'doc', pairs)  20.1 us
    unnamed x38, local copies, waits for them, and re-layouts  13.8 us
    ppermute x6, starting transfers between devices, shift_z(): return lax.ppermute(v, 'doc', pairs)  8.19 us
    ppermute x12, waiting for transfers between devices, shift_x(): return lax.ppermute(v, 'doc', pairs)  7.38 us
    pallas_call x1, Pallas kernels, project(): pl.pallas_call(_project_body, in_specs=[ANY] * 5, out_specs=[VMEM] * (1 +...  5.83 us
  transfers between devices with their start and end apart: 24, of which 10 were waited for; matrix products, arithmetic and copies ran while one was open for 2% of the time, Pallas kernels for 10%

profile of v1, /device:TPU:72, one launch (start us, length us, event | category | flops | bytes accessed | tf_op | source)
XLA Modules:
  0.0 157.6 jit_solution(10247309225351344133)
XLA Ops:
  0.6 0.9 copy-done.8
  1.5 5.8 %project.1 = (bf16[256,1024]{1,0:T(8,128)(2,1)}, bf16[256,1024]{1,0:T(8,128)(2,1)S(1)}, bf16[256,1024]{1,0:T(8,128)(2,1)S(1)}, bf16[256,1024]{1,0:T(8,128)(2,1)}, bf16[256,1024]{1,0:T(8,128)(2,1)}) custom-call(bf16[256,4096]{1,0:T(8,128)(2,1)} %bitcast.38, bf16[4096,256]{1,0:T(8,128)(2,1)} %wq_ref.3, bf16[4096,256]{1,0:T(8,128)(2,1)} %wk_ref.3, ...), custom_call_target="tpu_custom_call" | custom-call | flops 1610612736 | bytes 8388608 | tf_op jit(solution)/shard_map/project/pallas_call | solution.py:89
  7.4 1.6 collective-permute-start.1
  8.9 1.7 %collective-permute-start.2 = (bf16[256,1024]{1,0:T(8,128)(2,1)}, bf16[256,1024]{1,0:T(8,128)(2,1)S(1)}, u32[]{:S(2)}, u32[]{:S(2)}) collective-permute-start(bf16[256,1024]{1,0:T(8,128)(2,1)} %get-tuple-element.22), channel_id=1, source_target_pairs={{0,48},{16,0},{32,16},{48,32},{64,112},{80,64},{96,80},{112,96},{1... | collective-permute-start | bytes 1572872 | tf_op jit(solution)/shard_map/ppermute | solution.py:346
  10.7 6.8 %all-to-all-start = ((bf16[16,16,1024]{2,1,0:T(8,128)(2,1)}), bf16[16,16,1024]{2,1,0:T(8,128)(2,1)S(1)}, u32[]{:S(2)}, u32[]{:S(2)}) async-start(bf16[16,16,1024]{2,1,0:T(8,128)(2,1)} %bitcast.4), calls=%async_computation | async-start | bytes 1048576 | tf_op jit(solution)/shard_map/all_to_all | solution.py:385
  17.5 3.0 %collective-permute-start = (bf16[256,1024]{1,0:T(8,128)(2,1)}, bf16[256,1024]{1,0:T(8,128)(2,1)}, u32[]{:S(2)}, u32[]{:S(2)}) collective-permute-start(bf16[256,1024]{1,0:T(8,128)(2,1)} %get-tuple-element.19), channel_id=1, source_target_pairs={{0,32},{16,48},{32,0},{48,16},{64,96},{80,112},{96,64},{112,80},{1... | collective-permute-start | bytes 1572872 | tf_op jit(solution)/shard_map/ppermute | solution.py:346
  20.5 4.1 %collective-permute-done.1.refs_1_ = bf16[256,1024]{1,0:T(8,128)(2,1)S(1)} collective-permute-done((bf16[256,1024]{1,0:T(8,128)(2,1)S(1)}, bf16[256,1024]{1,0:T(8,128)(2,1)S(1)}, u32[]{:S(2)}, u32[]{:S(2)}) %collective-permute-start.1) | collective-permute-done | bytes 524320 | tf_op jit(solution)/shard_map/ppermute | solution.py:346
  24.6 3.2 %collective-permute-done.2.refs_2_ = bf16[256,1024]{1,0:T(8,128)(2,1)S(1)} collective-permute-done((bf16[256,1024]{1,0:T(8,128)(2,1)}, bf16[256,1024]{1,0:T(8,128)(2,1)S(1)}, u32[]{:S(2)}, u32[]{:S(2)}) %collective-permute-start.2) | collective-permute-done | bytes 524320 | tf_op jit(solution)/shard_map/ppermute | solution.py:346
  27.8 0.8 copy-done.17
  28.6 1.0 copy-done.18
  29.8 9.0 %all-to-all-done.all_ref = bf16[16,16,1024]{2,1,0:T(8,128)(2,1)S(1)} async-done(((bf16[16,16,1024]{2,1,0:T(8,128)(2,1)}), bf16[16,16,1024]{2,1,0:T(8,128)(2,1)S(1)}, u32[]{:S(2)}, u32[]{:S(2)}) %all-to-all-start) | async-done | bytes 524320 | tf_op jit(solution)/shard_map/all_to_all | solution.py:385
  38.8 1.5 pick.3
  40.3 10.1 %all-to-all-start.2 = ((bf16[16,2,16,512]{3,2,1,0:T(8,128)(2,1)}), bf16[16,2,16,512]{3,2,1,0:T(8,128)(2,1)S(1)}, u32[]{:S(2)}, u32[]{:S(2)}) async-start(bf16[16,2,16,512]{3,2,1,0:T(8,128)(2,1)} %pick.3), calls=%async_computation.2 | async-start | bytes 1048576 | tf_op jit(solution)/shard_map/all_to_all | solution.py:385
  50.4 1.1 stack.22.rest_0_.far_ref
  51.5 1.5 pick.2
  53.0 0.8 copy-done.6
  53.8 12.4 %all-to-all-done.2.kv_ref = bf16[16,2,16,512]{3,2,1,0:T(8,128)(2,1)S(1)} async-done(((bf16[16,2,16,512]{3,2,1,0:T(8,128)(2,1)}), bf16[16,2,16,512]{3,2,1,0:T(8,128)(2,1)S(1)}, u32[]{:S(2)}, u32[]{:S(2)}) %all-to-all-start.2) | async-done | bytes 524320 | tf_op jit(solution)/shard_map/all_to_all | solution.py:385
  66.2 5.2 %all-to-all-start.1 = ((bf16[16,2,16,512]{3,2,1,0:T(8,128)(2,1)}), bf16[16,2,16,512]{3,2,1,0:T(8,128)(2,1)S(1)}, u32[]{:S(2)}, u32[]{:S(2)}) async-start(bf16[16,2,16,512]{3,2,1,0:T(8,128)(2,1)} %pick.2), calls=%async_computation.1 | async-start | bytes 1048576 | tf_op jit(solution)/shard_map/all_to_all | solution.py:385
  71.3 2.7 %attend.1 = (bf16[256,256]{1,0:T(8,128)(2,1)S(1)}, f32[8,256]{1,0:T(8,128)S(1)}) custom-call(bf16[256,1024]{1,0:T(8,128)(2,1)} %get-tuple-element.18.qkv_ref, bf16[16,2,16,512]{3,2,1,0:T(8,128)(2,1)S(1)} %all-to-all-done.2.kv_ref), custom_call_target="tpu_custom_call" | custom-call | flops 369098752 | bytes 2621440 | tf_op jit(solution)/shard_map/attend/pallas_call | solution.py:204
  74.1 2.8 %collective-permute-start.5 = (f32[8,256]{1,0:T(8,128)S(1)}, f32[8,256]{1,0:T(8,128)S(1)}, u32[]{:S(2)}, u32[]{:S(2)}) collective-permute-start(f32[8,256]{1,0:T(8,128)S(1)} %get-tuple-element.23), channel_id=1, source_target_pairs={{0,48},{16,0},{32,16},{48,32},{64,112},{80,64},{96,80},{112,96},{1... | collective-permute-start | bytes 24584 | tf_op jit(solution)/shard_map/ppermute | solution.py:346
  76.8 0.9 collective-permute-start.4
  77.7 0.9 collective-permute-start.3
  78.5 1.8 %collective-permute-start.9 = (bf16[256,256]{1,0:T(8,128)(2,1)S(1)}, bf16[256,256]{1,0:T(8,128)(2,1)S(1)}, u32[]{:S(2)}, u32[]{:S(2)}) collective-permute-start(bf16[256,256]{1,0:T(8,128)(2,1)S(1)} %get-tuple-element.26.refs_0_.gq_ref), channel_id=1, source_target_pairs={{0,16},{16,32},{32,48},{48,0},{64,80},{80,96},{96,112},{112,64},{1... | collective-permute-start | bytes 393224 | tf_op jit(solution)/shard_map/ppermute | solution.py:346
  80.3 2.1 %collective-permute-start.10 = (bf16[256,256]{1,0:T(8,128)(2,1)S(1)}, bf16[256,256]{1,0:T(8,128)(2,1)S(1)}, u32[]{:S(2)}, u32[]{:S(2)}) collective-permute-start(bf16[256,256]{1,0:T(8,128)(2,1)S(1)} %get-tuple-element.26.refs_0_.gq_ref), channel_id=1, source_target_pairs={{0,32},{16,48},{32,0},{48,16},{64,96},{80,112},{96,64},{112,80},{1... | collective-permute-start | bytes 393224 | tf_op jit(solution)/shard_map/ppermute | solution.py:346
  82.4 2.2 %collective-permute-start.11 = (bf16[256,256]{1,0:T(8,128)(2,1)S(1)}, bf16[256,256]{1,0:T(8,128)(2,1)S(1)}, u32[]{:S(2)}, u32[]{:S(2)}) collective-permute-start(bf16[256,256]{1,0:T(8,128)(2,1)S(1)} %get-tuple-element.26.refs_0_.gq_ref), channel_id=1, source_target_pairs={{0,48},{16,0},{32,16},{48,32},{64,112},{80,64},{96,80},{112,96},{1... | collective-permute-start | bytes 393224 | tf_op jit(solution)/shard_map/ppermute | solution.py:346
  84.7 2.2 %collective-permute-start.7 = (f32[4,8,256]{2,1,0:T(8,128)S(1)}, f32[4,8,256]{2,1,0:T(8,128)S(1)}, u32[]{:S(2)}, u32[]{:S(2)}) collective-permute-start(f32[4,8,256]{2,1,0:T(8,128)S(1)} %pad_maximum_fusion.rest_0_), channel_id=1, source_target_pairs={{0,128},{16,144},{32,160},{48,176},{64,192},{80,208},{96,224},{112... | collective-permute-start | bytes 98312 | tf_op jit(solution)/shard_map/ppermute | solution.py:351
  86.9 1.7 %collective-permute-done.6.rest_1_ = f32[4,8,256]{2,1,0:T(8,128)S(1)} collective-permute-done((f32[4,8,256]{2,1,0:T(8,128)S(1)}, f32[4,8,256]{2,1,0:T(8,128)S(1)}, u32[]{:S(2)}, u32[]{:S(2)}) %collective-permute-start.6) | collective-permute-done | bytes 32800 | tf_op jit(solution)/shard_map/ppermute | solution.py:351
  89.8 2.7 %collective-permute-done.8.rest_3_ = f32[4,8,256]{2,1,0:T(8,128)S(1)} collective-permute-done((f32[4,8,256]{2,1,0:T(8,128)S(1)}, f32[4,8,256]{2,1,0:T(8,128)S(1)}, u32[]{:S(2)}, u32[]{:S(2)}) %collective-permute-start.8) | collective-permute-done | bytes 32800 | tf_op jit(solution)/shard_map/ppermute | solution.py:351
  92.5 1.6 %copy-done.1 = bf16[4096,256]{1,0:T(8,128)(2,1)S(1)} copy-done((bf16[4096,256]{1,0:T(8,128)(2,1)S(1)}, bf16[4096,256]{1,0:T(8,128)(2,1)}, u32[]{:S(2)}) %copy-start.1) | copy-done | bytes 2097176
  94.1 1.6 %copy-done.2 = bf16[4096,256]{1,0:T(8,128)(2,1)S(1)} copy-done((bf16[4096,256]{1,0:T(8,128)(2,1)S(1)}, bf16[4096,256]{1,0:T(8,128)(2,1)}, u32[]{:S(2)}) %copy-start.2) | copy-done | bytes 2097176
  95.7 3.2 %settle.1 = (bf16[256,256]{1,0:T(8,128)(2,1)}, bf16[256,256]{1,0:T(8,128)(2,1)}, bf16[256,512]{1,0:T(8,128)(2,1)S(1)}) custom-call(s32[16]{0:T(128)S(1)} %bitcast.34, s32[16]{0:T(128)S(1)} %bitcast.37, bf16[256,1024]{1,0:T(8,128)(2,1)} %get-tuple-element.18.qkv_ref, bf16[16,2,16,512]{3,2,1,0:T(8,128)(2,1)S(1)} %all-to-all-done.1.qdo_ref, ...), custom_call_target="tpu_custom_call" | custom-call | flops 402653184 | bytes 2097152 | tf_op jit(solution)/shard_map/settle/pallas_call | solution.py:265
  98.9 1.5 collective-permute-start.13
  100.4 1.8 %collective-permute-start.14 = (bf16[256,512]{1,0:T(8,128)(2,1)S(1)}, bf16[256,512]{1,0:T(8,128)(2,1)}, u32[]{:S(2)}, u32[]{:S(2)}) collective-permute-start(bf16[256,512]{1,0:T(8,128)(2,1)S(1)} %get-tuple-element.27.refs_4_.gkv_ref), channel_id=1, source_target_pairs={{0,48},{16,0},{32,16},{48,32},{64,112},{80,64},{96,80},{112,96},{1... | collective-permute-start | bytes 786440 | tf_op jit(solution)/shard_map/ppermute | solution.py:346
  102.1 1.8 %xgrad.1 = bf16[4,2,512,256]{3,2,1,0:T(8,128)(2,1)S(1)} custom-call(bf16[4096,256]{1,0:T(8,128)(2,1)S(1)} %copy-done, bf16[4096,256]{1,0:T(8,128)(2,1)S(1)} %copy-done.1, bf16[4096,256]{1,0:T(8,128)(2,1)S(1)} %copy-done.2, bf16[256,256]{1,0:T(8,128)(2,1)S(1)} %get-tuple-element.26.refs_0_.gq_ref, bf16[256,512]{1,0:T(8,128)(2,1)S(1)} %get-tuple-element.27.refs_4_.gkv_ref, ...), custom_call_target="tpu_custom_call" | custom-call | flops 1610612736 | bytes 8912896 | tf_op jit(solution)/shard_map/xgrad/pallas_call | solution.py:333
  104.0 1.3 copy-done.3
  107.3 5.0 %all-to-all-start.3 = ((bf16[4,2,512,256]{3,2,1,0:T(8,128)(2,1)}), bf16[4,2,512,256]{3,2,1,0:T(8,128)(2,1)}, u32[]{:S(2)}, u32[]{:S(2)}) async-start(bf16[4,2,512,256]{3,2,1,0:T(8,128)(2,1)} %copy-done.3), calls=%async_computation.3 | async-start | bytes 4194304 | tf_op jit(solution)/shard_map/all_to_all | solution.py:405
  112.3 1.0 copy-done.7
  113.4 0.9 copy-done.10
  114.3 0.9 copy-done.12
  115.2 0.9 copy-done.14
  116.1 3.9 %wgrad.1 = (f32[4,128,768]{2,1,0:T(8,128)S(1)}, bf16[4,128,768]{2,1,0:T(8,128)(2,1)}) custom-call(bf16[3,256,1024]{2,1,0:T(8,128)(2,1)S(1)} %copy-done.5, bf16[1,256,1024]{2,1,0:T(8,128)(2,1)S(1)} %copy-done.7, bf16[256,256]{1,0:T(8,128)(2,1)S(1)} %get-tuple-element.26.refs_0_.gq_ref, bf16[256,256]{1,0:T(8,128)(2,1)S(1)} %copy-done.10, ...), custom_call_target="tpu_custom_call" | custom-call | flops 1610612736 | bytes 5242880 | tf_op jit(solution)/shard_map/wgrad/pallas_call | solution.py:301
  120.0 2.5 %collective-permute-done.15 = bf16[4,128,768]{2,1,0:T(8,128)(2,1)S(1)} collective-permute-done((bf16[4,128,768]{2,1,0:T(8,128)(2,1)}, bf16[4,128,768]{2,1,0:T(8,128)(2,1)S(1)}, u32[]{:S(2)}, u32[]{:S(2)}) %collective-permute-start.15) | collective-permute-done | bytes 786464 | tf_op jit(solution)/shard_map/ppermute | solution.py:365
  122.7 0.8 collective-permute-start.18
  123.5 4.4 %collective-permute-start.17 = (bf16[128,768]{1,0:T(8,128)(2,1)S(1)}, bf16[128,768]{1,0:T(8,128)(2,1)S(1)}, u32[]{:S(2)}, u32[]{:S(2)}) collective-permute-start(bf16[128,768]{1,0:T(8,128)(2,1)S(1)} %get-tuple-element.32), channel_id=1, source_target_pairs={{0,128},{16,144},{32,160},{48,176},{64,192},{80,208},{96,224},{112... | collective-permute-start | bytes 589832 | tf_op jit(solution)/shard_map/ppermute | solution.py:351
  127.9 2.0 %convert_reduce_fusion = f32[2,512,256]{2,1,0:T(8,128)S(1)} fusion(bf16[4,2,512,256]{3,2,1,0:T(8,128)(2,1)} %all-to-all-done.3), kind=kLoop, calls=%fused_computation | loop fusion | flops 1835008 | bytes 3145728 | tf_op jit(solution)/shard_map/reduce_sum | solution.py:419
  129.9 4.6 %collective-permute-start.19 = (bf16[512,256]{1,0:T(8,128)(2,1)S(1)}, bf16[512,256]{1,0:T(8,128)(2,1)S(1)}, u32[]{:S(2)}, u32[]{:S(2)}) collective-permute-start(bf16[512,256]{1,0:T(8,128)(2,1)S(1)} %fusion.3), channel_id=1, source_target_pairs={{0,8},{2,10},{4,12},{6,14},{8,0},{10,2},{12,4},{14,6},{1,9},{3,11}... | collective-permute-start | bytes 786440 | tf_op jit(solution)/shard_map/ppermute | solution.py:361
  134.5 17.4 %collective-permute-done.17 = bf16[128,768]{1,0:T(8,128)(2,1)S(1)} collective-permute-done((bf16[128,768]{1,0:T(8,128)(2,1)S(1)}, bf16[128,768]{1,0:T(8,128)(2,1)S(1)}, u32[]{:S(2)}, u32[]{:S(2)}) %collective-permute-start.17) | collective-permute-done | bytes 196640 | tf_op jit(solution)/shard_map/ppermute | solution.py:351
  151.9 4.1 %collective-permute-done.16 = bf16[128,768]{1,0:T(8,128)(2,1)S(1)} collective-permute-done((bf16[128,768]{1,0:T(8,128)(2,1)S(1)}, bf16[128,768]{1,0:T(8,128)(2,1)S(1)}, u32[]{:S(2)}, u32[]{:S(2)}) %collective-permute-start.16) | collective-permute-done | bytes 196640 | tf_op jit(solution)/shard_map/ppermute | solution.py:351
  (55 shorter events, 5.3 us)
Async XLA Ops:
  0.6 0.9 copy-start.8
  7.4 17.2 %collective-permute-start.1 = (bf16[256,1024]{1,0:T(8,128)(2,1)S(1)}, bf16[256,1024]{1,0:T(8,128)(2,1)S(1)}, u32[]{:S(2)}, u32[]{:S(2)}) collective-permute-start(bf16[256,1024]{1,0:T(8,128)(2,1)S(1)} %get-tuple-element.21), channel_id=1, source_target_pairs={{0,16},{16,32},{32,48},{48,0},{64,80},{80,96},{96,112},{112,64},{1... | collective-permute-start | bytes 1572872 | tf_op jit(solution)/shard_map/ppermute | solution.py:346
  8.9 18.9 %collective-permute-start.2 = (bf16[256,1024]{1,0:T(8,128)(2,1)}, bf16[256,1024]{1,0:T(8,128)(2,1)S(1)}, u32[]{:S(2)}, u32[]{:S(2)}) collective-permute-start(bf16[256,1024]{1,0:T(8,128)(2,1)} %get-tuple-element.22), channel_id=1, source_target_pairs={{0,48},{16,0},{32,16},{48,32},{64,112},{80,64},{96,80},{112,96},{1... | collective-permute-start | bytes 1572872 | tf_op jit(solution)/shard_map/ppermute | solution.py:346
  10.7 28.1 %all-to-all-start = ((bf16[16,16,1024]{2,1,0:T(8,128)(2,1)}), bf16[16,16,1024]{2,1,0:T(8,128)(2,1)S(1)}, u32[]{:S(2)}, u32[]{:S(2)}) async-start(bf16[16,16,1024]{2,1,0:T(8,128)(2,1)} %bitcast.4), calls=%async_computation | async-start | bytes 1048576 | tf_op jit(solution)/shard_map/all_to_all | solution.py:385
  17.5 32.9 %collective-permute-start = (bf16[256,1024]{1,0:T(8,128)(2,1)}, bf16[256,1024]{1,0:T(8,128)(2,1)}, u32[]{:S(2)}, u32[]{:S(2)}) collective-permute-start(bf16[256,1024]{1,0:T(8,128)(2,1)} %get-tuple-element.19), channel_id=1, source_target_pairs={{0,32},{16,48},{32,0},{48,16},{64,96},{80,112},{96,64},{112,80},{1... | collective-permute-start | bytes 1572872 | tf_op jit(solution)/shard_map/ppermute | solution.py:346
  27.8 0.8 copy-start.17
  28.6 1.0 copy-start.18
  29.7 9.1 %copy-start.15 = (s32[1,16]{1,0:T(1,128)S(1)}, s32[1,16]{1,0:T(1,128)}, u32[]{:S(2)}) copy-start(s32[1,16]{1,0:T(1,128)} %param.12) | copy-start | bytes 196
  29.7 9.1 %copy-start.16 = (s32[1,16]{1,0:T(1,128)S(1)}, s32[1,16]{1,0:T(1,128)}, u32[]{:S(2)}) copy-start(s32[1,16]{1,0:T(1,128)} %param.13) | copy-start | bytes 196
  29.8 20.6 %copy-start.4 = (bf16[3,256,1024]{2,1,0:T(8,128)(2,1)}, bf16[3,256,1024]{2,1,0:T(8,128)(2,1)S(1)}, u32[]{:S(2)}) copy-start(bf16[3,256,1024]{2,1,0:T(8,128)(2,1)S(1)} %stack.23.rest_0_.near_ref) | copy-start | bytes 4718596
  40.3 25.9 %all-to-all-start.2 = ((bf16[16,2,16,512]{3,2,1,0:T(8,128)(2,1)}), bf16[16,2,16,512]{3,2,1,0:T(8,128)(2,1)S(1)}, u32[]{:S(2)}, u32[]{:S(2)}) async-start(bf16[16,2,16,512]{3,2,1,0:T(8,128)(2,1)} %pick.3), calls=%async_computation.2 | async-start | bytes 1048576 | tf_op jit(solution)/shard_map/all_to_all | solution.py:385
  51.5 41.0 %copy-start = (bf16[4096,256]{1,0:T(8,128)(2,1)S(1)}, bf16[4096,256]{1,0:T(8,128)(2,1)}, u32[]{:S(2)}) copy-start(bf16[4096,256]{1,0:T(8,128)(2,1)} %wq_ref.3) | copy-start | bytes 6291460
  53.0 0.8 copy-start.6
  66.2 23.2 %all-to-all-start.1 = ((bf16[16,2,16,512]{3,2,1,0:T(8,128)(2,1)}), bf16[16,2,16,512]{3,2,1,0:T(8,128)(2,1)S(1)}, u32[]{:S(2)}, u32[]{:S(2)}) async-start(bf16[16,2,16,512]{3,2,1,0:T(8,128)(2,1)} %pick.2), calls=%async_computation.1 | async-start | bytes 1048576 | tf_op jit(solution)/shard_map/all_to_all | solution.py:385
  74.1 8.3 %collective-permute-start.5 = (f32[8,256]{1,0:T(8,128)S(1)}, f32[8,256]{1,0:T(8,128)S(1)}, u32[]{:S(2)}, u32[]{:S(2)}) collective-permute-start(f32[8,256]{1,0:T(8,128)S(1)} %get-tuple-element.23), channel_id=1, source_target_pairs={{0,48},{16,0},{32,16},{48,32},{64,112},{80,64},{96,80},{112,96},{1... | collective-permute-start | bytes 24584 | tf_op jit(solution)/shard_map/ppermute | solution.py:346
  76.8 7.8 %collective-permute-start.4 = (f32[8,256]{1,0:T(8,128)S(1)}, f32[8,256]{1,0:T(8,128)S(1)}, u32[]{:S(2)}, u32[]{:S(2)}) collective-permute-start(f32[8,256]{1,0:T(8,128)S(1)} %get-tuple-element.23), channel_id=1, source_target_pairs={{0,32},{16,48},{32,0},{48,16},{64,96},{80,112},{96,64},{112,80},{1... | collective-permute-start | bytes 24584 | tf_op jit(solution)/shard_map/ppermute | solution.py:346
  77.7 6.9 %collective-permute-start.3 = (f32[8,256]{1,0:T(8,128)S(1)}, f32[8,256]{1,0:T(8,128)S(1)}, u32[]{:S(2)}, u32[]{:S(2)}) collective-permute-start(f32[8,256]{1,0:T(8,128)S(1)} %get-tuple-element.23), channel_id=1, source_target_pairs={{0,16},{16,32},{32,48},{48,0},{64,80},{80,96},{96,112},{112,64},{1... | collective-permute-start | bytes 24584 | tf_op jit(solution)/shard_map/ppermute | solution.py:346
  78.5 21.9 %collective-permute-start.9 = (bf16[256,256]{1,0:T(8,128)(2,1)S(1)}, bf16[256,256]{1,0:T(8,128)(2,1)S(1)}, u32[]{:S(2)}, u32[]{:S(2)}) collective-permute-start(bf16[256,256]{1,0:T(8,128)(2,1)S(1)} %get-tuple-element.26.refs_0_.gq_ref), channel_id=1, source_target_pairs={{0,16},{16,32},{32,48},{48,0},{64,80},{80,96},{96,112},{112,64},{1... | collective-permute-start | bytes 393224 | tf_op jit(solution)/shard_map/ppermute | solution.py:346
  80.3 21.8 %collective-permute-start.10 = (bf16[256,256]{1,0:T(8,128)(2,1)S(1)}, bf16[256,256]{1,0:T(8,128)(2,1)S(1)}, u32[]{:S(2)}, u32[]{:S(2)}) collective-permute-start(bf16[256,256]{1,0:T(8,128)(2,1)S(1)} %get-tuple-element.26.refs_0_.gq_ref), channel_id=1, source_target_pairs={{0,32},{16,48},{32,0},{48,16},{64,96},{80,112},{96,64},{112,80},{1... | collective-permute-start | bytes 393224 | tf_op jit(solution)/shard_map/ppermute | solution.py:346
  82.4 19.8 %collective-permute-start.11 = (bf16[256,256]{1,0:T(8,128)(2,1)S(1)}, bf16[256,256]{1,0:T(8,128)(2,1)S(1)}, u32[]{:S(2)}, u32[]{:S(2)}) collective-permute-start(bf16[256,256]{1,0:T(8,128)(2,1)S(1)} %get-tuple-element.26.refs_0_.gq_ref), channel_id=1, source_target_pairs={{0,48},{16,0},{32,16},{48,32},{64,112},{80,64},{96,80},{112,96},{1... | collective-permute-start | bytes 393224 | tf_op jit(solution)/shard_map/ppermute | solution.py:346
  84.6 4.0 %collective-permute-start.6 = (f32[4,8,256]{2,1,0:T(8,128)S(1)}, f32[4,8,256]{2,1,0:T(8,128)S(1)}, u32[]{:S(2)}, u32[]{:S(2)}) collective-permute-start(f32[4,8,256]{2,1,0:T(8,128)S(1)} %pad_maximum_fusion.rest_0_), channel_id=1, source_target_pairs={{0,64},{16,80},{32,96},{48,112},{64,128},{80,144},{96,160},{112,17... | collective-permute-start | bytes 98312 | tf_op jit(solution)/shard_map/ppermute | solution.py:351
  84.7 5.1 %collective-permute-start.7 = (f32[4,8,256]{2,1,0:T(8,128)S(1)}, f32[4,8,256]{2,1,0:T(8,128)S(1)}, u32[]{:S(2)}, u32[]{:S(2)}) collective-permute-start(f32[4,8,256]{2,1,0:T(8,128)S(1)} %pad_maximum_fusion.rest_0_), channel_id=1, source_target_pairs={{0,128},{16,144},{32,160},{48,176},{64,192},{80,208},{96,224},{112... | collective-permute-start | bytes 98312 | tf_op jit(solution)/shard_map/ppermute | solution.py:351
  88.6 3.9 %collective-permute-start.8 = (f32[4,8,256]{2,1,0:T(8,128)S(1)}, f32[4,8,256]{2,1,0:T(8,128)S(1)}, u32[]{:S(2)}, u32[]{:S(2)}) collective-permute-start(f32[4,8,256]{2,1,0:T(8,128)S(1)} %pad_maximum_fusion.rest_0_), channel_id=1, source_target_pairs={{0,192},{16,208},{32,224},{48,240},{64,0},{80,16},{96,32},{112,48}... | collective-permute-start | bytes 98312 | tf_op jit(solution)/shard_map/ppermute | solution.py:351
  92.5 1.6 %copy-start.1 = (bf16[4096,256]{1,0:T(8,128)(2,1)S(1)}, bf16[4096,256]{1,0:T(8,128)(2,1)}, u32[]{:S(2)}) copy-start(bf16[4096,256]{1,0:T(8,128)(2,1)} %wk_ref.3) | copy-start | bytes 6291460
  94.1 1.6 %copy-start.2 = (bf16[4096,256]{1,0:T(8,128)(2,1)S(1)}, bf16[4096,256]{1,0:T(8,128)(2,1)}, u32[]{:S(2)}) copy-start(bf16[4096,256]{1,0:T(8,128)(2,1)} %wv_ref.3) | copy-start | bytes 6291460
  98.9 13.4 %collective-permute-start.12 = (bf16[256,512]{1,0:T(8,128)(2,1)S(1)}, bf16[256,512]{1,0:T(8,128)(2,1)}, u32[]{:S(2)}, u32[]{:S(2)}) collective-permute-start(bf16[256,512]{1,0:T(8,128)(2,1)S(1)} %get-tuple-element.27.refs_4_.gkv_ref), channel_id=1, source_target_pairs={{0,16},{16,32},{32,48},{48,0},{64,80},{80,96},{96,112},{112,64},{1... | collective-permute-start | bytes 786440 | tf_op jit(solution)/shard_map/ppermute | solution.py:346
  98.9 13.4 %collective-permute-start.13 = (bf16[256,512]{1,0:T(8,128)(2,1)S(1)}, bf16[256,512]{1,0:T(8,128)(2,1)}, u32[]{:S(2)}, u32[]{:S(2)}) collective-permute-start(bf16[256,512]{1,0:T(8,128)(2,1)S(1)} %get-tuple-element.27.refs_4_.gkv_ref), channel_id=1, source_target_pairs={{0,32},{16,48},{32,0},{48,16},{64,96},{80,112},{96,64},{112,80},{1... | collective-permute-start | bytes 786440 | tf_op jit(solution)/shard_map/ppermute | solution.py:346
  100.4 11.9 %collective-permute-start.14 = (bf16[256,512]{1,0:T(8,128)(2,1)S(1)}, bf16[256,512]{1,0:T(8,128)(2,1)}, u32[]{:S(2)}, u32[]{:S(2)}) collective-permute-start(bf16[256,512]{1,0:T(8,128)(2,1)S(1)} %get-tuple-element.27.refs_4_.gkv_ref), channel_id=1, source_target_pairs={{0,48},{16,0},{32,16},{48,32},{64,112},{80,64},{96,80},{112,96},{1... | collective-permute-start | bytes 786440 | tf_op jit(solution)/shard_map/ppermute | solution.py:346
  104.0 1.3 copy-start.3
  105.3 0.7 copy-start.9
  106.0 0.7 copy-start.11
  106.6 0.7 copy-start.13
  107.3 5.1 %copy-start.5 = (bf16[3,256,1024]{2,1,0:T(8,128)(2,1)S(1)}, bf16[3,256,1024]{2,1,0:T(8,128)(2,1)}, u32[]{:S(2)}) copy-start(bf16[3,256,1024]{2,1,0:T(8,128)(2,1)} %copy-done.4) | copy-start | bytes 4718596
  107.3 20.6 %all-to-all-start.3 = ((bf16[4,2,512,256]{3,2,1,0:T(8,128)(2,1)}), bf16[4,2,512,256]{3,2,1,0:T(8,128)(2,1)}, u32[]{:S(2)}, u32[]{:S(2)}) async-start(bf16[4,2,512,256]{3,2,1,0:T(8,128)(2,1)} %copy-done.3), calls=%async_computation.3 | async-start | bytes 4194304 | tf_op jit(solution)/shard_map/all_to_all | solution.py:405
  112.3 1.0 copy-start.7
  113.4 0.9 copy-start.10
  114.3 0.9 copy-start.12
  115.2 0.9 copy-start.14
  120.0 2.5 %collective-permute-start.15 = (bf16[4,128,768]{2,1,0:T(8,128)(2,1)}, bf16[4,128,768]{2,1,0:T(8,128)(2,1)S(1)}, u32[]{:S(2)}, u32[]{:S(2)}) collective-permute-start(bf16[4,128,768]{2,1,0:T(8,128)(2,1)} %get-tuple-element.29), channel_id=1, source_target_pairs={{0,1},{1,0},{2,3},{3,2},{4,5},{5,4},{6,7},{7,6},{8,9},{9,8},{10,11... | collective-permute-start | bytes 2359304 | tf_op jit(solution)/shard_map/ppermute | solution.py:365
  122.7 11.8 %collective-permute-start.18 = (bf16[128,768]{1,0:T(8,128)(2,1)S(1)}, bf16[128,768]{1,0:T(8,128)(2,1)S(1)}, u32[]{:S(2)}, u32[]{:S(2)}) collective-permute-start(bf16[128,768]{1,0:T(8,128)(2,1)S(1)} %get-tuple-element.31), channel_id=1, source_target_pairs={{0,192},{16,208},{32,224},{48,240},{64,0},{80,16},{96,32},{112,48}... | collective-permute-start | bytes 589832 | tf_op jit(solution)/shard_map/ppermute | solution.py:351
  123.5 28.4 %collective-permute-start.17 = (bf16[128,768]{1,0:T(8,128)(2,1)S(1)}, bf16[128,768]{1,0:T(8,128)(2,1)S(1)}, u32[]{:S(2)}, u32[]{:S(2)}) collective-permute-start(bf16[128,768]{1,0:T(8,128)(2,1)S(1)} %get-tuple-element.32), channel_id=1, source_target_pairs={{0,128},{16,144},{32,160},{48,176},{64,192},{80,208},{96,224},{112... | collective-permute-start | bytes 589832 | tf_op jit(solution)/shard_map/ppermute | solution.py:351
  127.9 28.1 %collective-permute-start.16 = (bf16[128,768]{1,0:T(8,128)(2,1)S(1)}, bf16[128,768]{1,0:T(8,128)(2,1)S(1)}, u32[]{:S(2)}, u32[]{:S(2)}) collective-permute-start(bf16[128,768]{1,0:T(8,128)(2,1)S(1)} %get-tuple-element.30), channel_id=1, source_target_pairs={{0,64},{16,80},{32,96},{48,112},{64,128},{80,144},{96,160},{112,17... | collective-permute-start | bytes 589832 | tf_op jit(solution)/shard_map/ppermute | solution.py:351
  129.9 26.9 %collective-permute-start.19 = (bf16[512,256]{1,0:T(8,128)(2,1)S(1)}, bf16[512,256]{1,0:T(8,128)(2,1)S(1)}, u32[]{:S(2)}, u32[]{:S(2)}) collective-permute-start(bf16[512,256]{1,0:T(8,128)(2,1)S(1)} %fusion.3), channel_id=1, source_target_pairs={{0,8},{2,10},{4,12},{6,14},{8,0},{10,2},{12,4},{14,6},{1,9},{3,11}... | collective-permute-start | bytes 786440 | tf_op jit(solution)/shard_map/ppermute | solution.py:361

commit v2 on v1

--- a/solution.py
+++ b/solution.py
@@ -77,10 +77,13 @@
             else:
                 o_ref[:, cols] = (acc[:, cols] + prod).astype(BF)
     last.wait()
+    quarter = xs.shape[0] // YS
+    mine = pl.multiple_of(lax.rem(lax.axis_index("head"), YS) * quarter, quarter)
     for k in range(XS):
+        rows = slice(None) if k == 0 else pl.ds(mine, quarter)
         for z in range(ZS):
             start = pl.multiple_of((z * XS + lax.rem(my_x + k, XS)) * width, width)
-            outs[k][:, z * width : (z + 1) * width] = xs[:, pl.ds(start, width)]
+            outs[k][:, z * width : (z + 1) * width] = xs[rows, pl.ds(start, width)]
 
 
 def project(x, wq, wk, wv, do):
@@ -91,7 +94,7 @@
         in_specs=[ANY] * 5,
         out_specs=[VMEM] * (1 + XS),
         out_shape=[jax.ShapeDtypeStruct((t, 4 * n), BF)]
-        + [jax.ShapeDtypeStruct((t, d // XS), BF)] * XS,
+        + [jax.ShapeDtypeStruct((t if k == 0 else t // YS, d // XS), BF) for k in range(XS)],
         scratch_shapes=[
             pltpu.VMEM((t, d), BF),
             pltpu.VMEM((3, d, n), BF),
@@ -110,7 +113,7 @@
         o_ref[i] = r[...]
 
 
-def stack(parts, flops):
+def stack(parts):
     shape = (len(parts), *parts[0].shape)
     return pl.pallas_call(
         _stack_body,
@@ -118,9 +121,32 @@
         out_specs=VMEM,
         out_shape=jax.ShapeDtypeStruct(shape, BF),
         compiler_params=_params(SMALL),
-        cost_estimate=_cost(flops, 0),
+        cost_estimate=_cost(HINT, 0),
         name="stack",
     )(*parts)
+
+
+def _merge_body(own_ref, *refs):
+    parts, o_ref = refs[:YS], refs[-1]
+    quarter = parts[0].shape[1]
+    my_y = lax.rem(lax.axis_index("head"), YS)
+    o_ref[0] = own_ref[...]
+    for j in range(YS):
+        at = pl.multiple_of(lax.rem(my_y + YS - j, YS) * quarter, quarter)
+        for k in range(1, XS):
+            o_ref[k, pl.ds(at, quarter), :] = parts[j][k - 1]
+
+
+def merge(own, parts):
+    return pl.pallas_call(
+        _merge_body,
+        in_specs=[VMEM] * (1 + YS),
+        out_specs=VMEM,
+        out_shape=jax.ShapeDtypeStruct((XS, *own.shape), BF),
+        compiler_params=_params(SMALL),
+        cost_estimate=_cost(HINT, 0),
+        name="merge",
+    )(own, *parts)
 
 
 def _pick_kv_body(p1_ref, p2_ref, all_ref, *rest):
@@ -277,9 +303,9 @@
     )(p1, p2, qkv, qdo, *stats, *after)
 
 
-def _wgrad_body(near_ref, far_ref, *refs):
+def _wgrad_body(x_ref, *refs):
     gq, gkv = refs[0:XS], refs[XS : 2 * XS]
-    xs = (near_ref.at[0], near_ref.at[1], far_ref.at[0], near_ref.at[2])
+    xs = [x_ref.at[k] for k in range(XS)]
     keep_ref, send_ref = refs[-2:]
     first = lax.axis_index("cuts") == 0
     half, n = keep_ref.shape[1], gq[0].shape[1]
@@ -290,23 +316,45 @@
                 part = _tn(x[:, z * 2 * half : (z + 1) * 2 * half], g[...])
                 acc = part if acc is None else acc + part
             top, low = acc[:half], acc[half:]
-            keep_ref[z, :, cols] = jnp.where(first, top, low)
+            keep_ref[z, :, cols] = jnp.where(first, top, low).astype(BF)
             send_ref[z, :, cols] = jnp.where(first, low, top).astype(BF)
 
 
-def wgrad(near, far, gq, gkv):
-    _, t, rows = near.shape
+def wgrad(xs, gq, gkv):
+    _, t, rows = xs.shape
     n = gq[0].shape[1]
     shape = (ZS, rows // (2 * ZS), 3 * n)
     return pl.pallas_call(
         _wgrad_body,
-        in_specs=[VMEM] * (2 + 2 * XS),
+        in_specs=[VMEM] * (1 + 2 * XS),
         out_specs=[VMEM, VMEM],
-        out_shape=[jax.ShapeDtypeStruct(shape, F32), jax.ShapeDtypeStruct(shape, BF)],
+        out_shape=[jax.ShapeDtypeStruct(shape, BF), jax.ShapeDtypeStruct(shape, BF)],
         compiler_params=_params(SMALL),
         cost_estimate=_cost(2 * XS * t * rows * 3 * n, 2 * XS * t * (rows + 3 * n) + 6 * rows * n),
         name="wgrad",
-    )(near, far, *gq, *gkv)
+    )(xs, *gq, *gkv)
+
+
+def _pair_body(keep_ref, got_ref, own_ref, *outs):
+    my_z = lax.axis_index("doc") // XS
+    own_ref[...] = keep_ref[my_z].astype(F32) + got_ref[my_z].astype(F32)
+    for k, o_ref in enumerate(outs):
+        to = lax.rem(my_z + k + 1, ZS)
+        o_ref[...] = (keep_ref[to].astype(F32) + got_ref[to].astype(F32)).astype(BF)
+
+
+def pair(keep, got):
+    piece = keep.shape[1:]
+    return pl.pallas_call(
+        _pair_body,
+        in_specs=[VMEM] * 2,
+        out_specs=[VMEM] * ZS,
+        out_shape=[jax.ShapeDtypeStruct(piece, F32)]
+        + [jax.ShapeDtypeStruct(piece, BF)] * (ZS - 1),
+        compiler_params=_params(SMALL),
+        cost_estimate=_cost(4 * HINT // 30, 6 * keep.size),
+        name="pair",
+    )(keep, got)
 
 
 def _xgrad_body(wq_ref, wk_ref, wv_ref, gq_ref, gkv_ref, *rest):
@@ -379,19 +427,17 @@
     docs = lax.axis_size("doc")
     rows = t // docs
     p1, p2 = partner_one[0], partner_two[0]
-    me = lax.axis_index("doc")
-    my_z = me // XS
     def spread(v):
         return lax.all_to_all(v, "doc", split_axis=0, concat_axis=0, tiled=True)
 
     qkvd, *cuts = project(x, weight_query, weight_key, weight_value, do)
     blocks = spread(qkvd.reshape(docs, rows, 4 * n))
 
-    near = stack([cuts[0], shift_x(cuts[1], 1), shift_x(cuts[3], 3)], HINT)
-    far = stack([shift_x(cuts[2], 2)], HINT)
-
-    kv = spread(pick(_pick_kv_body, p1, p2, blocks, [near]))
-    qdo = spread(pick(_pick_qdo_body, p1, p2, blocks, [far]))
+    quarters = stack([shift_x(cuts[k], k) for k in range(1, XS)])
+    columns = merge(cuts[0], [shift_y(quarters, j) if j else quarters for j in range(YS)])
+
+    kv = spread(pick(_pick_kv_body, p1, p2, blocks, [quarters]))
+    qdo = spread(pick(_pick_qdo_body, p1, p2, blocks, [columns]))
     gq, stats = attend(factor, qkvd, kv, [])
     weights = [weight_query, weight_key, weight_value]
     row = jnp.stack([shift_x(stats, k) if k else stats for k in range(XS)])
@@ -406,16 +452,13 @@
         terms, "head", split_axis=0, concat_axis=0, tiled=True, axis_index_groups=groups
     )
     mine, theirs = wgrad(
-        near,
-        far,
+        columns,
         [gq_x[k] for k in range(XS)],
         [gkv_x[k] for k in range(XS)],
     )
-    pair = (mine + swap_cores(theirs).astype(F32)).astype(BF)
-    total = lax.dynamic_index_in_dim(pair, my_z, axis=0, keepdims=False).astype(F32)
+    total, *pieces = pair(mine, swap_cores(theirs))
     for k in range(1, ZS):
-        out = lax.dynamic_index_in_dim(pair, (my_z + k) % ZS, axis=0, keepdims=False)
-        total = total + shift_z(out, k).astype(F32)
+        total = total + shift_z(pieces[k - 1], k).astype(F32)
     sums = jnp.sum(terms.astype(F32), axis=0)
     my_half = lax.axis_index("head") // YS
     keep = lax.dynamic_index_in_dim(sums, my_half, axis=0, keepdims=False)

time: 158 us -> 142 us (0.90)
  waiting for transfers between devices: 57.6 us -> 47.4 us
  local copies, waits for them, and re-layouts: 14.6 us -> 9.6 us
    ppermute x12, waiting for transfers between devices: 7.38 us -> 0.03 us  [shift_x(): return lax.ppermute(v, 'doc', pairs)]
    ppermute x6, waiting for transfers between devices: 26.3 us -> 20.3 us  [shift_z(): return lax.ppermute(v, 'doc', pairs)]
    all_to_all x3, starting transfers between devices: 22.1 us -> 16.3 us  [spread(): return lax.all_to_all(v, 'doc', split_axis=0, concat_axis=0, tiled=True)]
    all_to_all x1, waiting for transfers between devices: 0.01 us -> 5.66 us  [per_device(): lax.all_to_all(terms, 'head', split_axis=0, concat_axis=0, tiled=True, ax...]
    ppermute x0 -> x3, starting transfers between devices: none -> 5 us  [shift_y(): return lax.ppermute(v, 'head', pairs)]
    unnamed x38 -> x22, local copies, waits for them, and re-layouts: 13.8 us -> 8.81 us
    all_to_all x3, waiting for transfers between devices: 21.4 us -> 18.9 us  [spread(): return lax.all_to_all(v, 'doc', split_axis=0, concat_axis=0, tiled=True)]
    pallas_call x1 -> x3, Pallas kernels: 3.88 us -> 4.02 us  [the longest x1 3.71 us: wgrad(): pl.pallas_call(_wgrad_body, in_specs=[VMEM] * (1 + 2 * XS), out_specs=[VM...]
  transfers between devices with their start and end apart: 24 -> 27, of which waited for: 10 -> 9; matrix products, arithmetic and copies ran while one was open for 2% -> 2% of each run, Pallas kernels for 10% -> 11%
where the time goes in v2:
time: 142 us; the launch traced here: 140 us
  starting transfers between devices  59.3 us (42%)
  waiting for transfers between devices  47.4 us (33%)
  Pallas kernels  20.2 us (14%)
  local copies, waits for them, and re-layouts  9.6 us (7%)
  other arithmetic  2.88 us (2%)
    ppermute x6, waiting for transfers between devices, shift_z(): return lax.ppermute(v, 'doc', pairs)  20.3 us
    ppermute x12, starting transfers between devices, shift_x(): return lax.ppermute(v, 'doc', pairs)  19.4 us
    all_to_all x3, waiting for transfers between devices, spread(): return lax.all_to_all(v, 'doc', split_axis=0, concat_axis=0, tiled=True)  18.9 us
    all_to_all x3, starting transfers between devices, spread(): return lax.all_to_all(v, 'doc', split_axis=0, concat_axis=0, tiled=True)  16.3 us
    unnamed x22, local copies, waits for them, and re-layouts  8.81 us
    ppermute x6, starting transfers between devices, shift_z(): return lax.ppermute(v, 'doc', pairs)  7.83 us
    all_to_all x1, waiting for transfers between devices, per_device(): lax.all_to_all(terms, 'head', split_axis=0, concat_axis=0, tiled=True, ax...  5.66 us
    ppermute x1, starting transfers between devices, swap_halves(): return lax.ppermute(v, 'head', pairs)  5.44 us
  transfers between devices with their start and end apart: 27, of which 9 were waited for; matrix products, arithmetic and copies ran while one was open for 2% of the time, Pallas kernels for 11%

profile of v2, /device:TPU:72, one launch (start us, length us, event | category | flops | bytes accessed | tf_op | source)
XLA Modules:
  0.0 140.2 jit_solution(6392187932716932335)
XLA Ops:
  0.6 0.9 copy-done.6
  1.5 5.4 %project.1 = (bf16[256,1024]{1,0:T(8,128)(2,1)}, bf16[256,1024]{1,0:T(8,128)(2,1)S(1)}, bf16[64,1024]{1,0:T(8,128)(2,1)S(1)}, bf16[64,1024]{1,0:T(8,128)(2,1)S(1)}, bf16[64,1024]{1,0:T(8,128)(2,1)S(1)}) custom-call(bf16[256,4096]{1,0:T(8,128)(2,1)} %bitcast.29, bf16[4096,256]{1,0:T(8,128)(2,1)} %wq_ref.3, bf16[4096,256]{1,0:T(8,128)(2,1)} %wk_ref.3, ...), custom_call_target="tpu_custom_call" | custom-call | flops 1610612736 | bytes 8388608 | tf_op jit(solution)/shard_map/project/pallas_call | solution.py:92
  7.0 1.6 %collective-permute-start = (bf16[64,1024]{1,0:T(8,128)(2,1)S(1)}, bf16[64,1024]{1,0:T(8,128)(2,1)S(1)}, u32[]{:S(2)}, u32[]{:S(2)}) collective-permute-start(bf16[64,1024]{1,0:T(8,128)(2,1)S(1)} %get-tuple-element.24), channel_id=1, source_target_pairs={{0,16},{16,32},{32,48},{48,0},{64,80},{80,96},{96,112},{112,64},{1... | collective-permute-start | bytes 393224 | tf_op jit(solution)/shard_map/ppermute | solution.py:394
  8.5 2.7 %collective-permute-start.1 = (bf16[64,1024]{1,0:T(8,128)(2,1)S(1)}, bf16[64,1024]{1,0:T(8,128)(2,1)S(1)}, u32[]{:S(2)}, u32[]{:S(2)}) collective-permute-start(bf16[64,1024]{1,0:T(8,128)(2,1)S(1)} %get-tuple-element.25), channel_id=1, source_target_pairs={{0,32},{16,48},{32,0},{48,16},{64,96},{80,112},{96,64},{112,80},{1... | collective-permute-start | bytes 393224 | tf_op jit(solution)/shard_map/ppermute | solution.py:394
  11.3 1.4 %collective-permute-start.2 = (bf16[64,1024]{1,0:T(8,128)(2,1)S(1)}, bf16[64,1024]{1,0:T(8,128)(2,1)S(1)}, u32[]{:S(2)}, u32[]{:S(2)}) collective-permute-start(bf16[64,1024]{1,0:T(8,128)(2,1)S(1)} %get-tuple-element.26), channel_id=1, source_target_pairs={{0,48},{16,0},{32,16},{48,32},{64,112},{80,64},{96,80},{112,96},{1... | collective-permute-start | bytes 393224 | tf_op jit(solution)/shard_map/ppermute | solution.py:394
  12.7 5.6 %all-to-all-start = ((bf16[16,16,1024]{2,1,0:T(8,128)(2,1)}), bf16[16,16,1024]{2,1,0:T(8,128)(2,1)S(1)}, u32[]{:S(2)}, u32[]{:S(2)}) async-start(bf16[16,16,1024]{2,1,0:T(8,128)(2,1)} %bitcast.4), calls=%async_computation | async-start | bytes 1048576 | tf_op jit(solution)/shard_map/all_to_all | solution.py:431
  18.4 1.7 %collective-permute-start.3 = (bf16[3,64,1024]{2,1,0:T(8,128)(2,1)S(1)}, bf16[3,64,1024]{2,1,0:T(8,128)(2,1)S(1)}, u32[]{:S(2)}, u32[]{:S(2)}) collective-permute-start(bf16[3,64,1024]{2,1,0:T(8,128)(2,1)S(1)} %stack.21.refs_0_.rest_0_), channel_id=1, source_target_pairs={{0,2},{2,4},{4,6},{6,0},{8,10},{10,12},{12,14},{14,8},{1,3},{3,5},... | collective-permute-start | bytes 1179656 | tf_op jit(solution)/shard_map/ppermute | solution.py:404
  20.0 0.9 collective-permute-start.4
  21.0 2.4 %collective-permute-start.5 = (bf16[3,64,1024]{2,1,0:T(8,128)(2,1)S(1)}, bf16[3,64,1024]{2,1,0:T(8,128)(2,1)S(1)}, u32[]{:S(2)}, u32[]{:S(2)}) collective-permute-start(bf16[3,64,1024]{2,1,0:T(8,128)(2,1)S(1)} %stack.21.refs_0_.rest_0_), channel_id=1, source_target_pairs={{0,6},{2,0},{4,2},{6,4},{8,14},{10,8},{12,10},{14,12},{1,7},{3,1},... | collective-permute-start | bytes 1179656 | tf_op jit(solution)/shard_map/ppermute | solution.py:404
  23.4 8.6 %all-to-all-done.all_ref = bf16[16,16,1024]{2,1,0:T(8,128)(2,1)S(1)} async-done(((bf16[16,16,1024]{2,1,0:T(8,128)(2,1)}), bf16[16,16,1024]{2,1,0:T(8,128)(2,1)S(1)}, u32[]{:S(2)}, u32[]{:S(2)}) %all-to-all-start) | async-done | bytes 524320 | tf_op jit(solution)/shard_map/all_to_all | solution.py:431
  32.0 1.5 %pick.3 = bf16[16,2,16,512]{3,2,1,0:T(8,128)(2,1)} custom-call(s32[16]{0:T(128)S(1)} %bitcast.23, s32[16]{0:T(128)S(1)} %bitcast.26, bf16[16,16,1024]{2,1,0:T(8,128)(2,1)S(1)} %all-to-all-done.all_ref, bf16[3,64,1024]{2,1,0:T(8,128)(2,1)S(1)} %stack.21.refs_0_.rest_0_), custom_call_target="tpu_custom_call" | custom-call | bytes 1048576 | tf_op jit(solution)/shard_map/pick/pallas_call | solution.py:181
  33.5 5.4 %all-to-all-start.2 = ((bf16[16,2,16,512]{3,2,1,0:T(8,128)(2,1)}), bf16[16,2,16,512]{3,2,1,0:T(8,128)(2,1)S(1)}, u32[]{:S(2)}, u32[]{:S(2)}) async-start(bf16[16,2,16,512]{3,2,1,0:T(8,128)(2,1)} %pick.3), calls=%async_computation.2 | async-start | bytes 1048576 | tf_op jit(solution)/shard_map/all_to_all | solution.py:431
  39.1 1.5 %pick.2 = bf16[16,2,16,512]{3,2,1,0:T(8,128)(2,1)} custom-call(s32[16]{0:T(128)S(1)} %bitcast.24, s32[16]{0:T(128)S(1)} %bitcast.27, bf16[16,16,1024]{2,1,0:T(8,128)(2,1)S(1)} %all-to-all-done.all_ref, bf16[4,256,1024]{2,1,0:T(8,128)(2,1)S(1)} %merge.1.rest_0_.x_ref), custom_call_target="tpu_custom_call" | custom-call | bytes 1048576 | tf_op jit(solution)/shard_map/pick/pallas_call | solution.py:181
  40.5 1.4 copy-done.4
  41.9 10.3 %all-to-all-done.2.kv_ref = bf16[16,2,16,512]{3,2,1,0:T(8,128)(2,1)S(1)} async-done(((bf16[16,2,16,512]{3,2,1,0:T(8,128)(2,1)}), bf16[16,2,16,512]{3,2,1,0:T(8,128)(2,1)S(1)}, u32[]{:S(2)}, u32[]{:S(2)}) %all-to-all-start.2) | async-done | bytes 524320 | tf_op jit(solution)/shard_map/all_to_all | solution.py:431
  52.2 5.4 %all-to-all-start.1 = ((bf16[16,2,16,512]{3,2,1,0:T(8,128)(2,1)}), bf16[16,2,16,512]{3,2,1,0:T(8,128)(2,1)S(1)}, u32[]{:S(2)}, u32[]{:S(2)}) async-start(bf16[16,2,16,512]{3,2,1,0:T(8,128)(2,1)} %pick.2), calls=%async_computation.1 | async-start | bytes 1048576 | tf_op jit(solution)/shard_map/all_to_all | solution.py:431
  57.6 2.7 %attend.1 = (bf16[256,256]{1,0:T(8,128)(2,1)S(1)}, f32[8,256]{1,0:T(8,128)S(1)}) custom-call(bf16[256,1024]{1,0:T(8,128)(2,1)} %get-tuple-element.22.qkv_ref, bf16[16,2,16,512]{3,2,1,0:T(8,128)(2,1)S(1)} %all-to-all-done.2.kv_ref), custom_call_target="tpu_custom_call" | custom-call | flops 369098752 | bytes 2621440 | tf_op jit(solution)/shard_map/attend/pallas_call | solution.py:230
  60.3 2.8 %collective-permute-start.8 = (f32[8,256]{1,0:T(8,128)S(1)}, f32[8,256]{1,0:T(8,128)S(1)}, u32[]{:S(2)}, u32[]{:S(2)}) collective-permute-start(f32[8,256]{1,0:T(8,128)S(1)} %get-tuple-element.27), channel_id=1, source_target_pairs={{0,48},{16,0},{32,16},{48,32},{64,112},{80,64},{96,80},{112,96},{1... | collective-permute-start | bytes 24584 | tf_op jit(solution)/shard_map/ppermute | solution.py:394
  63.1 0.9 collective-permute-start.7
  63.9 0.9 collective-permute-start.6
  64.8 1.8 %collective-permute-start.12 = (bf16[256,256]{1,0:T(8,128)(2,1)S(1)}, bf16[256,256]{1,0:T(8,128)(2,1)S(1)}, u32[]{:S(2)}, u32[]{:S(2)}) collective-permute-start(bf16[256,256]{1,0:T(8,128)(2,1)S(1)} %get-tuple-element.30.refs_0_.gq_ref), channel_id=1, source_target_pairs={{0,16},{16,32},{32,48},{48,0},{64,80},{80,96},{96,112},{112,64},{1... | collective-permute-start | bytes 393224 | tf_op jit(solution)/shard_map/ppermute | solution.py:394
  66.6 2.1 %collective-permute-start.13 = (bf16[256,256]{1,0:T(8,128)(2,1)S(1)}, bf16[256,256]{1,0:T(8,128)(2,1)S(1)}, u32[]{:S(2)}, u32[]{:S(2)}) collective-permute-start(bf16[256,256]{1,0:T(8,128)(2,1)S(1)} %get-tuple-element.30.refs_0_.gq_ref), channel_id=1, source_target_pairs={{0,32},{16,48},{32,0},{48,16},{64,96},{80,112},{96,64},{112,80},{1... | collective-permute-start | bytes 393224 | tf_op jit(solution)/shard_map/ppermute | solution.py:394
  68.6 0.6 collective-permute-start.14
  69.3 1.5 %collective-permute-start.9 = (f32[4,8,256]{2,1,0:T(8,128)S(1)}, f32[4,8,256]{2,1,0:T(8,128)S(1)}, u32[]{:S(2)}, u32[]{:S(2)}) collective-permute-start(f32[4,8,256]{2,1,0:T(8,128)S(1)} %pad_maximum_fusion.rest_0_), channel_id=1, source_target_pairs={{0,64},{16,80},{32,96},{48,112},{64,128},{80,144},{96,160},{112,17... | collective-permute-start | bytes 98312 | tf_op jit(solution)/shard_map/ppermute | solution.py:399
  71.4 2.0 %collective-permute-done.9.rest_1_ = f32[4,8,256]{2,1,0:T(8,128)S(1)} collective-permute-done((f32[4,8,256]{2,1,0:T(8,128)S(1)}, f32[4,8,256]{2,1,0:T(8,128)S(1)}, u32[]{:S(2)}, u32[]{:S(2)}) %collective-permute-start.9) | collective-permute-done | bytes 32800 | tf_op jit(solution)/shard_map/ppermute | solution.py:399
  73.9 1.7 %collective-permute-done.10.rest_2_ = f32[4,8,256]{2,1,0:T(8,128)S(1)} collective-permute-done((f32[4,8,256]{2,1,0:T(8,128)S(1)}, f32[4,8,256]{2,1,0:T(8,128)S(1)}, u32[]{:S(2)}, u32[]{:S(2)}) %collective-permute-start.10) | collective-permute-done | bytes 32800 | tf_op jit(solution)/shard_map/ppermute | solution.py:399
  75.6 1.7 %collective-permute-done.11.rest_3_ = f32[4,8,256]{2,1,0:T(8,128)S(1)} collective-permute-done((f32[4,8,256]{2,1,0:T(8,128)S(1)}, f32[4,8,256]{2,1,0:T(8,128)S(1)}, u32[]{:S(2)}, u32[]{:S(2)}) %collective-permute-start.11) | collective-permute-done | bytes 32800 | tf_op jit(solution)/shard_map/ppermute | solution.py:399
  77.3 1.6 %copy-done.1 = bf16[4096,256]{1,0:T(8,128)(2,1)S(1)} copy-done((bf16[4096,256]{1,0:T(8,128)(2,1)S(1)}, bf16[4096,256]{1,0:T(8,128)(2,1)}, u32[]{:S(2)}) %copy-start.1) | copy-done | bytes 2097176
  78.9 1.6 %copy-done.2 = bf16[4096,256]{1,0:T(8,128)(2,1)S(1)} copy-done((bf16[4096,256]{1,0:T(8,128)(2,1)S(1)}, bf16[4096,256]{1,0:T(8,128)(2,1)}, u32[]{:S(2)}) %copy-start.2) | copy-done | bytes 2097176
  80.5 3.2 %settle.1 = (bf16[256,256]{1,0:T(8,128)(2,1)}, bf16[256,256]{1,0:T(8,128)(2,1)}, bf16[256,512]{1,0:T(8,128)(2,1)S(1)}) custom-call(s32[16]{0:T(128)S(1)} %bitcast.25, s32[16]{0:T(128)S(1)} %bitcast.28, bf16[256,1024]{1,0:T(8,128)(2,1)} %get-tuple-element.22.qkv_ref, bf16[16,2,16,512]{3,2,1,0:T(8,128)(2,1)S(1)} %all-to-all-done.1.qdo_ref, ...), custom_call_target="tpu_custom_call" | custom-call | flops 402653184 | bytes 2097152 | tf_op jit(solution)/shard_map/settle/pallas_call | solution.py:291
  83.7 1.4 %collective-permute-start.15 = (bf16[256,512]{1,0:T(8,128)(2,1)S(1)}, bf16[256,512]{1,0:T(8,128)(2,1)S(1)}, u32[]{:S(2)}, u32[]{:S(2)}) collective-permute-start(bf16[256,512]{1,0:T(8,128)(2,1)S(1)} %get-tuple-element.31.refs_4_.gkv_ref), channel_id=1, source_target_pairs={{0,16},{16,32},{32,48},{48,0},{64,80},{80,96},{96,112},{112,64},{1... | collective-permute-start | bytes 786440 | tf_op jit(solution)/shard_map/ppermute | solution.py:394
  85.1 1.6 %collective-permute-start.16 = (bf16[256,512]{1,0:T(8,128)(2,1)S(1)}, bf16[256,512]{1,0:T(8,128)(2,1)S(1)}, u32[]{:S(2)}, u32[]{:S(2)}) collective-permute-start(bf16[256,512]{1,0:T(8,128)(2,1)S(1)} %get-tuple-element.31.refs_4_.gkv_ref), channel_id=1, source_target_pairs={{0,32},{16,48},{32,0},{48,16},{64,96},{80,112},{96,64},{112,80},{1... | collective-permute-start | bytes 786440 | tf_op jit(solution)/shard_map/ppermute | solution.py:394
  86.7 1.7 %collective-permute-start.17 = (bf16[256,512]{1,0:T(8,128)(2,1)S(1)}, bf16[256,512]{1,0:T(8,128)(2,1)}, u32[]{:S(2)}, u32[]{:S(2)}) collective-permute-start(bf16[256,512]{1,0:T(8,128)(2,1)S(1)} %get-tuple-element.31.refs_4_.gkv_ref), channel_id=1, source_target_pairs={{0,48},{16,0},{32,16},{48,32},{64,112},{80,64},{96,80},{112,96},{1... | collective-permute-start | bytes 786440 | tf_op jit(solution)/shard_map/ppermute | solution.py:394
  88.4 1.8 %xgrad.1 = bf16[4,2,512,256]{3,2,1,0:T(8,128)(2,1)S(1)} custom-call(bf16[4096,256]{1,0:T(8,128)(2,1)S(1)} %copy-done, bf16[4096,256]{1,0:T(8,128)(2,1)S(1)} %copy-done.1, bf16[4096,256]{1,0:T(8,128)(2,1)S(1)} %copy-done.2, bf16[256,256]{1,0:T(8,128)(2,1)S(1)} %get-tuple-element.30.refs_0_.gq_ref, bf16[256,512]{1,0:T(8,128)(2,1)S(1)} %get-tuple-element.31.refs_4_.gkv_ref, ...), custom_call_target="tpu_custom_call" | custom-call | flops 1610612736 | bytes 8912896 | tf_op jit(solution)/shard_map/xgrad/pallas_call | solution.py:381
  90.3 1.3 copy-done.3
  91.6 5.3 %all-to-all-start.3 = ((bf16[4,2,512,256]{3,2,1,0:T(8,128)(2,1)}), bf16[4,2,512,256]{3,2,1,0:T(8,128)(2,1)}, u32[]{:S(2)}, u32[]{:S(2)}) async-start(bf16[4,2,512,256]{3,2,1,0:T(8,128)(2,1)} %copy-done.3), calls=%async_computation.3 | async-start | bytes 4194304 | tf_op jit(solution)/shard_map/all_to_all | solution.py:451
  96.9 3.7 %wgrad.1 = (bf16[4,128,768]{2,1,0:T(8,128)(2,1)S(1)}, bf16[4,128,768]{2,1,0:T(8,128)(2,1)}) custom-call(bf16[4,256,1024]{2,1,0:T(8,128)(2,1)S(1)} %copy-done.5, bf16[256,256]{1,0:T(8,128)(2,1)S(1)} %get-tuple-element.30.refs_0_.gq_ref, bf16[256,256]{1,0:T(8,128)(2,1)S(1)} %collective-permute-done.12.refs_1_.rest_0_, ...), custom_call_target="tpu_custom_call" | custom-call | flops 1610612736 | bytes 5242880 | tf_op jit(solution)/shard_map/wgrad/pallas_call | solution.py:327
  100.7 0.9 copy-done.9
  101.5 2.5 %collective-permute-done.18.got_ref = bf16[4,128,768]{2,1,0:T(8,128)(2,1)S(1)} collective-permute-done((bf16[4,128,768]{2,1,0:T(8,128)(2,1)}, bf16[4,128,768]{2,1,0:T(8,128)(2,1)S(1)}, u32[]{:S(2)}, u32[]{:S(2)}) %collective-permute-start.18) | collective-permute-done | bytes 786464 | tf_op jit(solution)/shard_map/ppermute | solution.py:413
  104.0 1.1 copy-done.10
  105.6 5.0 %collective-permute-start.20 = (bf16[128,768]{1,0:T(8,128)(2,1)S(1)}, bf16[128,768]{1,0:T(8,128)(2,1)S(1)}, u32[]{:S(2)}, u32[]{:S(2)}) collective-permute-start(bf16[128,768]{1,0:T(8,128)(2,1)S(1)} %get-tuple-element.36), channel_id=1, source_target_pairs={{0,128},{16,144},{32,160},{48,176},{64,192},{80,208},{96,224},{112... | collective-permute-start | bytes 589832 | tf_op jit(solution)/shard_map/ppermute | solution.py:399
  110.5 5.7 %all-to-all-done.3 = bf16[4,2,512,256]{3,2,1,0:T(8,128)(2,1)} async-done(((bf16[4,2,512,256]{3,2,1,0:T(8,128)(2,1)}), bf16[4,2,512,256]{3,2,1,0:T(8,128)(2,1)}, u32[]{:S(2)}, u32[]{:S(2)}) %all-to-all-start.3) | async-done | bytes 2097184 | tf_op jit(solution)/shard_map/all_to_all | solution.py:451
  116.2 2.0 %convert_reduce_fusion = f32[2,512,256]{2,1,0:T(8,128)S(1)} fusion(bf16[4,2,512,256]{3,2,1,0:T(8,128)(2,1)} %all-to-all-done.3), kind=kLoop, calls=%fused_computation | loop fusion | flops 1835008 | bytes 3145728 | tf_op jit(solution)/shard_map/reduce_sum | solution.py:462
  118.2 5.4 %collective-permute-start.22 = (bf16[512,256]{1,0:T(8,128)(2,1)S(1)}, bf16[512,256]{1,0:T(8,128)(2,1)S(1)}, u32[]{:S(2)}, u32[]{:S(2)}) collective-permute-start(bf16[512,256]{1,0:T(8,128)(2,1)S(1)} %fusion.1), channel_id=1, source_target_pairs={{0,8},{2,10},{4,12},{6,14},{8,0},{10,2},{12,4},{14,6},{1,9},{3,11}... | collective-permute-start | bytes 786440 | tf_op jit(solution)/shard_map/ppermute | solution.py:409
  123.7 10.8 %collective-permute-done.20 = bf16[128,768]{1,0:T(8,128)(2,1)S(1)} collective-permute-done((bf16[128,768]{1,0:T(8,128)(2,1)S(1)}, bf16[128,768]{1,0:T(8,128)(2,1)S(1)}, u32[]{:S(2)}, u32[]{:S(2)}) %collective-permute-start.20) | collective-permute-done | bytes 196640 | tf_op jit(solution)/shard_map/ppermute | solution.py:399
  134.5 4.1 %collective-permute-done.19 = bf16[128,768]{1,0:T(8,128)(2,1)S(1)} collective-permute-done((bf16[128,768]{1,0:T(8,128)(2,1)S(1)}, bf16[128,768]{1,0:T(8,128)(2,1)S(1)}, u32[]{:S(2)}, u32[]{:S(2)}) %collective-permute-start.19) | collective-permute-done | bytes 196640 | tf_op jit(solution)/shard_map/ppermute | solution.py:399
  138.7 0.8 fusion.3
  139.4 0.8 fusion.2
  (44 shorter events, 1.9 us)
Async XLA Ops:
  0.6 0.9 copy-start.6
  7.0 11.4 %collective-permute-start = (bf16[64,1024]{1,0:T(8,128)(2,1)S(1)}, bf16[64,1024]{1,0:T(8,128)(2,1)S(1)}, u32[]{:S(2)}, u32[]{:S(2)}) collective-permute-start(bf16[64,1024]{1,0:T(8,128)(2,1)S(1)} %get-tuple-element.24), channel_id=1, source_target_pairs={{0,16},{16,32},{32,48},{48,0},{64,80},{80,96},{96,112},{112,64},{1... | collective-permute-start | bytes 393224 | tf_op jit(solution)/shard_map/ppermute | solution.py:394
  8.5 9.8 %collective-permute-start.1 = (bf16[64,1024]{1,0:T(8,128)(2,1)S(1)}, bf16[64,1024]{1,0:T(8,128)(2,1)S(1)}, u32[]{:S(2)}, u32[]{:S(2)}) collective-permute-start(bf16[64,1024]{1,0:T(8,128)(2,1)S(1)} %get-tuple-element.25), channel_id=1, source_target_pairs={{0,32},{16,48},{32,0},{48,16},{64,96},{80,112},{96,64},{112,80},{1... | collective-permute-start | bytes 393224 | tf_op jit(solution)/shard_map/ppermute | solution.py:394
  11.3 7.1 %collective-permute-start.2 = (bf16[64,1024]{1,0:T(8,128)(2,1)S(1)}, bf16[64,1024]{1,0:T(8,128)(2,1)S(1)}, u32[]{:S(2)}, u32[]{:S(2)}) collective-permute-start(bf16[64,1024]{1,0:T(8,128)(2,1)S(1)} %get-tuple-element.26), channel_id=1, source_target_pairs={{0,48},{16,0},{32,16},{48,32},{64,112},{80,64},{96,80},{112,96},{1... | collective-permute-start | bytes 393224 | tf_op jit(solution)/shard_map/ppermute | solution.py:394
  12.7 19.3 %all-to-all-start = ((bf16[16,16,1024]{2,1,0:T(8,128)(2,1)}), bf16[16,16,1024]{2,1,0:T(8,128)(2,1)S(1)}, u32[]{:S(2)}, u32[]{:S(2)}) async-start(bf16[16,16,1024]{2,1,0:T(8,128)(2,1)} %bitcast.4), calls=%async_computation | async-start | bytes 1048576 | tf_op jit(solution)/shard_map/all_to_all | solution.py:431
  18.3 13.7 %copy-start.7 = (s32[1,16]{1,0:T(1,128)S(1)}, s32[1,16]{1,0:T(1,128)}, u32[]{:S(2)}) copy-start(s32[1,16]{1,0:T(1,128)} %param.12) | copy-start | bytes 196
  18.3 13.7 %copy-start.8 = (s32[1,16]{1,0:T(1,128)S(1)}, s32[1,16]{1,0:T(1,128)}, u32[]{:S(2)}) copy-start(s32[1,16]{1,0:T(1,128)} %param.13) | copy-start | bytes 196
  18.4 20.5 %collective-permute-start.3 = (bf16[3,64,1024]{2,1,0:T(8,128)(2,1)S(1)}, bf16[3,64,1024]{2,1,0:T(8,128)(2,1)S(1)}, u32[]{:S(2)}, u32[]{:S(2)}) collective-permute-start(bf16[3,64,1024]{2,1,0:T(8,128)(2,1)S(1)} %stack.21.refs_0_.rest_0_), channel_id=1, source_target_pairs={{0,2},{2,4},{4,6},{6,0},{8,10},{10,12},{12,14},{14,8},{1,3},{3,5},... | collective-permute-start | bytes 1179656 | tf_op jit(solution)/shard_map/ppermute | solution.py:404
  20.0 18.8 %collective-permute-start.4 = (bf16[3,64,1024]{2,1,0:T(8,128)(2,1)S(1)}, bf16[3,64,1024]{2,1,0:T(8,128)(2,1)S(1)}, u32[]{:S(2)}, u32[]{:S(2)}) collective-permute-start(bf16[3,64,1024]{2,1,0:T(8,128)(2,1)S(1)} %stack.21.refs_0_.rest_0_), channel_id=1, source_target_pairs={{0,4},{2,6},{4,0},{6,2},{8,12},{10,14},{12,8},{14,10},{1,5},{3,7},... | collective-permute-start | bytes 1179656 | tf_op jit(solution)/shard_map/ppermute | solution.py:404
  21.0 17.9 %collective-permute-start.5 = (bf16[3,64,1024]{2,1,0:T(8,128)(2,1)S(1)}, bf16[3,64,1024]{2,1,0:T(8,128)(2,1)S(1)}, u32[]{:S(2)}, u32[]{:S(2)}) collective-permute-start(bf16[3,64,1024]{2,1,0:T(8,128)(2,1)S(1)} %stack.21.refs_0_.rest_0_), channel_id=1, source_target_pairs={{0,6},{2,0},{4,2},{6,4},{8,14},{10,8},{12,10},{14,12},{1,7},{3,1},... | collective-permute-start | bytes 1179656 | tf_op jit(solution)/shard_map/ppermute | solution.py:404
  33.5 18.7 %all-to-all-start.2 = ((bf16[16,2,16,512]{3,2,1,0:T(8,128)(2,1)}), bf16[16,2,16,512]{3,2,1,0:T(8,128)(2,1)S(1)}, u32[]{:S(2)}, u32[]{:S(2)}) async-start(bf16[16,2,16,512]{3,2,1,0:T(8,128)(2,1)} %pick.3), calls=%async_computation.2 | async-start | bytes 1048576 | tf_op jit(solution)/shard_map/all_to_all | solution.py:431
  39.1 38.3 %copy-start = (bf16[4096,256]{1,0:T(8,128)(2,1)S(1)}, bf16[4096,256]{1,0:T(8,128)(2,1)}, u32[]{:S(2)}) copy-start(bf16[4096,256]{1,0:T(8,128)(2,1)} %wq_ref.3) | copy-start | bytes 6291460
  40.5 1.4 copy-start.4
  52.2 21.7 %all-to-all-start.1 = ((bf16[16,2,16,512]{3,2,1,0:T(8,128)(2,1)}), bf16[16,2,16,512]{3,2,1,0:T(8,128)(2,1)S(1)}, u32[]{:S(2)}, u32[]{:S(2)}) async-start(bf16[16,2,16,512]{3,2,1,0:T(8,128)(2,1)} %pick.2), calls=%async_computation.1 | async-start | bytes 1048576 | tf_op jit(solution)/shard_map/all_to_all | solution.py:431
  60.3 8.3 %collective-permute-start.8 = (f32[8,256]{1,0:T(8,128)S(1)}, f32[8,256]{1,0:T(8,128)S(1)}, u32[]{:S(2)}, u32[]{:S(2)}) collective-permute-start(f32[8,256]{1,0:T(8,128)S(1)} %get-tuple-element.27), channel_id=1, source_target_pairs={{0,48},{16,0},{32,16},{48,32},{64,112},{80,64},{96,80},{112,96},{1... | collective-permute-start | bytes 24584 | tf_op jit(solution)/shard_map/ppermute | solution.py:394
  63.1 6.2 %collective-permute-start.7 = (f32[8,256]{1,0:T(8,128)S(1)}, f32[8,256]{1,0:T(8,128)S(1)}, u32[]{:S(2)}, u32[]{:S(2)}) collective-permute-start(f32[8,256]{1,0:T(8,128)S(1)} %get-tuple-element.27), channel_id=1, source_target_pairs={{0,32},{16,48},{32,0},{48,16},{64,96},{80,112},{96,64},{112,80},{1... | collective-permute-start | bytes 24584 | tf_op jit(solution)/shard_map/ppermute | solution.py:394
  63.9 5.4 %collective-permute-start.6 = (f32[8,256]{1,0:T(8,128)S(1)}, f32[8,256]{1,0:T(8,128)S(1)}, u32[]{:S(2)}, u32[]{:S(2)}) collective-permute-start(f32[8,256]{1,0:T(8,128)S(1)} %get-tuple-element.27), channel_id=1, source_target_pairs={{0,16},{16,32},{32,48},{48,0},{64,80},{80,96},{96,112},{112,64},{1... | collective-permute-start | bytes 24584 | tf_op jit(solution)/shard_map/ppermute | solution.py:394
  64.8 21.9 %collective-permute-start.12 = (bf16[256,256]{1,0:T(8,128)(2,1)S(1)}, bf16[256,256]{1,0:T(8,128)(2,1)S(1)}, u32[]{:S(2)}, u32[]{:S(2)}) collective-permute-start(bf16[256,256]{1,0:T(8,128)(2,1)S(1)} %get-tuple-element.30.refs_0_.gq_ref), channel_id=1, source_target_pairs={{0,16},{16,32},{32,48},{48,0},{64,80},{80,96},{96,112},{112,64},{1... | collective-permute-start | bytes 393224 | tf_op jit(solution)/shard_map/ppermute | solution.py:394
  66.6 21.9 %collective-permute-start.13 = (bf16[256,256]{1,0:T(8,128)(2,1)S(1)}, bf16[256,256]{1,0:T(8,128)(2,1)S(1)}, u32[]{:S(2)}, u32[]{:S(2)}) collective-permute-start(bf16[256,256]{1,0:T(8,128)(2,1)S(1)} %get-tuple-element.30.refs_0_.gq_ref), channel_id=1, source_target_pairs={{0,32},{16,48},{32,0},{48,16},{64,96},{80,112},{96,64},{112,80},{1... | collective-permute-start | bytes 393224 | tf_op jit(solution)/shard_map/ppermute | solution.py:394
  68.6 19.8 %collective-permute-start.14 = (bf16[256,256]{1,0:T(8,128)(2,1)S(1)}, bf16[256,256]{1,0:T(8,128)(2,1)S(1)}, u32[]{:S(2)}, u32[]{:S(2)}) collective-permute-start(bf16[256,256]{1,0:T(8,128)(2,1)S(1)} %get-tuple-element.30.refs_0_.gq_ref), channel_id=1, source_target_pairs={{0,48},{16,0},{32,16},{48,32},{64,112},{80,64},{96,80},{112,96},{1... | collective-permute-start | bytes 393224 | tf_op jit(solution)/shard_map/ppermute | solution.py:394
  69.3 4.1 %collective-permute-start.9 = (f32[4,8,256]{2,1,0:T(8,128)S(1)}, f32[4,8,256]{2,1,0:T(8,128)S(1)}, u32[]{:S(2)}, u32[]{:S(2)}) collective-permute-start(f32[4,8,256]{2,1,0:T(8,128)S(1)} %pad_maximum_fusion.rest_0_), channel_id=1, source_target_pairs={{0,64},{16,80},{32,96},{48,112},{64,128},{80,144},{96,160},{112,17... | collective-permute-start | bytes 98312 | tf_op jit(solution)/shard_map/ppermute | solution.py:399
  70.8 4.8 %collective-permute-start.10 = (f32[4,8,256]{2,1,0:T(8,128)S(1)}, f32[4,8,256]{2,1,0:T(8,128)S(1)}, u32[]{:S(2)}, u32[]{:S(2)}) collective-permute-start(f32[4,8,256]{2,1,0:T(8,128)S(1)} %pad_maximum_fusion.rest_0_), channel_id=1, source_target_pairs={{0,128},{16,144},{32,160},{48,176},{64,192},{80,208},{96,224},{112... | collective-permute-start | bytes 98312 | tf_op jit(solution)/shard_map/ppermute | solution.py:399
  73.4 3.9 %collective-permute-start.11 = (f32[4,8,256]{2,1,0:T(8,128)S(1)}, f32[4,8,256]{2,1,0:T(8,128)S(1)}, u32[]{:S(2)}, u32[]{:S(2)}) collective-permute-start(f32[4,8,256]{2,1,0:T(8,128)S(1)} %pad_maximum_fusion.rest_0_), channel_id=1, source_target_pairs={{0,192},{16,208},{32,224},{48,240},{64,0},{80,16},{96,32},{112,48}... | collective-permute-start | bytes 98312 | tf_op jit(solution)/shard_map/ppermute | solution.py:399
  77.3 1.6 %copy-start.1 = (bf16[4096,256]{1,0:T(8,128)(2,1)S(1)}, bf16[4096,256]{1,0:T(8,128)(2,1)}, u32[]{:S(2)}) copy-start(bf16[4096,256]{1,0:T(8,128)(2,1)} %wk_ref.3) | copy-start | bytes 6291460
  78.9 1.6 %copy-start.2 = (bf16[4096,256]{1,0:T(8,128)(2,1)S(1)}, bf16[4096,256]{1,0:T(8,128)(2,1)}, u32[]{:S(2)}) copy-start(bf16[4096,256]{1,0:T(8,128)(2,1)} %wv_ref.3) | copy-start | bytes 6291460
  83.7 13.2 %collective-permute-start.15 = (bf16[256,512]{1,0:T(8,128)(2,1)S(1)}, bf16[256,512]{1,0:T(8,128)(2,1)S(1)}, u32[]{:S(2)}, u32[]{:S(2)}) collective-permute-start(bf16[256,512]{1,0:T(8,128)(2,1)S(1)} %get-tuple-element.31.refs_4_.gkv_ref), channel_id=1, source_target_pairs={{0,16},{16,32},{32,48},{48,0},{64,80},{80,96},{96,112},{112,64},{1... | collective-permute-start | bytes 786440 | tf_op jit(solution)/shard_map/ppermute | solution.py:394
  85.1 11.8 %collective-permute-start.16 = (bf16[256,512]{1,0:T(8,128)(2,1)S(1)}, bf16[256,512]{1,0:T(8,128)(2,1)S(1)}, u32[]{:S(2)}, u32[]{:S(2)}) collective-permute-start(bf16[256,512]{1,0:T(8,128)(2,1)S(1)} %get-tuple-element.31.refs_4_.gkv_ref), channel_id=1, source_target_pairs={{0,32},{16,48},{32,0},{48,16},{64,96},{80,112},{96,64},{112,80},{1... | collective-permute-start | bytes 786440 | tf_op jit(solution)/shard_map/ppermute | solution.py:394
  86.7 10.2 %collective-permute-start.17 = (bf16[256,512]{1,0:T(8,128)(2,1)S(1)}, bf16[256,512]{1,0:T(8,128)(2,1)}, u32[]{:S(2)}, u32[]{:S(2)}) collective-permute-start(bf16[256,512]{1,0:T(8,128)(2,1)S(1)} %get-tuple-element.31.refs_4_.gkv_ref), channel_id=1, source_target_pairs={{0,48},{16,0},{32,16},{48,32},{64,112},{80,64},{96,80},{112,96},{1... | collective-permute-start | bytes 786440 | tf_op jit(solution)/shard_map/ppermute | solution.py:394
  90.3 1.3 copy-start.3
  91.6 5.3 %copy-start.5 = (bf16[4,256,1024]{2,1,0:T(8,128)(2,1)S(1)}, bf16[4,256,1024]{2,1,0:T(8,128)(2,1)}, u32[]{:S(2)}) copy-start(bf16[4,256,1024]{2,1,0:T(8,128)(2,1)} %copy-done.4) | copy-start | bytes 6291460
  91.6 24.6 %all-to-all-start.3 = ((bf16[4,2,512,256]{3,2,1,0:T(8,128)(2,1)}), bf16[4,2,512,256]{3,2,1,0:T(8,128)(2,1)}, u32[]{:S(2)}, u32[]{:S(2)}) async-start(bf16[4,2,512,256]{3,2,1,0:T(8,128)(2,1)} %copy-done.3), calls=%async_computation.3 | async-start | bytes 4194304 | tf_op jit(solution)/shard_map/all_to_all | solution.py:451
  100.7 0.9 copy-start.9
  101.5 2.5 %collective-permute-start.18 = (bf16[4,128,768]{2,1,0:T(8,128)(2,1)}, bf16[4,128,768]{2,1,0:T(8,128)(2,1)S(1)}, u32[]{:S(2)}, u32[]{:S(2)}) collective-permute-start(bf16[4,128,768]{2,1,0:T(8,128)(2,1)} %get-tuple-element.33), channel_id=1, source_target_pairs={{0,1},{1,0},{2,3},{3,2},{4,5},{5,4},{6,7},{7,6},{8,9},{9,8},{10,11... | collective-permute-start | bytes 2359304 | tf_op jit(solution)/shard_map/ppermute | solution.py:413
  104.0 1.1 copy-start.10
  105.3 18.4 %collective-permute-start.21 = (bf16[128,768]{1,0:T(8,128)(2,1)S(1)}, bf16[128,768]{1,0:T(8,128)(2,1)S(1)}, u32[]{:S(2)}, u32[]{:S(2)}) collective-permute-start(bf16[128,768]{1,0:T(8,128)(2,1)S(1)} %get-tuple-element.37), channel_id=1, source_target_pairs={{0,192},{16,208},{32,224},{48,240},{64,0},{80,16},{96,32},{112,48}... | collective-permute-start | bytes 589832 | tf_op jit(solution)/shard_map/ppermute | solution.py:399
  105.6 28.9 %collective-permute-start.20 = (bf16[128,768]{1,0:T(8,128)(2,1)S(1)}, bf16[128,768]{1,0:T(8,128)(2,1)S(1)}, u32[]{:S(2)}, u32[]{:S(2)}) collective-permute-start(bf16[128,768]{1,0:T(8,128)(2,1)S(1)} %get-tuple-element.36), channel_id=1, source_target_pairs={{0,128},{16,144},{32,160},{48,176},{64,192},{80,208},{96,224},{112... | collective-permute-start | bytes 589832 | tf_op jit(solution)/shard_map/ppermute | solution.py:399
  110.5 28.1 %collective-permute-start.19 = (bf16[128,768]{1,0:T(8,128)(2,1)S(1)}, bf16[128,768]{1,0:T(8,128)(2,1)S(1)}, u32[]{:S(2)}, u32[]{:S(2)}) collective-permute-start(bf16[128,768]{1,0:T(8,128)(2,1)S(1)} %get-tuple-element.35), channel_id=1, source_target_pairs={{0,64},{16,80},{32,96},{48,112},{64,128},{80,144},{96,160},{112,17... | collective-permute-start | bytes 589832 | tf_op jit(solution)/shard_map/ppermute | solution.py:399
  118.2 21.2 %collective-permute-start.22 = (bf16[512,256]{1,0:T(8,128)(2,1)S(1)}, bf16[512,256]{1,0:T(8,128)(2,1)S(1)}, u32[]{:S(2)}, u32[]{:S(2)}) collective-permute-start(bf16[512,256]{1,0:T(8,128)(2,1)S(1)} %fusion.1), channel_id=1, source_target_pairs={{0,8},{2,10},{4,12},{6,14},{8,0},{10,2},{12,4},{14,6},{1,9},{3,11}... | collective-permute-start | bytes 786440 | tf_op jit(solution)/shard_map/ppermute | solution.py:409

commit v3 on v2

--- a/solution.py
+++ b/solution.py
@@ -303,34 +303,37 @@
     )(p1, p2, qkv, qdo, *stats, *after)
 
 
-def _wgrad_body(x_ref, *refs):
-    gq, gkv = refs[0:XS], refs[XS : 2 * XS]
-    xs = [x_ref.at[k] for k in range(XS)]
-    keep_ref, send_ref = refs[-2:]
-    first = lax.axis_index("cuts") == 0
-    half, n = keep_ref.shape[1], gq[0].shape[1]
-    for z in range(ZS):
-        for cols, gs in ((slice(0, n), gq), (slice(n, 3 * n), gkv)):
-            acc = None
-            for x, g in zip(xs, gs):
-                part = _tn(x[:, z * 2 * half : (z + 1) * 2 * half], g[...])
-                acc = part if acc is None else acc + part
-            top, low = acc[:half], acc[half:]
-            keep_ref[z, :, cols] = jnp.where(first, top, low).astype(BF)
-            send_ref[z, :, cols] = jnp.where(first, low, top).astype(BF)
-
-
-def wgrad(xs, gq, gkv):
+def _wgrad_body(flip, x_ref, *refs):
+    gq, gkv, o_ref = refs[0:XS], refs[XS : 2 * XS], refs[2 * XS]
+    half, n = o_ref.shape[1], gq[0].shape[1]
+    core = lax.axis_index("cuts")
+    if flip:
+        core = 1 - core
+    at = pl.multiple_of(core * half, half)
+    xs = [
+        jnp.concatenate([x_ref[k, :, pl.ds(z * 2 * half + at, half)] for z in range(ZS)], axis=1)
+        for k in range(XS)
+    ]
+    for cols, gs in ((slice(0, n), gq), (slice(n, 2 * n), gkv), (slice(2 * n, 3 * n), gkv)):
+        acc = None
+        for x, g in zip(xs, gs):
+            right = g[...] if gs is gq else g[:, cols.start - n : cols.stop - n]
+            part = _tn(x, right)
+            acc = part if acc is None else acc + part
+        for z in range(ZS):
+            o_ref[z, :, cols] = acc[z * half : (z + 1) * half].astype(BF)
+
+
+def wgrad(flip, xs, gq, gkv):
     _, t, rows = xs.shape
     n = gq[0].shape[1]
-    shape = (ZS, rows // (2 * ZS), 3 * n)
-    return pl.pallas_call(
-        _wgrad_body,
+    return pl.pallas_call(
+        functools.partial(_wgrad_body, flip),
         in_specs=[VMEM] * (1 + 2 * XS),
-        out_specs=[VMEM, VMEM],
-        out_shape=[jax.ShapeDtypeStruct(shape, BF), jax.ShapeDtypeStruct(shape, BF)],
-        compiler_params=_params(SMALL),
-        cost_estimate=_cost(2 * XS * t * rows * 3 * n, 2 * XS * t * (rows + 3 * n) + 6 * rows * n),
+        out_specs=VMEM,
+        out_shape=jax.ShapeDtypeStruct((ZS, rows // (2 * ZS), 3 * n), BF),
+        compiler_params=_params(SMALL),
+        cost_estimate=_cost(3 * XS * t * rows * 3 * n, 2 * XS * t * (rows + 3 * n) + 3 * rows * n),
         name="wgrad",
     )(xs, *gq, *gkv)
 
@@ -352,7 +355,7 @@
         out_shape=[jax.ShapeDtypeStruct(piece, F32)]
         + [jax.ShapeDtypeStruct(piece, BF)] * (ZS - 1),
         compiler_params=_params(SMALL),
-        cost_estimate=_cost(4 * HINT // 30, 6 * keep.size),
+        cost_estimate=_cost(8 * HINT // 30, 6 * keep.size),
         name="pair",
     )(keep, got)
 
@@ -451,11 +454,9 @@
     terms = lax.all_to_all(
         terms, "head", split_axis=0, concat_axis=0, tiled=True, axis_index_groups=groups
     )
-    mine, theirs = wgrad(
-        columns,
-        [gq_x[k] for k in range(XS)],
-        [gkv_x[k] for k in range(XS)],
-    )
+    operands = (columns, [gq_x[k] for k in range(XS)], [gkv_x[k] for k in range(XS)])
+    theirs = wgrad(True, *operands)
+    mine = wgrad(False, *operands)
     total, *pieces = pair(mine, swap_cores(theirs))
     for k in range(1, ZS):
         total = total + shift_z(pieces[k - 1], k).astype(F32)

time: 142 us -> 138 us (0.972)
  waiting for transfers between devices: 47.4 us -> 43.1 us
  Pallas kernels: 20.2 us -> 22.5 us
  local copies, waits for them, and re-layouts: 9.6 us -> 7.58 us
    ppermute x6, waiting for transfers between devices: 20.3 us -> 13.1 us  [shift_z(): return lax.ppermute(v, 'doc', pairs)]
    all_to_all x1, waiting for transfers between devices: 5.66 us -> 8.12 us  [per_device(): lax.all_to_all(terms, 'head', split_axis=0, concat_axis=0, tiled=True, ax...]
    ppermute x12, waiting for transfers between devices: 0.03 us -> 2.36 us  [shift_x(): return lax.ppermute(v, 'doc', pairs)]
    unnamed x22 -> x18, local copies, waits for them, and re-layouts: 8.81 us -> 6.79 us
    ppermute x1, waiting for transfers between devices: 2.49 us -> 0.61 us  [swap_cores(): return lax.ppermute(v, 'cuts', [(0, 1), (1, 0)])]
    pallas_call x1 -> x2, Pallas kernels: 3.71 us -> 4.95 us  [wgrad(): pl.pallas_call(functools.partial(_wgrad_body, flip), in_specs=[VMEM] * (1...]
  transfers between devices with their start and end apart: 27 -> 27, of which waited for: 9 -> 9; matrix products, arithmetic and copies ran while one was open for 2% -> 2% of each run, Pallas kernels for 11% -> 13%
where the time goes in v3:
time: 138 us; the launch traced here: 136 us
  starting transfers between devices  58.8 us (43%)
  waiting for transfers between devices  43.1 us (31%)
  Pallas kernels  22.5 us (16%)
  local copies, waits for them, and re-layouts  7.58 us (5%)
  other arithmetic  2.88 us (2%)
    all_to_all x3, waiting for transfers between devices, spread(): return lax.all_to_all(v, 'doc', split_axis=0, concat_axis=0, tiled=True)  18.9 us
    ppermute x12, starting transfers between devices, shift_x(): return lax.ppermute(v, 'doc', pairs)  18.4 us
    all_to_all x3, starting transfers between devices, spread(): return lax.all_to_all(v, 'doc', split_axis=0, concat_axis=0, tiled=True)  16.3 us
    ppermute x6, waiting for transfers between devices, shift_z(): return lax.ppermute(v, 'doc', pairs)  13.1 us
    ppermute x6, starting transfers between devices, shift_z(): return lax.ppermute(v, 'doc', pairs)  8.73 us
    all_to_all x1, waiting for transfers between devices, per_device(): lax.all_to_all(terms, 'head', split_axis=0, concat_axis=0, tiled=True, ax...  8.12 us
    unnamed x18, local copies, waits for them, and re-layouts  6.79 us
    pallas_call x1, Pallas kernels, project(): pl.pallas_call(_project_body, in_specs=[ANY] * 5, out_specs=[VMEM] * (1 +...  5.42 us
  transfers between devices with their start and end apart: 27, of which 9 were waited for; matrix products, arithmetic and copies ran while one was open for 2% of the time, Pallas kernels for 13%

profile of v3, /device:TPU:72, one launch (start us, length us, event | category | flops | bytes accessed | tf_op | source)
XLA Modules:
  0.0 135.8 jit_solution(8395345126304936425)
XLA Ops:
  0.6 0.9 copy-done.6
  1.5 5.4 %project.1 = (bf16[256,1024]{1,0:T(8,128)(2,1)}, bf16[256,1024]{1,0:T(8,128)(2,1)S(1)}, bf16[64,1024]{1,0:T(8,128)(2,1)S(1)}, bf16[64,1024]{1,0:T(8,128)(2,1)S(1)}, bf16[64,1024]{1,0:T(8,128)(2,1)S(1)}) custom-call(bf16[256,4096]{1,0:T(8,128)(2,1)} %bitcast.29, bf16[4096,256]{1,0:T(8,128)(2,1)} %wq_ref.3, bf16[4096,256]{1,0:T(8,128)(2,1)} %wk_ref.3, ...), custom_call_target="tpu_custom_call" | custom-call | flops 1610612736 | bytes 8388608 | tf_op jit(solution)/shard_map/project/pallas_call | solution.py:92
  7.0 1.6 %collective-permute-start = (bf16[64,1024]{1,0:T(8,128)(2,1)S(1)}, bf16[64,1024]{1,0:T(8,128)(2,1)S(1)}, u32[]{:S(2)}, u32[]{:S(2)}) collective-permute-start(bf16[64,1024]{1,0:T(8,128)(2,1)S(1)} %get-tuple-element.22), channel_id=1, source_target_pairs={{0,16},{16,32},{32,48},{48,0},{64,80},{80,96},{96,112},{112,64},{1... | collective-permute-start | bytes 393224 | tf_op jit(solution)/shard_map/ppermute | solution.py:397
  8.5 2.7 %collective-permute-start.1 = (bf16[64,1024]{1,0:T(8,128)(2,1)S(1)}, bf16[64,1024]{1,0:T(8,128)(2,1)S(1)}, u32[]{:S(2)}, u32[]{:S(2)}) collective-permute-start(bf16[64,1024]{1,0:T(8,128)(2,1)S(1)} %get-tuple-element.23), channel_id=1, source_target_pairs={{0,32},{16,48},{32,0},{48,16},{64,96},{80,112},{96,64},{112,80},{1... | collective-permute-start | bytes 393224 | tf_op jit(solution)/shard_map/ppermute | solution.py:397
  11.3 1.4 %collective-permute-start.2 = (bf16[64,1024]{1,0:T(8,128)(2,1)S(1)}, bf16[64,1024]{1,0:T(8,128)(2,1)S(1)}, u32[]{:S(2)}, u32[]{:S(2)}) collective-permute-start(bf16[64,1024]{1,0:T(8,128)(2,1)S(1)} %get-tuple-element.24), channel_id=1, source_target_pairs={{0,48},{16,0},{32,16},{48,32},{64,112},{80,64},{96,80},{112,96},{1... | collective-permute-start | bytes 393224 | tf_op jit(solution)/shard_map/ppermute | solution.py:397
  12.7 5.6 %all-to-all-start = ((bf16[16,16,1024]{2,1,0:T(8,128)(2,1)}), bf16[16,16,1024]{2,1,0:T(8,128)(2,1)S(1)}, u32[]{:S(2)}, u32[]{:S(2)}) async-start(bf16[16,16,1024]{2,1,0:T(8,128)(2,1)} %bitcast.4), calls=%async_computation | async-start | bytes 1048576 | tf_op jit(solution)/shard_map/all_to_all | solution.py:434
  18.4 1.7 %collective-permute-start.3 = (bf16[3,64,1024]{2,1,0:T(8,128)(2,1)S(1)}, bf16[3,64,1024]{2,1,0:T(8,128)(2,1)S(1)}, u32[]{:S(2)}, u32[]{:S(2)}) collective-permute-start(bf16[3,64,1024]{2,1,0:T(8,128)(2,1)S(1)} %stack.21.refs_0_.rest_0_), channel_id=1, source_target_pairs={{0,2},{2,4},{4,6},{6,0},{8,10},{10,12},{12,14},{14,8},{1,3},{3,5},... | collective-permute-start | bytes 1179656 | tf_op jit(solution)/shard_map/ppermute | solution.py:407
  20.0 0.9 collective-permute-start.4
  21.0 2.4 %collective-permute-start.5 = (bf16[3,64,1024]{2,1,0:T(8,128)(2,1)S(1)}, bf16[3,64,1024]{2,1,0:T(8,128)(2,1)S(1)}, u32[]{:S(2)}, u32[]{:S(2)}) collective-permute-start(bf16[3,64,1024]{2,1,0:T(8,128)(2,1)S(1)} %stack.21.refs_0_.rest_0_), channel_id=1, source_target_pairs={{0,6},{2,0},{4,2},{6,4},{8,14},{10,8},{12,10},{14,12},{1,7},{3,1},... | collective-permute-start | bytes 1179656 | tf_op jit(solution)/shard_map/ppermute | solution.py:407
  23.4 8.6 %all-to-all-done.all_ref = bf16[16,16,1024]{2,1,0:T(8,128)(2,1)S(1)} async-done(((bf16[16,16,1024]{2,1,0:T(8,128)(2,1)}), bf16[16,16,1024]{2,1,0:T(8,128)(2,1)S(1)}, u32[]{:S(2)}, u32[]{:S(2)}) %all-to-all-start) | async-done | bytes 524320 | tf_op jit(solution)/shard_map/all_to_all | solution.py:434
  32.0 1.5 %pick.3 = bf16[16,2,16,512]{3,2,1,0:T(8,128)(2,1)} custom-call(s32[16]{0:T(128)S(1)} %bitcast.23, s32[16]{0:T(128)S(1)} %bitcast.26, bf16[16,16,1024]{2,1,0:T(8,128)(2,1)S(1)} %all-to-all-done.all_ref, bf16[3,64,1024]{2,1,0:T(8,128)(2,1)S(1)} %stack.21.refs_0_.rest_0_), custom_call_target="tpu_custom_call" | custom-call | bytes 1048576 | tf_op jit(solution)/shard_map/pick/pallas_call | solution.py:181
  33.5 5.4 %all-to-all-start.2 = ((bf16[16,2,16,512]{3,2,1,0:T(8,128)(2,1)}), bf16[16,2,16,512]{3,2,1,0:T(8,128)(2,1)S(1)}, u32[]{:S(2)}, u32[]{:S(2)}) async-start(bf16[16,2,16,512]{3,2,1,0:T(8,128)(2,1)} %pick.3), calls=%async_computation.2 | async-start | bytes 1048576 | tf_op jit(solution)/shard_map/all_to_all | solution.py:434
  39.0 1.5 %pick.2 = bf16[16,2,16,512]{3,2,1,0:T(8,128)(2,1)} custom-call(s32[16]{0:T(128)S(1)} %bitcast.24, s32[16]{0:T(128)S(1)} %bitcast.27, bf16[16,16,1024]{2,1,0:T(8,128)(2,1)S(1)} %all-to-all-done.all_ref, bf16[4,256,1024]{2,1,0:T(8,128)(2,1)S(1)} %merge.1.rest_0_.x_ref), custom_call_target="tpu_custom_call" | custom-call | bytes 1048576 | tf_op jit(solution)/shard_map/pick/pallas_call | solution.py:181
  40.5 1.4 %copy-done.4 = bf16[4,256,1024]{2,1,0:T(8,128)(2,1)} copy-done((bf16[4,256,1024]{2,1,0:T(8,128)(2,1)}, bf16[4,256,1024]{2,1,0:T(8,128)(2,1)S(1)}, u32[]{:S(2)}) %copy-start.4) | copy-done | bytes 2097176
  41.9 10.3 %all-to-all-done.2.kv_ref = bf16[16,2,16,512]{3,2,1,0:T(8,128)(2,1)S(1)} async-done(((bf16[16,2,16,512]{3,2,1,0:T(8,128)(2,1)}), bf16[16,2,16,512]{3,2,1,0:T(8,128)(2,1)S(1)}, u32[]{:S(2)}, u32[]{:S(2)}) %all-to-all-start.2) | async-done | bytes 524320 | tf_op jit(solution)/shard_map/all_to_all | solution.py:434
  52.2 5.4 %all-to-all-start.1 = ((bf16[16,2,16,512]{3,2,1,0:T(8,128)(2,1)}), bf16[16,2,16,512]{3,2,1,0:T(8,128)(2,1)S(1)}, u32[]{:S(2)}, u32[]{:S(2)}) async-start(bf16[16,2,16,512]{3,2,1,0:T(8,128)(2,1)} %pick.2), calls=%async_computation.1 | async-start | bytes 1048576 | tf_op jit(solution)/shard_map/all_to_all | solution.py:434
  57.6 2.7 %attend.1 = (bf16[256,256]{1,0:T(8,128)(2,1)S(1)}, f32[8,256]{1,0:T(8,128)S(1)}) custom-call(bf16[256,1024]{1,0:T(8,128)(2,1)} %get-tuple-element.20.qkv_ref, bf16[16,2,16,512]{3,2,1,0:T(8,128)(2,1)S(1)} %all-to-all-done.2.kv_ref), custom_call_target="tpu_custom_call" | custom-call | flops 369098752 | bytes 2621440 | tf_op jit(solution)/shard_map/attend/pallas_call | solution.py:230
  60.3 2.7 %collective-permute-start.8 = (f32[8,256]{1,0:T(8,128)S(1)}, f32[8,256]{1,0:T(8,128)S(1)}, u32[]{:S(2)}, u32[]{:S(2)}) collective-permute-start(f32[8,256]{1,0:T(8,128)S(1)} %get-tuple-element.25), channel_id=1, source_target_pairs={{0,48},{16,0},{32,16},{48,32},{64,112},{80,64},{96,80},{112,96},{1... | collective-permute-start | bytes 24584 | tf_op jit(solution)/shard_map/ppermute | solution.py:397
  63.0 0.9 collective-permute-start.7
  63.9 0.9 collective-permute-start.6
  64.8 1.8 %collective-permute-start.12 = (bf16[256,256]{1,0:T(8,128)(2,1)S(1)}, bf16[256,256]{1,0:T(8,128)(2,1)S(1)}, u32[]{:S(2)}, u32[]{:S(2)}) collective-permute-start(bf16[256,256]{1,0:T(8,128)(2,1)S(1)} %get-tuple-element.28.refs_0_.gq_ref), channel_id=1, source_target_pairs={{0,16},{16,32},{32,48},{48,0},{64,80},{80,96},{96,112},{112,64},{1... | collective-permute-start | bytes 393224 | tf_op jit(solution)/shard_map/ppermute | solution.py:397
  66.5 1.7 %collective-permute-done.7 = f32[8,256]{1,0:T(8,128)S(1)} collective-permute-done((f32[8,256]{1,0:T(8,128)S(1)}, f32[8,256]{1,0:T(8,128)S(1)}, u32[]{:S(2)}, u32[]{:S(2)}) %collective-permute-start.7) | collective-permute-done | bytes 8224 | tf_op jit(solution)/shard_map/ppermute | solution.py:397
  68.3 0.6 collective-permute-done.6
  68.9 1.4 collective-permute-start.9
  70.8 1.5 %collective-permute-start.11 = (f32[4,8,256]{2,1,0:T(8,128)S(1)}, f32[4,8,256]{2,1,0:T(8,128)S(1)}, u32[]{:S(2)}, u32[]{:S(2)}) collective-permute-start(f32[4,8,256]{2,1,0:T(8,128)S(1)} %pad_maximum_fusion.rest_0_), channel_id=1, source_target_pairs={{0,192},{16,208},{32,224},{48,240},{64,0},{80,16},{96,32},{112,48}... | collective-permute-start | bytes 98312 | tf_op jit(solution)/shard_map/ppermute | solution.py:402
  72.3 1.5 %collective-permute-start.13 = (bf16[256,256]{1,0:T(8,128)(2,1)S(1)}, bf16[256,256]{1,0:T(8,128)(2,1)S(1)}, u32[]{:S(2)}, u32[]{:S(2)}) collective-permute-start(bf16[256,256]{1,0:T(8,128)(2,1)S(1)} %get-tuple-element.28.refs_0_.gq_ref), channel_id=1, source_target_pairs={{0,32},{16,48},{32,0},{48,16},{64,96},{80,112},{96,64},{112,80},{1... | collective-permute-start | bytes 393224 | tf_op jit(solution)/shard_map/ppermute | solution.py:397
  73.7 0.9 collective-permute-start.14
  75.1 1.6 %copy-done.1 = bf16[4096,256]{1,0:T(8,128)(2,1)S(1)} copy-done((bf16[4096,256]{1,0:T(8,128)(2,1)S(1)}, bf16[4096,256]{1,0:T(8,128)(2,1)}, u32[]{:S(2)}) %copy-start.1) | copy-done | bytes 2097176
  76.7 1.6 %copy-done.2 = bf16[4096,256]{1,0:T(8,128)(2,1)S(1)} copy-done((bf16[4096,256]{1,0:T(8,128)(2,1)S(1)}, bf16[4096,256]{1,0:T(8,128)(2,1)}, u32[]{:S(2)}) %copy-start.2) | copy-done | bytes 2097176
  78.2 3.2 %settle.1 = (bf16[256,256]{1,0:T(8,128)(2,1)}, bf16[256,256]{1,0:T(8,128)(2,1)}, bf16[256,512]{1,0:T(8,128)(2,1)S(1)}) custom-call(s32[16]{0:T(128)S(1)} %bitcast.25, s32[16]{0:T(128)S(1)} %bitcast.28, bf16[256,1024]{1,0:T(8,128)(2,1)} %get-tuple-element.20.qkv_ref, bf16[16,2,16,512]{3,2,1,0:T(8,128)(2,1)S(1)} %all-to-all-done.1.qdo_ref, ...), custom_call_target="tpu_custom_call" | custom-call | flops 402653184 | bytes 2097152 | tf_op jit(solution)/shard_map/settle/pallas_call | solution.py:291
  81.4 0.7 collective-permute-start.15
  82.2 2.1 %collective-permute-start.16 = (bf16[256,512]{1,0:T(8,128)(2,1)S(1)}, bf16[256,512]{1,0:T(8,128)(2,1)S(1)}, u32[]{:S(2)}, u32[]{:S(2)}) collective-permute-start(bf16[256,512]{1,0:T(8,128)(2,1)S(1)} %get-tuple-element.29.refs_4_.gkv_ref), channel_id=1, source_target_pairs={{0,32},{16,48},{32,0},{48,16},{64,96},{80,112},{96,64},{112,80},{1... | collective-permute-start | bytes 786440 | tf_op jit(solution)/shard_map/ppermute | solution.py:397
  84.2 1.3 collective-permute-start.17
  85.5 1.8 %xgrad.1 = bf16[4,2,512,256]{3,2,1,0:T(8,128)(2,1)S(1)} custom-call(bf16[4096,256]{1,0:T(8,128)(2,1)S(1)} %copy-done, bf16[4096,256]{1,0:T(8,128)(2,1)S(1)} %copy-done.1, bf16[4096,256]{1,0:T(8,128)(2,1)S(1)} %copy-done.2, bf16[256,256]{1,0:T(8,128)(2,1)S(1)} %get-tuple-element.28.refs_0_.gq_ref, bf16[256,512]{1,0:T(8,128)(2,1)S(1)} %get-tuple-element.29.refs_4_.gkv_ref, ...), custom_call_target="tpu_custom_call" | custom-call | flops 1610612736 | bytes 8912896 | tf_op jit(solution)/shard_map/xgrad/pallas_call | solution.py:384
  87.4 1.3 copy-done.3
  88.7 5.2 %all-to-all-start.3 = ((bf16[4,2,512,256]{3,2,1,0:T(8,128)(2,1)}), bf16[4,2,512,256]{3,2,1,0:T(8,128)(2,1)}, u32[]{:S(2)}, u32[]{:S(2)}) async-start(bf16[4,2,512,256]{3,2,1,0:T(8,128)(2,1)} %copy-done.3), calls=%async_computation.3 | async-start | bytes 4194304 | tf_op jit(solution)/shard_map/all_to_all | solution.py:454
  93.9 2.9 %wgrad.3 = bf16[4,128,768]{2,1,0:T(8,128)(2,1)} custom-call(bf16[4,256,1024]{2,1,0:T(8,128)(2,1)S(1)} %copy-done.5, bf16[256,256]{1,0:T(8,128)(2,1)S(1)} %get-tuple-element.28.refs_0_.gq_ref, bf16[256,256]{1,0:T(8,128)(2,1)S(1)} %collective-permute-done.12.refs_1_.rest_0_, bf16[256,256]{1,0:T(8,128)(2,1)S(1)} %collective-permute-done.13.refs_2_.rest_2_, ...), custom_call_target="tpu_custom_call" | custom-call | flops 2415919104 | bytes 4456448 | tf_op jit(solution)/shard_map/wgrad/pallas_call | solution.py:330
  96.8 2.0 %wgrad.2.keep_ref = bf16[4,128,768]{2,1,0:T(8,128)(2,1)S(1)} custom-call(bf16[4,256,1024]{2,1,0:T(8,128)(2,1)S(1)} %copy-done.5, bf16[256,256]{1,0:T(8,128)(2,1)S(1)} %get-tuple-element.28.refs_0_.gq_ref, bf16[256,256]{1,0:T(8,128)(2,1)S(1)} %collective-permute-done.12.refs_1_.rest_0_, bf16[256,256]{1,0:T(8,128)(2,1)S(1)} %collective-permute-done.13.refs_2_.rest_2_, ...), custom_call_target="tpu_custom_call" | custom-call | flops 2415919104 | bytes 4456448 | tf_op jit(solution)/shard_map/wgrad/pallas_call | solution.py:330
  99.4 1.3 pair.1
  100.8 1.2 collective-permute-start.21
  102.0 4.1 %collective-permute-start.20 = (bf16[128,768]{1,0:T(8,128)(2,1)S(1)}, bf16[128,768]{1,0:T(8,128)(2,1)S(1)}, u32[]{:S(2)}, u32[]{:S(2)}) collective-permute-start(bf16[128,768]{1,0:T(8,128)(2,1)S(1)} %get-tuple-element.32), channel_id=1, source_target_pairs={{0,128},{16,144},{32,160},{48,176},{64,192},{80,208},{96,224},{112... | collective-permute-start | bytes 589832 | tf_op jit(solution)/shard_map/ppermute | solution.py:402
  106.1 8.1 %all-to-all-done.3 = bf16[4,2,512,256]{3,2,1,0:T(8,128)(2,1)} async-done(((bf16[4,2,512,256]{3,2,1,0:T(8,128)(2,1)}), bf16[4,2,512,256]{3,2,1,0:T(8,128)(2,1)}, u32[]{:S(2)}, u32[]{:S(2)}) %all-to-all-start.3) | async-done | bytes 2097184 | tf_op jit(solution)/shard_map/all_to_all | solution.py:454
  114.2 2.0 %convert_reduce_fusion = f32[2,512,256]{2,1,0:T(8,128)S(1)} fusion(bf16[4,2,512,256]{3,2,1,0:T(8,128)(2,1)} %all-to-all-done.3), kind=kLoop, calls=%fused_computation | loop fusion | flops 1835008 | bytes 3145728 | tf_op jit(solution)/shard_map/reduce_sum | solution.py:463
  116.3 5.2 %collective-permute-start.22 = (bf16[512,256]{1,0:T(8,128)(2,1)S(1)}, bf16[512,256]{1,0:T(8,128)(2,1)S(1)}, u32[]{:S(2)}, u32[]{:S(2)}) collective-permute-start(bf16[512,256]{1,0:T(8,128)(2,1)S(1)} %fusion.1), channel_id=1, source_target_pairs={{0,8},{2,10},{4,12},{6,14},{8,0},{10,2},{12,4},{14,6},{1,9},{3,11}... | collective-permute-start | bytes 786440 | tf_op jit(solution)/shard_map/ppermute | solution.py:412
  121.5 2.5 %collective-permute-done.20 = bf16[128,768]{1,0:T(8,128)(2,1)S(1)} collective-permute-done((bf16[128,768]{1,0:T(8,128)(2,1)S(1)}, bf16[128,768]{1,0:T(8,128)(2,1)S(1)}, u32[]{:S(2)}, u32[]{:S(2)}) %collective-permute-start.20) | collective-permute-done | bytes 196640 | tf_op jit(solution)/shard_map/ppermute | solution.py:402
  124.0 10.2 %collective-permute-done.19 = bf16[128,768]{1,0:T(8,128)(2,1)S(1)} collective-permute-done((bf16[128,768]{1,0:T(8,128)(2,1)S(1)}, bf16[128,768]{1,0:T(8,128)(2,1)S(1)}, u32[]{:S(2)}, u32[]{:S(2)}) %collective-permute-start.19) | collective-permute-done | bytes 196640 | tf_op jit(solution)/shard_map/ppermute | solution.py:402
  134.2 0.8 fusion.3
  135.0 0.8 fusion.2
  (41 shorter events, 2.0 us)
Async XLA Ops:
  0.6 0.9 copy-start.6
  7.0 11.4 %collective-permute-start = (bf16[64,1024]{1,0:T(8,128)(2,1)S(1)}, bf16[64,1024]{1,0:T(8,128)(2,1)S(1)}, u32[]{:S(2)}, u32[]{:S(2)}) collective-permute-start(bf16[64,1024]{1,0:T(8,128)(2,1)S(1)} %get-tuple-element.22), channel_id=1, source_target_pairs={{0,16},{16,32},{32,48},{48,0},{64,80},{80,96},{96,112},{112,64},{1... | collective-permute-start | bytes 393224 | tf_op jit(solution)/shard_map/ppermute | solution.py:397
  8.5 9.8 %collective-permute-start.1 = (bf16[64,1024]{1,0:T(8,128)(2,1)S(1)}, bf16[64,1024]{1,0:T(8,128)(2,1)S(1)}, u32[]{:S(2)}, u32[]{:S(2)}) collective-permute-start(bf16[64,1024]{1,0:T(8,128)(2,1)S(1)} %get-tuple-element.23), channel_id=1, source_target_pairs={{0,32},{16,48},{32,0},{48,16},{64,96},{80,112},{96,64},{112,80},{1... | collective-permute-start | bytes 393224 | tf_op jit(solution)/shard_map/ppermute | solution.py:397
  11.3 7.1 %collective-permute-start.2 = (bf16[64,1024]{1,0:T(8,128)(2,1)S(1)}, bf16[64,1024]{1,0:T(8,128)(2,1)S(1)}, u32[]{:S(2)}, u32[]{:S(2)}) collective-permute-start(bf16[64,1024]{1,0:T(8,128)(2,1)S(1)} %get-tuple-element.24), channel_id=1, source_target_pairs={{0,48},{16,0},{32,16},{48,32},{64,112},{80,64},{96,80},{112,96},{1... | collective-permute-start | bytes 393224 | tf_op jit(solution)/shard_map/ppermute | solution.py:397
  12.7 19.3 %all-to-all-start = ((bf16[16,16,1024]{2,1,0:T(8,128)(2,1)}), bf16[16,16,1024]{2,1,0:T(8,128)(2,1)S(1)}, u32[]{:S(2)}, u32[]{:S(2)}) async-start(bf16[16,16,1024]{2,1,0:T(8,128)(2,1)} %bitcast.4), calls=%async_computation | async-start | bytes 1048576 | tf_op jit(solution)/shard_map/all_to_all | solution.py:434
  18.3 13.7 %copy-start.7 = (s32[1,16]{1,0:T(1,128)S(1)}, s32[1,16]{1,0:T(1,128)}, u32[]{:S(2)}) copy-start(s32[1,16]{1,0:T(1,128)} %param.12) | copy-start | bytes 196
  18.3 13.7 %copy-start.8 = (s32[1,16]{1,0:T(1,128)S(1)}, s32[1,16]{1,0:T(1,128)}, u32[]{:S(2)}) copy-start(s32[1,16]{1,0:T(1,128)} %param.13) | copy-start | bytes 196
  18.4 20.5 %collective-permute-start.3 = (bf16[3,64,1024]{2,1,0:T(8,128)(2,1)S(1)}, bf16[3,64,1024]{2,1,0:T(8,128)(2,1)S(1)}, u32[]{:S(2)}, u32[]{:S(2)}) collective-permute-start(bf16[3,64,1024]{2,1,0:T(8,128)(2,1)S(1)} %stack.21.refs_0_.rest_0_), channel_id=1, source_target_pairs={{0,2},{2,4},{4,6},{6,0},{8,10},{10,12},{12,14},{14,8},{1,3},{3,5},... | collective-permute-start | bytes 1179656 | tf_op jit(solution)/shard_map/ppermute | solution.py:407
  20.0 18.8 %collective-permute-start.4 = (bf16[3,64,1024]{2,1,0:T(8,128)(2,1)S(1)}, bf16[3,64,1024]{2,1,0:T(8,128)(2,1)S(1)}, u32[]{:S(2)}, u32[]{:S(2)}) collective-permute-start(bf16[3,64,1024]{2,1,0:T(8,128)(2,1)S(1)} %stack.21.refs_0_.rest_0_), channel_id=1, source_target_pairs={{0,4},{2,6},{4,0},{6,2},{8,12},{10,14},{12,8},{14,10},{1,5},{3,7},... | collective-permute-start | bytes 1179656 | tf_op jit(solution)/shard_map/ppermute | solution.py:407
  21.0 17.9 %collective-permute-start.5 = (bf16[3,64,1024]{2,1,0:T(8,128)(2,1)S(1)}, bf16[3,64,1024]{2,1,0:T(8,128)(2,1)S(1)}, u32[]{:S(2)}, u32[]{:S(2)}) collective-permute-start(bf16[3,64,1024]{2,1,0:T(8,128)(2,1)S(1)} %stack.21.refs_0_.rest_0_), channel_id=1, source_target_pairs={{0,6},{2,0},{4,2},{6,4},{8,14},{10,8},{12,10},{14,12},{1,7},{3,1},... | collective-permute-start | bytes 1179656 | tf_op jit(solution)/shard_map/ppermute | solution.py:407
  33.5 18.7 %all-to-all-start.2 = ((bf16[16,2,16,512]{3,2,1,0:T(8,128)(2,1)}), bf16[16,2,16,512]{3,2,1,0:T(8,128)(2,1)S(1)}, u32[]{:S(2)}, u32[]{:S(2)}) async-start(bf16[16,2,16,512]{3,2,1,0:T(8,128)(2,1)} %pick.3), calls=%async_computation.2 | async-start | bytes 1048576 | tf_op jit(solution)/shard_map/all_to_all | solution.py:434
  39.0 36.0 %copy-start = (bf16[4096,256]{1,0:T(8,128)(2,1)S(1)}, bf16[4096,256]{1,0:T(8,128)(2,1)}, u32[]{:S(2)}) copy-start(bf16[4096,256]{1,0:T(8,128)(2,1)} %wq_ref.3) | copy-start | bytes 6291460
  40.5 1.4 %copy-start.4 = (bf16[4,256,1024]{2,1,0:T(8,128)(2,1)}, bf16[4,256,1024]{2,1,0:T(8,128)(2,1)S(1)}, u32[]{:S(2)}) copy-start(bf16[4,256,1024]{2,1,0:T(8,128)(2,1)S(1)} %merge.1.rest_0_.x_ref) | copy-start | bytes 6291460
  52.2 22.4 %all-to-all-start.1 = ((bf16[16,2,16,512]{3,2,1,0:T(8,128)(2,1)}), bf16[16,2,16,512]{3,2,1,0:T(8,128)(2,1)S(1)}, u32[]{:S(2)}, u32[]{:S(2)}) async-start(bf16[16,2,16,512]{3,2,1,0:T(8,128)(2,1)} %pick.2), calls=%async_computation.1 | async-start | bytes 1048576 | tf_op jit(solution)/shard_map/all_to_all | solution.py:434
  60.3 6.2 %collective-permute-start.8 = (f32[8,256]{1,0:T(8,128)S(1)}, f32[8,256]{1,0:T(8,128)S(1)}, u32[]{:S(2)}, u32[]{:S(2)}) collective-permute-start(f32[8,256]{1,0:T(8,128)S(1)} %get-tuple-element.25), channel_id=1, source_target_pairs={{0,48},{16,0},{32,16},{48,32},{64,112},{80,64},{96,80},{112,96},{1... | collective-permute-start | bytes 24584 | tf_op jit(solution)/shard_map/ppermute | solution.py:397
  63.0 5.2 %collective-permute-start.7 = (f32[8,256]{1,0:T(8,128)S(1)}, f32[8,256]{1,0:T(8,128)S(1)}, u32[]{:S(2)}, u32[]{:S(2)}) collective-permute-start(f32[8,256]{1,0:T(8,128)S(1)} %get-tuple-element.25), channel_id=1, source_target_pairs={{0,32},{16,48},{32,0},{48,16},{64,96},{80,112},{96,64},{112,80},{1... | collective-permute-start | bytes 24584 | tf_op jit(solution)/shard_map/ppermute | solution.py:397
  63.9 5.0 %collective-permute-start.6 = (f32[8,256]{1,0:T(8,128)S(1)}, f32[8,256]{1,0:T(8,128)S(1)}, u32[]{:S(2)}, u32[]{:S(2)}) collective-permute-start(f32[8,256]{1,0:T(8,128)S(1)} %get-tuple-element.25), channel_id=1, source_target_pairs={{0,16},{16,32},{32,48},{48,0},{64,80},{80,96},{96,112},{112,64},{1... | collective-permute-start | bytes 24584 | tf_op jit(solution)/shard_map/ppermute | solution.py:397
  64.8 19.5 %collective-permute-start.12 = (bf16[256,256]{1,0:T(8,128)(2,1)S(1)}, bf16[256,256]{1,0:T(8,128)(2,1)S(1)}, u32[]{:S(2)}, u32[]{:S(2)}) collective-permute-start(bf16[256,256]{1,0:T(8,128)(2,1)S(1)} %get-tuple-element.28.refs_0_.gq_ref), channel_id=1, source_target_pairs={{0,16},{16,32},{32,48},{48,0},{64,80},{80,96},{96,112},{112,64},{1... | collective-permute-start | bytes 393224 | tf_op jit(solution)/shard_map/ppermute | solution.py:397
  68.9 4.8 %collective-permute-start.9 = (f32[4,8,256]{2,1,0:T(8,128)S(1)}, f32[4,8,256]{2,1,0:T(8,128)S(1)}, u32[]{:S(2)}, u32[]{:S(2)}) collective-permute-start(f32[4,8,256]{2,1,0:T(8,128)S(1)} %pad_maximum_fusion.rest_0_), channel_id=1, source_target_pairs={{0,64},{16,80},{32,96},{48,112},{64,128},{80,144},{96,160},{112,17... | collective-permute-start | bytes 98312 | tf_op jit(solution)/shard_map/ppermute | solution.py:402
  70.2 4.8 %collective-permute-start.10 = (f32[4,8,256]{2,1,0:T(8,128)S(1)}, f32[4,8,256]{2,1,0:T(8,128)S(1)}, u32[]{:S(2)}, u32[]{:S(2)}) collective-permute-start(f32[4,8,256]{2,1,0:T(8,128)S(1)} %pad_maximum_fusion.rest_0_), channel_id=1, source_target_pairs={{0,128},{16,144},{32,160},{48,176},{64,192},{80,208},{96,224},{112... | collective-permute-start | bytes 98312 | tf_op jit(solution)/shard_map/ppermute | solution.py:402
  70.8 4.3 %collective-permute-start.11 = (f32[4,8,256]{2,1,0:T(8,128)S(1)}, f32[4,8,256]{2,1,0:T(8,128)S(1)}, u32[]{:S(2)}, u32[]{:S(2)}) collective-permute-start(f32[4,8,256]{2,1,0:T(8,128)S(1)} %pad_maximum_fusion.rest_0_), channel_id=1, source_target_pairs={{0,192},{16,208},{32,224},{48,240},{64,0},{80,16},{96,32},{112,48}... | collective-permute-start | bytes 98312 | tf_op jit(solution)/shard_map/ppermute | solution.py:402
  72.3 13.3 %collective-permute-start.13 = (bf16[256,256]{1,0:T(8,128)(2,1)S(1)}, bf16[256,256]{1,0:T(8,128)(2,1)S(1)}, u32[]{:S(2)}, u32[]{:S(2)}) collective-permute-start(bf16[256,256]{1,0:T(8,128)(2,1)S(1)} %get-tuple-element.28.refs_0_.gq_ref), channel_id=1, source_target_pairs={{0,32},{16,48},{32,0},{48,16},{64,96},{80,112},{96,64},{112,80},{1... | collective-permute-start | bytes 393224 | tf_op jit(solution)/shard_map/ppermute | solution.py:397
  73.7 11.8 %collective-permute-start.14 = (bf16[256,256]{1,0:T(8,128)(2,1)S(1)}, bf16[256,256]{1,0:T(8,128)(2,1)S(1)}, u32[]{:S(2)}, u32[]{:S(2)}) collective-permute-start(bf16[256,256]{1,0:T(8,128)(2,1)S(1)} %get-tuple-element.28.refs_0_.gq_ref), channel_id=1, source_target_pairs={{0,48},{16,0},{32,16},{48,32},{64,112},{80,64},{96,80},{112,96},{1... | collective-permute-start | bytes 393224 | tf_op jit(solution)/shard_map/ppermute | solution.py:397
  75.1 1.6 %copy-start.1 = (bf16[4096,256]{1,0:T(8,128)(2,1)S(1)}, bf16[4096,256]{1,0:T(8,128)(2,1)}, u32[]{:S(2)}) copy-start(bf16[4096,256]{1,0:T(8,128)(2,1)} %wk_ref.3) | copy-start | bytes 6291460
  76.7 1.6 %copy-start.2 = (bf16[4096,256]{1,0:T(8,128)(2,1)S(1)}, bf16[4096,256]{1,0:T(8,128)(2,1)}, u32[]{:S(2)}) copy-start(bf16[4096,256]{1,0:T(8,128)(2,1)} %wv_ref.3) | copy-start | bytes 6291460
  81.4 12.4 %collective-permute-start.15 = (bf16[256,512]{1,0:T(8,128)(2,1)S(1)}, bf16[256,512]{1,0:T(8,128)(2,1)S(1)}, u32[]{:S(2)}, u32[]{:S(2)}) collective-permute-start(bf16[256,512]{1,0:T(8,128)(2,1)S(1)} %get-tuple-element.29.refs_4_.gkv_ref), channel_id=1, source_target_pairs={{0,16},{16,32},{32,48},{48,0},{64,80},{80,96},{96,112},{112,64},{1... | collective-permute-start | bytes 786440 | tf_op jit(solution)/shard_map/ppermute | solution.py:397
  82.2 11.7 %collective-permute-start.16 = (bf16[256,512]{1,0:T(8,128)(2,1)S(1)}, bf16[256,512]{1,0:T(8,128)(2,1)S(1)}, u32[]{:S(2)}, u32[]{:S(2)}) collective-permute-start(bf16[256,512]{1,0:T(8,128)(2,1)S(1)} %get-tuple-element.29.refs_4_.gkv_ref), channel_id=1, source_target_pairs={{0,32},{16,48},{32,0},{48,16},{64,96},{80,112},{96,64},{112,80},{1... | collective-permute-start | bytes 786440 | tf_op jit(solution)/shard_map/ppermute | solution.py:397
  84.2 9.6 %collective-permute-start.17 = (bf16[256,512]{1,0:T(8,128)(2,1)S(1)}, bf16[256,512]{1,0:T(8,128)(2,1)}, u32[]{:S(2)}, u32[]{:S(2)}) collective-permute-start(bf16[256,512]{1,0:T(8,128)(2,1)S(1)} %get-tuple-element.29.refs_4_.gkv_ref), channel_id=1, source_target_pairs={{0,48},{16,0},{32,16},{48,32},{64,112},{80,64},{96,80},{112,96},{1... | collective-permute-start | bytes 786440 | tf_op jit(solution)/shard_map/ppermute | solution.py:397
  87.4 1.3 copy-start.3
  88.7 5.2 %copy-start.5 = (bf16[4,256,1024]{2,1,0:T(8,128)(2,1)S(1)}, bf16[4,256,1024]{2,1,0:T(8,128)(2,1)}, u32[]{:S(2)}) copy-start(bf16[4,256,1024]{2,1,0:T(8,128)(2,1)} %copy-done.4) | copy-start | bytes 6291460
  88.7 25.5 %all-to-all-start.3 = ((bf16[4,2,512,256]{3,2,1,0:T(8,128)(2,1)}), bf16[4,2,512,256]{3,2,1,0:T(8,128)(2,1)}, u32[]{:S(2)}, u32[]{:S(2)}) async-start(bf16[4,2,512,256]{3,2,1,0:T(8,128)(2,1)} %copy-done.3), calls=%async_computation.3 | async-start | bytes 4194304 | tf_op jit(solution)/shard_map/all_to_all | solution.py:454
  96.8 2.6 %collective-permute-start.18 = (bf16[4,128,768]{2,1,0:T(8,128)(2,1)}, bf16[4,128,768]{2,1,0:T(8,128)(2,1)}, u32[]{:S(2)}, u32[]{:S(2)}) collective-permute-start(bf16[4,128,768]{2,1,0:T(8,128)(2,1)} %wgrad.3), channel_id=1, source_target_pairs={{0,1},{1,0},{2,3},{3,2},{4,5},{5,4},{6,7},{7,6},{8,9},{9,8},{10,11... | collective-permute-start | bytes 2359304 | tf_op jit(solution)/shard_map/ppermute | solution.py:416
  100.8 20.8 %collective-permute-start.21 = (bf16[128,768]{1,0:T(8,128)(2,1)S(1)}, bf16[128,768]{1,0:T(8,128)(2,1)S(1)}, u32[]{:S(2)}, u32[]{:S(2)}) collective-permute-start(bf16[128,768]{1,0:T(8,128)(2,1)S(1)} %get-tuple-element.33), channel_id=1, source_target_pairs={{0,192},{16,208},{32,224},{48,240},{64,0},{80,16},{96,32},{112,48}... | collective-permute-start | bytes 589832 | tf_op jit(solution)/shard_map/ppermute | solution.py:402
  102.0 22.0 %collective-permute-start.20 = (bf16[128,768]{1,0:T(8,128)(2,1)S(1)}, bf16[128,768]{1,0:T(8,128)(2,1)S(1)}, u32[]{:S(2)}, u32[]{:S(2)}) collective-permute-start(bf16[128,768]{1,0:T(8,128)(2,1)S(1)} %get-tuple-element.32), channel_id=1, source_target_pairs={{0,128},{16,144},{32,160},{48,176},{64,192},{80,208},{96,224},{112... | collective-permute-start | bytes 589832 | tf_op jit(solution)/shard_map/ppermute | solution.py:402
  106.1 28.0 %collective-permute-start.19 = (bf16[128,768]{1,0:T(8,128)(2,1)S(1)}, bf16[128,768]{1,0:T(8,128)(2,1)S(1)}, u32[]{:S(2)}, u32[]{:S(2)}) collective-permute-start(bf16[128,768]{1,0:T(8,128)(2,1)S(1)} %get-tuple-element.31), channel_id=1, source_target_pairs={{0,64},{16,80},{32,96},{48,112},{64,128},{80,144},{96,160},{112,17... | collective-permute-start | bytes 589832 | tf_op jit(solution)/shard_map/ppermute | solution.py:402
  116.3 18.7 %collective-permute-start.22 = (bf16[512,256]{1,0:T(8,128)(2,1)S(1)}, bf16[512,256]{1,0:T(8,128)(2,1)S(1)}, u32[]{:S(2)}, u32[]{:S(2)}) collective-permute-start(bf16[512,256]{1,0:T(8,128)(2,1)S(1)} %fusion.1), channel_id=1, source_target_pairs={{0,8},{2,10},{4,12},{6,14},{8,0},{10,2},{12,4},{14,6},{1,9},{3,11}... | collective-permute-start | bytes 786440 | tf_op jit(solution)/shard_map/ppermute | solution.py:412

commit v4 on v3

--- a/solution.py
+++ b/solution.py
@@ -19,6 +19,7 @@
 VMEM = pl.BlockSpec(memory_space=pltpu.VMEM)
 SMEM = pl.BlockSpec(memory_space=pltpu.SMEM)
 ANY = pl.BlockSpec(memory_space=pl.ANY)
+HBM = pl.BlockSpec(memory_space=pltpu.HBM)
 
 
 def _params(limit):
@@ -392,6 +393,28 @@
     )(wq, wk, wv, gq, gkv, *after)
 
 
+def _join_body(terms_ref, keep_ref, send_ref):
+    mine = lax.axis_index("head") // YS
+    for half, o_ref in ((mine, keep_ref), (1 - mine, send_ref)):
+        acc = terms_ref[0, half].astype(F32)
+        for y in range(1, YS):
+            acc = acc + terms_ref[y, half].astype(F32)
+        o_ref[...] = acc.astype(o_ref.dtype)
+
+
+def join(terms):
+    shape = terms.shape[2:]
+    return pl.pallas_call(
+        _join_body,
+        in_specs=[VMEM],
+        out_specs=[VMEM, VMEM],
+        out_shape=[jax.ShapeDtypeStruct(shape, F32), jax.ShapeDtypeStruct(shape, BF)],
+        compiler_params=_params(SMALL),
+        cost_estimate=_cost(4 * HINT // 30, 2 * terms.size),
+        name="join",
+    )(terms)
+
+
 def shift_x(v, k):
     pairs = [(z * XS + x, z * XS + (x + k) % XS) for z in range(ZS) for x in range(XS)]
     return lax.ppermute(v, "doc", pairs)
@@ -460,11 +483,8 @@
     total, *pieces = pair(mine, swap_cores(theirs))
     for k in range(1, ZS):
         total = total + shift_z(pieces[k - 1], k).astype(F32)
-    sums = jnp.sum(terms.astype(F32), axis=0)
-    my_half = lax.axis_index("head") // YS
-    keep = lax.dynamic_index_in_dim(sums, my_half, axis=0, keepdims=False)
-    send = lax.dynamic_index_in_dim(sums, 1 - my_half, axis=0, keepdims=False)
-    features = (keep + swap_halves(send.astype(BF)).astype(F32)).astype(BF)
+    keep, send = join(terms)
+    features = (keep + swap_halves(send).astype(F32)).astype(BF)
     return (
         gk.reshape(1, 1, t, n),
         gv.reshape(1, 1, t, n),

time: 138 us -> 137 us (level)
    ppermute x1, waiting for transfers between devices: 0.01 us -> 9.62 us  [swap_halves(): return lax.ppermute(v, 'head', pairs)]
    ppermute x6, waiting for transfers between devices: 13.1 us -> 4.73 us  [shift_z(): return lax.ppermute(v, 'doc', pairs)]
    reduce_sum x1 -> x0, other arithmetic: 2.02 us -> none  [per_device(): sums = jnp.sum(terms.astype(F32), axis=0)]
    pallas_call x0 -> x1, Pallas kernels: none -> 1.84 us  [join(): pl.pallas_call(_join_body, in_specs=[VMEM], out_specs=[VMEM, VMEM], out_s...]
    all_to_all x1, waiting for transfers between devices: 8.12 us -> 9.79 us  [per_device(): lax.all_to_all(terms, 'head', split_axis=0, concat_axis=0, tiled=True, ax...]
    ppermute x12, starting transfers between devices: 18.4 us -> 16.9 us  [shift_x(): return lax.ppermute(v, 'doc', pairs)]
  transfers between devices with their start and end apart: 27 -> 27, of which waited for: 9 -> 11; matrix products, arithmetic and copies ran while one was open for 2% -> 1% of each run, Pallas kernels for 13% -> 13%
where the time goes in v4:
time: 137 us; the launch traced here: 135 us
  starting transfers between devices  57.5 us (42%)
  waiting for transfers between devices  44.3 us (32%)
  Pallas kernels  23.3 us (17%)
  local copies, waits for them, and re-layouts  7.57 us (6%)
  other arithmetic  1.77 us (1%)
    all_to_all x3, waiting for transfers between devices, spread(): return lax.all_to_all(v, 'doc', split_axis=0, concat_axis=0, tiled=True)  18 us
    ppermute x12, starting transfers between devices, shift_x(): return lax.ppermute(v, 'doc', pairs)  16.9 us
    all_to_all x3, starting transfers between devices, spread(): return lax.all_to_all(v, 'doc', split_axis=0, concat_axis=0, tiled=True)  16.3 us
    all_to_all x1, waiting for transfers between devices, per_device(): lax.all_to_all(terms, 'head', split_axis=0, concat_axis=0, tiled=True, ax...  9.79 us
    ppermute x1, waiting for transfers between devices, swap_halves(): return lax.ppermute(v, 'head', pairs)  9.62 us
    ppermute x6, starting transfers between devices, shift_z(): return lax.ppermute(v, 'doc', pairs)  8.43 us
    unnamed x18, local copies, waits for them, and re-layouts  6.82 us
    pallas_call x1, Pallas kernels, project(): pl.pallas_call(_project_body, in_specs=[ANY] * 5, out_specs=[VMEM] * (1 +...  5.45 us
  transfers between devices with their start and end apart: 27, of which 11 were waited for; matrix products, arithmetic and copies ran while one was open for 1% of the time, Pallas kernels for 13%

profile of v4, /device:TPU:72, one launch (start us, length us, event | category | flops | bytes accessed | tf_op | source)
XLA Modules:
  0.0 135.2 jit_solution(1633443735941960174)
XLA Ops:
  0.6 0.9 copy-done.6
  1.5 5.4 %project.1 = (bf16[256,1024]{1,0:T(8,128)(2,1)}, bf16[256,1024]{1,0:T(8,128)(2,1)S(1)}, bf16[64,1024]{1,0:T(8,128)(2,1)S(1)}, bf16[64,1024]{1,0:T(8,128)(2,1)S(1)}, bf16[64,1024]{1,0:T(8,128)(2,1)S(1)}) custom-call(bf16[256,4096]{1,0:T(8,128)(2,1)} %bitcast.21, bf16[4096,256]{1,0:T(8,128)(2,1)} %wq_ref.3, bf16[4096,256]{1,0:T(8,128)(2,1)} %wk_ref.3, ...), custom_call_target="tpu_custom_call" | custom-call | flops 1610612736 | bytes 8388608 | tf_op jit(solution)/shard_map/project/pallas_call | solution.py:93
  7.0 1.6 %collective-permute-start = (bf16[64,1024]{1,0:T(8,128)(2,1)S(1)}, bf16[64,1024]{1,0:T(8,128)(2,1)S(1)}, u32[]{:S(2)}, u32[]{:S(2)}) collective-permute-start(bf16[64,1024]{1,0:T(8,128)(2,1)S(1)} %get-tuple-element.24), channel_id=1, source_target_pairs={{0,16},{16,32},{32,48},{48,0},{64,80},{80,96},{96,112},{112,64},{1... | collective-permute-start | bytes 393224 | tf_op jit(solution)/shard_map/ppermute | solution.py:420
  8.6 2.7 %collective-permute-start.1 = (bf16[64,1024]{1,0:T(8,128)(2,1)S(1)}, bf16[64,1024]{1,0:T(8,128)(2,1)S(1)}, u32[]{:S(2)}, u32[]{:S(2)}) collective-permute-start(bf16[64,1024]{1,0:T(8,128)(2,1)S(1)} %get-tuple-element.25), channel_id=1, source_target_pairs={{0,32},{16,48},{32,0},{48,16},{64,96},{80,112},{96,64},{112,80},{1... | collective-permute-start | bytes 393224 | tf_op jit(solution)/shard_map/ppermute | solution.py:420
  11.3 1.4 %collective-permute-start.2 = (bf16[64,1024]{1,0:T(8,128)(2,1)S(1)}, bf16[64,1024]{1,0:T(8,128)(2,1)S(1)}, u32[]{:S(2)}, u32[]{:S(2)}) collective-permute-start(bf16[64,1024]{1,0:T(8,128)(2,1)S(1)} %get-tuple-element.26), channel_id=1, source_target_pairs={{0,48},{16,0},{32,16},{48,32},{64,112},{80,64},{96,80},{112,96},{1... | collective-permute-start | bytes 393224 | tf_op jit(solution)/shard_map/ppermute | solution.py:420
  12.7 5.6 %all-to-all-start = ((bf16[16,16,1024]{2,1,0:T(8,128)(2,1)}), bf16[16,16,1024]{2,1,0:T(8,128)(2,1)S(1)}, u32[]{:S(2)}, u32[]{:S(2)}) async-start(bf16[16,16,1024]{2,1,0:T(8,128)(2,1)} %bitcast.4), calls=%async_computation | async-start | bytes 1048576 | tf_op jit(solution)/shard_map/all_to_all | solution.py:457
  18.9 2.6 %collective-permute-start.4 = (bf16[3,64,1024]{2,1,0:T(8,128)(2,1)S(1)}, bf16[3,64,1024]{2,1,0:T(8,128)(2,1)S(1)}, u32[]{:S(2)}, u32[]{:S(2)}) collective-permute-start(bf16[3,64,1024]{2,1,0:T(8,128)(2,1)S(1)} %stack.21.refs_0_.rest_0_), channel_id=1, source_target_pairs={{0,4},{2,6},{4,0},{6,2},{8,12},{10,14},{12,8},{14,10},{1,5},{3,7},... | collective-permute-start | bytes 1179656 | tf_op jit(solution)/shard_map/ppermute | solution.py:430
  21.5 1.9 %collective-permute-start.3 = (bf16[3,64,1024]{2,1,0:T(8,128)(2,1)S(1)}, bf16[3,64,1024]{2,1,0:T(8,128)(2,1)}, u32[]{:S(2)}, u32[]{:S(2)}) collective-permute-start(bf16[3,64,1024]{2,1,0:T(8,128)(2,1)S(1)} %stack.21.refs_0_.rest_0_), channel_id=1, source_target_pairs={{0,2},{2,4},{4,6},{6,0},{8,10},{10,12},{12,14},{14,8},{1,3},{3,5},... | collective-permute-start | bytes 1179656 | tf_op jit(solution)/shard_map/ppermute | solution.py:430
  23.4 8.6 %all-to-all-done.all_ref = bf16[16,16,1024]{2,1,0:T(8,128)(2,1)S(1)} async-done(((bf16[16,16,1024]{2,1,0:T(8,128)(2,1)}), bf16[16,16,1024]{2,1,0:T(8,128)(2,1)S(1)}, u32[]{:S(2)}, u32[]{:S(2)}) %all-to-all-start) | async-done | bytes 524320 | tf_op jit(solution)/shard_map/all_to_all | solution.py:457
  32.1 1.5 %pick.3 = bf16[16,2,16,512]{3,2,1,0:T(8,128)(2,1)} custom-call(s32[16]{0:T(128)S(1)} %bitcast.15, s32[16]{0:T(128)S(1)} %bitcast.18, bf16[16,16,1024]{2,1,0:T(8,128)(2,1)S(1)} %all-to-all-done.all_ref, bf16[3,64,1024]{2,1,0:T(8,128)(2,1)S(1)} %stack.21.refs_0_.rest_0_), custom_call_target="tpu_custom_call" | custom-call | bytes 1048576 | tf_op jit(solution)/shard_map/pick/pallas_call | solution.py:182
  33.5 5.4 %all-to-all-start.2 = ((bf16[16,2,16,512]{3,2,1,0:T(8,128)(2,1)}), bf16[16,2,16,512]{3,2,1,0:T(8,128)(2,1)S(1)}, u32[]{:S(2)}, u32[]{:S(2)}) async-start(bf16[16,2,16,512]{3,2,1,0:T(8,128)(2,1)} %pick.3), calls=%async_computation.2 | async-start | bytes 1048576 | tf_op jit(solution)/shard_map/all_to_all | solution.py:457
  38.9 1.1 merge.1.rest_0_.x_ref
  40.1 1.4 %pick.2 = bf16[16,2,16,512]{3,2,1,0:T(8,128)(2,1)} custom-call(s32[16]{0:T(128)S(1)} %bitcast.16, s32[16]{0:T(128)S(1)} %bitcast.19, bf16[16,16,1024]{2,1,0:T(8,128)(2,1)S(1)} %all-to-all-done.all_ref, bf16[4,256,1024]{2,1,0:T(8,128)(2,1)S(1)} %merge.1.rest_0_.x_ref), custom_call_target="tpu_custom_call" | custom-call | bytes 1048576 | tf_op jit(solution)/shard_map/pick/pallas_call | solution.py:182
  41.5 1.3 copy-done.4
  42.9 9.4 %all-to-all-done.2.kv_ref = bf16[16,2,16,512]{3,2,1,0:T(8,128)(2,1)S(1)} async-done(((bf16[16,2,16,512]{3,2,1,0:T(8,128)(2,1)}), bf16[16,2,16,512]{3,2,1,0:T(8,128)(2,1)S(1)}, u32[]{:S(2)}, u32[]{:S(2)}) %all-to-all-start.2) | async-done | bytes 524320 | tf_op jit(solution)/shard_map/all_to_all | solution.py:457
  52.2 5.4 %all-to-all-start.1 = ((bf16[16,2,16,512]{3,2,1,0:T(8,128)(2,1)}), bf16[16,2,16,512]{3,2,1,0:T(8,128)(2,1)S(1)}, u32[]{:S(2)}, u32[]{:S(2)}) async-start(bf16[16,2,16,512]{3,2,1,0:T(8,128)(2,1)} %pick.2), calls=%async_computation.1 | async-start | bytes 1048576 | tf_op jit(solution)/shard_map/all_to_all | solution.py:457
  57.6 2.7 %attend.1 = (bf16[256,256]{1,0:T(8,128)(2,1)S(1)}, f32[8,256]{1,0:T(8,128)S(1)}) custom-call(bf16[256,1024]{1,0:T(8,128)(2,1)} %get-tuple-element.22.qkv_ref, bf16[16,2,16,512]{3,2,1,0:T(8,128)(2,1)S(1)} %all-to-all-done.2.kv_ref), custom_call_target="tpu_custom_call" | custom-call | flops 369098752 | bytes 2621440 | tf_op jit(solution)/shard_map/attend/pallas_call | solution.py:231
  60.3 2.8 %collective-permute-start.8 = (f32[8,256]{1,0:T(8,128)S(1)}, f32[8,256]{1,0:T(8,128)S(1)}, u32[]{:S(2)}, u32[]{:S(2)}) collective-permute-start(f32[8,256]{1,0:T(8,128)S(1)} %get-tuple-element.27), channel_id=1, source_target_pairs={{0,48},{16,0},{32,16},{48,32},{64,112},{80,64},{96,80},{112,96},{1... | collective-permute-start | bytes 24584 | tf_op jit(solution)/shard_map/ppermute | solution.py:420
  63.1 0.9 collective-permute-start.7
  63.9 0.9 collective-permute-start.6
  64.8 2.4 %collective-permute-start.14 = (bf16[256,256]{1,0:T(8,128)(2,1)S(1)}, bf16[256,256]{1,0:T(8,128)(2,1)S(1)}, u32[]{:S(2)}, u32[]{:S(2)}) collective-permute-start(bf16[256,256]{1,0:T(8,128)(2,1)S(1)} %get-tuple-element.30.refs_0_.gq_ref), channel_id=1, source_target_pairs={{0,48},{16,0},{32,16},{48,32},{64,112},{80,64},{96,80},{112,96},{1... | collective-permute-start | bytes 393224 | tf_op jit(solution)/shard_map/ppermute | solution.py:420
  67.2 1.1 collective-permute-done.7
  69.4 3.3 %collective-permute-start.10 = (f32[4,8,256]{2,1,0:T(8,128)S(1)}, f32[4,8,256]{2,1,0:T(8,128)S(1)}, u32[]{:S(2)}, u32[]{:S(2)}) collective-permute-start(f32[4,8,256]{2,1,0:T(8,128)S(1)} %pad_maximum_fusion.rest_0_), channel_id=1, source_target_pairs={{0,128},{16,144},{32,160},{48,176},{64,192},{80,208},{96,224},{112... | collective-permute-start | bytes 98312 | tf_op jit(solution)/shard_map/ppermute | solution.py:425
  72.6 1.5 %collective-permute-start.13 = (bf16[256,256]{1,0:T(8,128)(2,1)S(1)}, bf16[256,256]{1,0:T(8,128)(2,1)S(1)}, u32[]{:S(2)}, u32[]{:S(2)}) collective-permute-start(bf16[256,256]{1,0:T(8,128)(2,1)S(1)} %get-tuple-element.30.refs_0_.gq_ref), channel_id=1, source_target_pairs={{0,32},{16,48},{32,0},{48,16},{64,96},{80,112},{96,64},{112,80},{1... | collective-permute-start | bytes 393224 | tf_op jit(solution)/shard_map/ppermute | solution.py:420
  74.1 0.8 collective-permute-done.10.rest_2_
  74.9 1.6 %collective-permute-done.9.rest_1_ = f32[4,8,256]{2,1,0:T(8,128)S(1)} collective-permute-done((f32[4,8,256]{2,1,0:T(8,128)S(1)}, f32[4,8,256]{2,1,0:T(8,128)S(1)}, u32[]{:S(2)}, u32[]{:S(2)}) %collective-permute-start.9) | collective-permute-done | bytes 32800 | tf_op jit(solution)/shard_map/ppermute | solution.py:425
  76.6 1.6 %copy-done.1 = bf16[4096,256]{1,0:T(8,128)(2,1)S(1)} copy-done((bf16[4096,256]{1,0:T(8,128)(2,1)S(1)}, bf16[4096,256]{1,0:T(8,128)(2,1)}, u32[]{:S(2)}) %copy-start.1) | copy-done | bytes 2097176
  78.2 1.6 %copy-done.2 = bf16[4096,256]{1,0:T(8,128)(2,1)S(1)} copy-done((bf16[4096,256]{1,0:T(8,128)(2,1)S(1)}, bf16[4096,256]{1,0:T(8,128)(2,1)}, u32[]{:S(2)}) %copy-start.2) | copy-done | bytes 2097176
  79.7 3.2 %settle.1 = (bf16[256,256]{1,0:T(8,128)(2,1)}, bf16[256,256]{1,0:T(8,128)(2,1)}, bf16[256,512]{1,0:T(8,128)(2,1)S(1)}) custom-call(s32[16]{0:T(128)S(1)} %bitcast.17, s32[16]{0:T(128)S(1)} %bitcast.20, bf16[256,1024]{1,0:T(8,128)(2,1)} %get-tuple-element.22.qkv_ref, bf16[16,2,16,512]{3,2,1,0:T(8,128)(2,1)S(1)} %all-to-all-done.1.qdo_ref, ...), custom_call_target="tpu_custom_call" | custom-call | flops 402653184 | bytes 2097152 | tf_op jit(solution)/shard_map/settle/pallas_call | solution.py:292
  82.9 0.8 collective-permute-start.17
  83.7 0.9 collective-permute-start.16
  84.7 1.2 collective-permute-start.15
  85.8 1.8 %xgrad.1 = bf16[4,2,512,256]{3,2,1,0:T(8,128)(2,1)S(1)} custom-call(bf16[4096,256]{1,0:T(8,128)(2,1)S(1)} %copy-done, bf16[4096,256]{1,0:T(8,128)(2,1)S(1)} %copy-done.1, bf16[4096,256]{1,0:T(8,128)(2,1)S(1)} %copy-done.2, bf16[256,256]{1,0:T(8,128)(2,1)S(1)} %get-tuple-element.30.refs_0_.gq_ref, bf16[256,512]{1,0:T(8,128)(2,1)S(1)} %get-tuple-element.31.refs_4_.gkv_ref, ...), custom_call_target="tpu_custom_call" | custom-call | flops 1610612736 | bytes 8912896 | tf_op jit(solution)/shard_map/xgrad/pallas_call | solution.py:385
  87.7 1.4 %copy-done.3 = bf16[4,2,512,256]{3,2,1,0:T(8,128)(2,1)} copy-done((bf16[4,2,512,256]{3,2,1,0:T(8,128)(2,1)}, bf16[4,2,512,256]{3,2,1,0:T(8,128)(2,1)S(1)}, u32[]{:S(2)}) %copy-start.3) | copy-done | bytes 2097176
  89.0 5.3 %all-to-all-start.3 = ((bf16[4,2,512,256]{3,2,1,0:T(8,128)(2,1)}), bf16[4,2,512,256]{3,2,1,0:T(8,128)(2,1)}, u32[]{:S(2)}, u32[]{:S(2)}) async-start(bf16[4,2,512,256]{3,2,1,0:T(8,128)(2,1)} %copy-done.3), calls=%async_computation.3 | async-start | bytes 4194304 | tf_op jit(solution)/shard_map/all_to_all | solution.py:477
  94.5 2.0 %wgrad.3 = bf16[4,128,768]{2,1,0:T(8,128)(2,1)S(1)} custom-call(bf16[4,256,1024]{2,1,0:T(8,128)(2,1)S(1)} %copy-done.5, bf16[256,256]{1,0:T(8,128)(2,1)S(1)} %get-tuple-element.30.refs_0_.gq_ref, bf16[256,256]{1,0:T(8,128)(2,1)S(1)} %collective-permute-done.12.refs_1_.rest_0_, bf16[256,256]{1,0:T(8,128)(2,1)S(1)} %collective-permute-done.13.refs_2_.rest_2_, ...), custom_call_target="tpu_custom_call" | custom-call | flops 2415919104 | bytes 4456448 | tf_op jit(solution)/shard_map/wgrad/pallas_call | solution.py:331
  96.7 2.0 %wgrad.2.keep_ref = bf16[4,128,768]{2,1,0:T(8,128)(2,1)S(1)} custom-call(bf16[4,256,1024]{2,1,0:T(8,128)(2,1)S(1)} %copy-done.5, bf16[256,256]{1,0:T(8,128)(2,1)S(1)} %get-tuple-element.30.refs_0_.gq_ref, bf16[256,256]{1,0:T(8,128)(2,1)S(1)} %collective-permute-done.12.refs_1_.rest_0_, bf16[256,256]{1,0:T(8,128)(2,1)S(1)} %collective-permute-done.13.refs_2_.rest_2_, ...), custom_call_target="tpu_custom_call" | custom-call | flops 2415919104 | bytes 4456448 | tf_op jit(solution)/shard_map/wgrad/pallas_call | solution.py:331
  99.1 2.0 %collective-permute-start.19 = (bf16[128,768]{1,0:T(8,128)(2,1)S(1)}, bf16[128,768]{1,0:T(8,128)(2,1)S(1)}, u32[]{:S(2)}, u32[]{:S(2)}) collective-permute-start(bf16[128,768]{1,0:T(8,128)(2,1)S(1)} %get-tuple-element.33), channel_id=1, source_target_pairs={{0,64},{16,80},{32,96},{48,112},{64,128},{80,144},{96,160},{112,17... | collective-permute-start | bytes 589832 | tf_op jit(solution)/shard_map/ppermute | solution.py:425
  101.1 1.6 %collective-permute-start.20 = (bf16[128,768]{1,0:T(8,128)(2,1)S(1)}, bf16[128,768]{1,0:T(8,128)(2,1)S(1)}, u32[]{:S(2)}, u32[]{:S(2)}) collective-permute-start(bf16[128,768]{1,0:T(8,128)(2,1)S(1)} %get-tuple-element.34), channel_id=1, source_target_pairs={{0,128},{16,144},{32,160},{48,176},{64,192},{80,208},{96,224},{112... | collective-permute-start | bytes 589832 | tf_op jit(solution)/shard_map/ppermute | solution.py:425
  102.7 1.1 collective-permute-start.21
  103.7 9.8 %all-to-all-done.3.terms_ref = bf16[4,2,512,256]{3,2,1,0:T(8,128)(2,1)} async-done(((bf16[4,2,512,256]{3,2,1,0:T(8,128)(2,1)}), bf16[4,2,512,256]{3,2,1,0:T(8,128)(2,1)}, u32[]{:S(2)}, u32[]{:S(2)}) %all-to-all-start.3) | async-done | bytes 2097184 | tf_op jit(solution)/shard_map/all_to_all | solution.py:477
  113.5 1.8 %join.1 = (f32[512,256]{1,0:T(8,128)S(1)}, bf16[512,256]{1,0:T(8,128)(2,1)S(1)}) custom-call(bf16[4,2,512,256]{3,2,1,0:T(8,128)(2,1)} %all-to-all-done.3.terms_ref), custom_call_target="tpu_custom_call" | custom-call | flops 4000000000 | bytes 2097152 | tf_op jit(solution)/shard_map/join/pallas_call | solution.py:407
  115.4 5.4 %collective-permute-start.22 = (bf16[512,256]{1,0:T(8,128)(2,1)S(1)}, bf16[512,256]{1,0:T(8,128)(2,1)S(1)}, u32[]{:S(2)}, u32[]{:S(2)}) collective-permute-start(bf16[512,256]{1,0:T(8,128)(2,1)S(1)} %get-tuple-element.37), channel_id=1, source_target_pairs={{0,8},{2,10},{4,12},{6,14},{8,0},{10,2},{12,4},{14,6},{1,9},{3,11}... | collective-permute-start | bytes 786440 | tf_op jit(solution)/shard_map/ppermute | solution.py:435
  120.8 2.3 %collective-permute-done.21 = bf16[128,768]{1,0:T(8,128)(2,1)} collective-permute-done((bf16[128,768]{1,0:T(8,128)(2,1)S(1)}, bf16[128,768]{1,0:T(8,128)(2,1)}, u32[]{:S(2)}, u32[]{:S(2)}) %collective-permute-start.21) | collective-permute-done | bytes 196640 | tf_op jit(solution)/shard_map/ppermute | solution.py:425
  123.1 1.0 convert_add_fusion
  124.1 0.8 fusion.1
  124.8 9.6 %collective-permute-done.22 = bf16[512,256]{1,0:T(8,128)(2,1)S(1)} collective-permute-done((bf16[512,256]{1,0:T(8,128)(2,1)S(1)}, bf16[512,256]{1,0:T(8,128)(2,1)S(1)}, u32[]{:S(2)}, u32[]{:S(2)}) %collective-permute-start.22) | collective-permute-done | bytes 262176 | tf_op jit(solution)/shard_map/ppermute | solution.py:435
  134.4 0.8 fusion
  (40 shorter events, 2.4 us)
Async XLA Ops:
  0.6 0.9 copy-start.6
  7.0 11.4 %collective-permute-start = (bf16[64,1024]{1,0:T(8,128)(2,1)S(1)}, bf16[64,1024]{1,0:T(8,128)(2,1)S(1)}, u32[]{:S(2)}, u32[]{:S(2)}) collective-permute-start(bf16[64,1024]{1,0:T(8,128)(2,1)S(1)} %get-tuple-element.24), channel_id=1, source_target_pairs={{0,16},{16,32},{32,48},{48,0},{64,80},{80,96},{96,112},{112,64},{1... | collective-permute-start | bytes 393224 | tf_op jit(solution)/shard_map/ppermute | solution.py:420
  8.6 9.8 %collective-permute-start.1 = (bf16[64,1024]{1,0:T(8,128)(2,1)S(1)}, bf16[64,1024]{1,0:T(8,128)(2,1)S(1)}, u32[]{:S(2)}, u32[]{:S(2)}) collective-permute-start(bf16[64,1024]{1,0:T(8,128)(2,1)S(1)} %get-tuple-element.25), channel_id=1, source_target_pairs={{0,32},{16,48},{32,0},{48,16},{64,96},{80,112},{96,64},{112,80},{1... | collective-permute-start | bytes 393224 | tf_op jit(solution)/shard_map/ppermute | solution.py:420
  11.3 7.1 %collective-permute-start.2 = (bf16[64,1024]{1,0:T(8,128)(2,1)S(1)}, bf16[64,1024]{1,0:T(8,128)(2,1)S(1)}, u32[]{:S(2)}, u32[]{:S(2)}) collective-permute-start(bf16[64,1024]{1,0:T(8,128)(2,1)S(1)} %get-tuple-element.26), channel_id=1, source_target_pairs={{0,48},{16,0},{32,16},{48,32},{64,112},{80,64},{96,80},{112,96},{1... | collective-permute-start | bytes 393224 | tf_op jit(solution)/shard_map/ppermute | solution.py:420
  12.7 19.3 %all-to-all-start = ((bf16[16,16,1024]{2,1,0:T(8,128)(2,1)}), bf16[16,16,1024]{2,1,0:T(8,128)(2,1)S(1)}, u32[]{:S(2)}, u32[]{:S(2)}) async-start(bf16[16,16,1024]{2,1,0:T(8,128)(2,1)} %bitcast.4), calls=%async_computation | async-start | bytes 1048576 | tf_op jit(solution)/shard_map/all_to_all | solution.py:457
  18.3 13.7 %copy-start.7 = (s32[1,16]{1,0:T(1,128)S(1)}, s32[1,16]{1,0:T(1,128)}, u32[]{:S(2)}) copy-start(s32[1,16]{1,0:T(1,128)} %param.12) | copy-start | bytes 196
  18.3 13.7 %copy-start.8 = (s32[1,16]{1,0:T(1,128)S(1)}, s32[1,16]{1,0:T(1,128)}, u32[]{:S(2)}) copy-start(s32[1,16]{1,0:T(1,128)} %param.13) | copy-start | bytes 196
  18.4 20.5 %collective-permute-start.5 = (bf16[3,64,1024]{2,1,0:T(8,128)(2,1)S(1)}, bf16[3,64,1024]{2,1,0:T(8,128)(2,1)S(1)}, u32[]{:S(2)}, u32[]{:S(2)}) collective-permute-start(bf16[3,64,1024]{2,1,0:T(8,128)(2,1)S(1)} %stack.21.refs_0_.rest_0_), channel_id=1, source_target_pairs={{0,6},{2,0},{4,2},{6,4},{8,14},{10,8},{12,10},{14,12},{1,7},{3,1},... | collective-permute-start | bytes 1179656 | tf_op jit(solution)/shard_map/ppermute | solution.py:430
  18.9 20.0 %collective-permute-start.4 = (bf16[3,64,1024]{2,1,0:T(8,128)(2,1)S(1)}, bf16[3,64,1024]{2,1,0:T(8,128)(2,1)S(1)}, u32[]{:S(2)}, u32[]{:S(2)}) collective-permute-start(bf16[3,64,1024]{2,1,0:T(8,128)(2,1)S(1)} %stack.21.refs_0_.rest_0_), channel_id=1, source_target_pairs={{0,4},{2,6},{4,0},{6,2},{8,12},{10,14},{12,8},{14,10},{1,5},{3,7},... | collective-permute-start | bytes 1179656 | tf_op jit(solution)/shard_map/ppermute | solution.py:430
  21.5 17.4 %collective-permute-start.3 = (bf16[3,64,1024]{2,1,0:T(8,128)(2,1)S(1)}, bf16[3,64,1024]{2,1,0:T(8,128)(2,1)}, u32[]{:S(2)}, u32[]{:S(2)}) collective-permute-start(bf16[3,64,1024]{2,1,0:T(8,128)(2,1)S(1)} %stack.21.refs_0_.rest_0_), channel_id=1, source_target_pairs={{0,2},{2,4},{4,6},{6,0},{8,10},{10,12},{12,14},{14,8},{1,3},{3,5},... | collective-permute-start | bytes 1179656 | tf_op jit(solution)/shard_map/ppermute | solution.py:430
  33.5 18.7 %all-to-all-start.2 = ((bf16[16,2,16,512]{3,2,1,0:T(8,128)(2,1)}), bf16[16,2,16,512]{3,2,1,0:T(8,128)(2,1)S(1)}, u32[]{:S(2)}, u32[]{:S(2)}) async-start(bf16[16,2,16,512]{3,2,1,0:T(8,128)(2,1)} %pick.3), calls=%async_computation.2 | async-start | bytes 1048576 | tf_op jit(solution)/shard_map/all_to_all | solution.py:457
  40.1 36.5 %copy-start = (bf16[4096,256]{1,0:T(8,128)(2,1)S(1)}, bf16[4096,256]{1,0:T(8,128)(2,1)}, u32[]{:S(2)}) copy-start(bf16[4096,256]{1,0:T(8,128)(2,1)} %wq_ref.3) | copy-start | bytes 6291460
  41.5 1.4 copy-start.4
  52.2 21.9 %all-to-all-start.1 = ((bf16[16,2,16,512]{3,2,1,0:T(8,128)(2,1)}), bf16[16,2,16,512]{3,2,1,0:T(8,128)(2,1)S(1)}, u32[]{:S(2)}, u32[]{:S(2)}) async-start(bf16[16,2,16,512]{3,2,1,0:T(8,128)(2,1)} %pick.2), calls=%async_computation.1 | async-start | bytes 1048576 | tf_op jit(solution)/shard_map/all_to_all | solution.py:457
  60.3 6.8 %collective-permute-start.8 = (f32[8,256]{1,0:T(8,128)S(1)}, f32[8,256]{1,0:T(8,128)S(1)}, u32[]{:S(2)}, u32[]{:S(2)}) collective-permute-start(f32[8,256]{1,0:T(8,128)S(1)} %get-tuple-element.27), channel_id=1, source_target_pairs={{0,48},{16,0},{32,16},{48,32},{64,112},{80,64},{96,80},{112,96},{1... | collective-permute-start | bytes 24584 | tf_op jit(solution)/shard_map/ppermute | solution.py:420
  63.1 5.2 %collective-permute-start.7 = (f32[8,256]{1,0:T(8,128)S(1)}, f32[8,256]{1,0:T(8,128)S(1)}, u32[]{:S(2)}, u32[]{:S(2)}) collective-permute-start(f32[8,256]{1,0:T(8,128)S(1)} %get-tuple-element.27), channel_id=1, source_target_pairs={{0,32},{16,48},{32,0},{48,16},{64,96},{80,112},{96,64},{112,80},{1... | collective-permute-start | bytes 24584 | tf_op jit(solution)/shard_map/ppermute | solution.py:420
  63.9 4.9 %collective-permute-start.6 = (f32[8,256]{1,0:T(8,128)S(1)}, f32[8,256]{1,0:T(8,128)S(1)}, u32[]{:S(2)}, u32[]{:S(2)}) collective-permute-start(f32[8,256]{1,0:T(8,128)S(1)} %get-tuple-element.27), channel_id=1, source_target_pairs={{0,16},{16,32},{32,48},{48,0},{64,80},{80,96},{96,112},{112,64},{1... | collective-permute-start | bytes 24584 | tf_op jit(solution)/shard_map/ppermute | solution.py:420
  64.8 19.8 %collective-permute-start.14 = (bf16[256,256]{1,0:T(8,128)(2,1)S(1)}, bf16[256,256]{1,0:T(8,128)(2,1)S(1)}, u32[]{:S(2)}, u32[]{:S(2)}) collective-permute-start(bf16[256,256]{1,0:T(8,128)(2,1)S(1)} %get-tuple-element.30.refs_0_.gq_ref), channel_id=1, source_target_pairs={{0,48},{16,0},{32,16},{48,32},{64,112},{80,64},{96,80},{112,96},{1... | collective-permute-start | bytes 393224 | tf_op jit(solution)/shard_map/ppermute | solution.py:420
  68.8 5.3 %collective-permute-start.11 = (f32[4,8,256]{2,1,0:T(8,128)S(1)}, f32[4,8,256]{2,1,0:T(8,128)S(1)}, u32[]{:S(2)}, u32[]{:S(2)}) collective-permute-start(f32[4,8,256]{2,1,0:T(8,128)S(1)} %pad_maximum_fusion.rest_0_), channel_id=1, source_target_pairs={{0,192},{16,208},{32,224},{48,240},{64,0},{80,16},{96,32},{112,48}... | collective-permute-start | bytes 98312 | tf_op jit(solution)/shard_map/ppermute | solution.py:425
  69.4 5.5 %collective-permute-start.10 = (f32[4,8,256]{2,1,0:T(8,128)S(1)}, f32[4,8,256]{2,1,0:T(8,128)S(1)}, u32[]{:S(2)}, u32[]{:S(2)}) collective-permute-start(f32[4,8,256]{2,1,0:T(8,128)S(1)} %pad_maximum_fusion.rest_0_), channel_id=1, source_target_pairs={{0,128},{16,144},{32,160},{48,176},{64,192},{80,208},{96,224},{112... | collective-permute-start | bytes 98312 | tf_op jit(solution)/shard_map/ppermute | solution.py:425
  72.6 3.9 %collective-permute-start.9 = (f32[4,8,256]{2,1,0:T(8,128)S(1)}, f32[4,8,256]{2,1,0:T(8,128)S(1)}, u32[]{:S(2)}, u32[]{:S(2)}) collective-permute-start(f32[4,8,256]{2,1,0:T(8,128)S(1)} %pad_maximum_fusion.rest_0_), channel_id=1, source_target_pairs={{0,64},{16,80},{32,96},{48,112},{64,128},{80,144},{96,160},{112,17... | collective-permute-start | bytes 98312 | tf_op jit(solution)/shard_map/ppermute | solution.py:425
  72.6 13.2 %collective-permute-start.13 = (bf16[256,256]{1,0:T(8,128)(2,1)S(1)}, bf16[256,256]{1,0:T(8,128)(2,1)S(1)}, u32[]{:S(2)}, u32[]{:S(2)}) collective-permute-start(bf16[256,256]{1,0:T(8,128)(2,1)S(1)} %get-tuple-element.30.refs_0_.gq_ref), channel_id=1, source_target_pairs={{0,32},{16,48},{32,0},{48,16},{64,96},{80,112},{96,64},{112,80},{1... | collective-permute-start | bytes 393224 | tf_op jit(solution)/shard_map/ppermute | solution.py:420
  74.1 11.7 %collective-permute-start.12 = (bf16[256,256]{1,0:T(8,128)(2,1)S(1)}, bf16[256,256]{1,0:T(8,128)(2,1)S(1)}, u32[]{:S(2)}, u32[]{:S(2)}) collective-permute-start(bf16[256,256]{1,0:T(8,128)(2,1)S(1)} %get-tuple-element.30.refs_0_.gq_ref), channel_id=1, source_target_pairs={{0,16},{16,32},{32,48},{48,0},{64,80},{80,96},{96,112},{112,64},{1... | collective-permute-start | bytes 393224 | tf_op jit(solution)/shard_map/ppermute | solution.py:420
  76.6 1.6 %copy-start.1 = (bf16[4096,256]{1,0:T(8,128)(2,1)S(1)}, bf16[4096,256]{1,0:T(8,128)(2,1)}, u32[]{:S(2)}) copy-start(bf16[4096,256]{1,0:T(8,128)(2,1)} %wk_ref.3) | copy-start | bytes 6291460
  78.2 1.6 %copy-start.2 = (bf16[4096,256]{1,0:T(8,128)(2,1)S(1)}, bf16[4096,256]{1,0:T(8,128)(2,1)}, u32[]{:S(2)}) copy-start(bf16[4096,256]{1,0:T(8,128)(2,1)} %wv_ref.3) | copy-start | bytes 6291460
  82.9 11.4 %collective-permute-start.17 = (bf16[256,512]{1,0:T(8,128)(2,1)S(1)}, bf16[256,512]{1,0:T(8,128)(2,1)S(1)}, u32[]{:S(2)}, u32[]{:S(2)}) collective-permute-start(bf16[256,512]{1,0:T(8,128)(2,1)S(1)} %get-tuple-element.31.refs_4_.gkv_ref), channel_id=1, source_target_pairs={{0,48},{16,0},{32,16},{48,32},{64,112},{80,64},{96,80},{112,96},{1... | collective-permute-start | bytes 786440 | tf_op jit(solution)/shard_map/ppermute | solution.py:420
  83.7 10.6 %collective-permute-start.16 = (bf16[256,512]{1,0:T(8,128)(2,1)S(1)}, bf16[256,512]{1,0:T(8,128)(2,1)S(1)}, u32[]{:S(2)}, u32[]{:S(2)}) collective-permute-start(bf16[256,512]{1,0:T(8,128)(2,1)S(1)} %get-tuple-element.31.refs_4_.gkv_ref), channel_id=1, source_target_pairs={{0,32},{16,48},{32,0},{48,16},{64,96},{80,112},{96,64},{112,80},{1... | collective-permute-start | bytes 786440 | tf_op jit(solution)/shard_map/ppermute | solution.py:420
  84.7 9.9 %collective-permute-start.15 = (bf16[256,512]{1,0:T(8,128)(2,1)S(1)}, bf16[256,512]{1,0:T(8,128)(2,1)}, u32[]{:S(2)}, u32[]{:S(2)}) collective-permute-start(bf16[256,512]{1,0:T(8,128)(2,1)S(1)} %get-tuple-element.31.refs_4_.gkv_ref), channel_id=1, source_target_pairs={{0,16},{16,32},{32,48},{48,0},{64,80},{80,96},{96,112},{112,64},{1... | collective-permute-start | bytes 786440 | tf_op jit(solution)/shard_map/ppermute | solution.py:420
  87.7 1.4 %copy-start.3 = (bf16[4,2,512,256]{3,2,1,0:T(8,128)(2,1)}, bf16[4,2,512,256]{3,2,1,0:T(8,128)(2,1)S(1)}, u32[]{:S(2)}) copy-start(bf16[4,2,512,256]{3,2,1,0:T(8,128)(2,1)S(1)} %xgrad.1) | copy-start | bytes 6291460
  89.0 5.5 %copy-start.5 = (bf16[4,256,1024]{2,1,0:T(8,128)(2,1)S(1)}, bf16[4,256,1024]{2,1,0:T(8,128)(2,1)}, u32[]{:S(2)}) copy-start(bf16[4,256,1024]{2,1,0:T(8,128)(2,1)} %copy-done.4) | copy-start | bytes 6291460
  89.0 24.5 %all-to-all-start.3 = ((bf16[4,2,512,256]{3,2,1,0:T(8,128)(2,1)}), bf16[4,2,512,256]{3,2,1,0:T(8,128)(2,1)}, u32[]{:S(2)}, u32[]{:S(2)}) async-start(bf16[4,2,512,256]{3,2,1,0:T(8,128)(2,1)} %copy-done.3), calls=%async_computation.3 | async-start | bytes 4194304 | tf_op jit(solution)/shard_map/all_to_all | solution.py:477
  96.6 2.4 %collective-permute-start.18 = (bf16[4,128,768]{2,1,0:T(8,128)(2,1)S(1)}, bf16[4,128,768]{2,1,0:T(8,128)(2,1)S(1)}, u32[]{:S(2)}, u32[]{:S(2)}) collective-permute-start(bf16[4,128,768]{2,1,0:T(8,128)(2,1)S(1)} %wgrad.3), channel_id=1, source_target_pairs={{0,1},{1,0},{2,3},{3,2},{4,5},{5,4},{6,7},{7,6},{8,9},{9,8},{10,11... | collective-permute-start | bytes 2359304 | tf_op jit(solution)/shard_map/ppermute | solution.py:439
  99.1 21.6 %collective-permute-start.19 = (bf16[128,768]{1,0:T(8,128)(2,1)S(1)}, bf16[128,768]{1,0:T(8,128)(2,1)S(1)}, u32[]{:S(2)}, u32[]{:S(2)}) collective-permute-start(bf16[128,768]{1,0:T(8,128)(2,1)S(1)} %get-tuple-element.33), channel_id=1, source_target_pairs={{0,64},{16,80},{32,96},{48,112},{64,128},{80,144},{96,160},{112,17... | collective-permute-start | bytes 589832 | tf_op jit(solution)/shard_map/ppermute | solution.py:425
  101.1 19.7 %collective-permute-start.20 = (bf16[128,768]{1,0:T(8,128)(2,1)S(1)}, bf16[128,768]{1,0:T(8,128)(2,1)S(1)}, u32[]{:S(2)}, u32[]{:S(2)}) collective-permute-start(bf16[128,768]{1,0:T(8,128)(2,1)S(1)} %get-tuple-element.34), channel_id=1, source_target_pairs={{0,128},{16,144},{32,160},{48,176},{64,192},{80,208},{96,224},{112... | collective-permute-start | bytes 589832 | tf_op jit(solution)/shard_map/ppermute | solution.py:425
  102.7 20.4 %collective-permute-start.21 = (bf16[128,768]{1,0:T(8,128)(2,1)S(1)}, bf16[128,768]{1,0:T(8,128)(2,1)}, u32[]{:S(2)}, u32[]{:S(2)}) collective-permute-start(bf16[128,768]{1,0:T(8,128)(2,1)S(1)} %get-tuple-element.35), channel_id=1, source_target_pairs={{0,192},{16,208},{32,224},{48,240},{64,0},{80,16},{96,32},{112,48}... | collective-permute-start | bytes 589832 | tf_op jit(solution)/shard_map/ppermute | solution.py:425
  115.4 19.1 %collective-permute-start.22 = (bf16[512,256]{1,0:T(8,128)(2,1)S(1)}, bf16[512,256]{1,0:T(8,128)(2,1)S(1)}, u32[]{:S(2)}, u32[]{:S(2)}) collective-permute-start(bf16[512,256]{1,0:T(8,128)(2,1)S(1)} %get-tuple-element.37), channel_id=1, source_target_pairs={{0,8},{2,10},{4,12},{6,14},{8,0},{10,2},{12,4},{14,6},{1,9},{3,11}... | collective-permute-start | bytes 786440 | tf_op jit(solution)/shard_map/ppermute | solution.py:435

commit v5 on v4

--- a/solution.py
+++ b/solution.py
@@ -415,6 +415,29 @@
     )(terms)
 
 
+def _finish_body(own_ref, a_ref, b_ref, c_ref, *outs):
+    n = outs[0].shape[1]
+    for i in range(3):
+        cols = slice(i * n, (i + 1) * n)
+        total = own_ref[:, cols]
+        for r in (a_ref, b_ref, c_ref):
+            total = total + r[:, cols].astype(F32)
+        outs[i][...] = total
+
+
+def finish(own, pieces):
+    rows, n = own.shape
+    return pl.pallas_call(
+        _finish_body,
+        in_specs=[VMEM] * 4,
+        out_specs=[VMEM] * 3,
+        out_shape=[jax.ShapeDtypeStruct((rows, n // 3), F32)] * 3,
+        compiler_params=_params(SMALL),
+        cost_estimate=_cost(4 * HINT // 30, 16 * own.size),
+        name="finish",
+    )(own, *pieces)
+
+
 def shift_x(v, k):
     pairs = [(z * XS + x, z * XS + (x + k) % XS) for z in range(ZS) for x in range(XS)]
     return lax.ppermute(v, "doc", pairs)
@@ -469,7 +492,7 @@
     row = jnp.stack([shift_x(stats, k) if k else stats for k in range(XS)])
     all_stats = [shift_z(row, k) if k else row for k in range(ZS)]
     gq_x = {0: gq, **{k: shift_x(gq, k) for k in ORDER}}
-    gk, gv, gkv = settle(factor, p1, p2, qkvd, qdo, all_stats, weights)
+    gk, gv, gkv = settle(factor, p1, p2, qkvd, qdo, all_stats, [])
     gkv_x = {0: gkv, **{k: shift_x(gkv, k) for k in ORDER}}
 
     terms = xgrad(*weights, gq, gkv, [gq_x[k] for k in ORDER])
@@ -481,16 +504,15 @@
     theirs = wgrad(True, *operands)
     mine = wgrad(False, *operands)
     total, *pieces = pair(mine, swap_cores(theirs))
-    for k in range(1, ZS):
-        total = total + shift_z(pieces[k - 1], k).astype(F32)
+    gwq, gwk, gwv = finish(total, [shift_z(pieces[k - 1], k) for k in range(1, ZS)])
     keep, send = join(terms)
     features = (keep + swap_halves(send).astype(F32)).astype(BF)
     return (
         gk.reshape(1, 1, t, n),
         gv.reshape(1, 1, t, n),
-        total[:, :n],
-        total[:, n : 2 * n],
-        total[:, 2 * n :],
+        gwq,
+        gwk,
+        gwv,
         features.reshape(1, 1, features.shape[0], t),
     )
 

time: 137 us -> 138 us (level)
  waiting for transfers between devices: 44.3 us -> 49 us
  local copies, waits for them, and re-layouts: 7.57 us -> 5.45 us
    ppermute x1, waiting for transfers between devices: 9.62 us -> 13 us  [swap_halves(): return lax.ppermute(v, 'head', pairs)]
    pallas_call x1, Pallas kernels: 1.82 us -> 3.21 us  [xgrad(): pl.pallas_call(_xgrad_body, in_specs=[VMEM] * (5 + len(after)), out_specs...]
    unnamed x18 -> x16, local copies, waits for them, and re-layouts: 6.82 us -> 5.45 us
  transfers between devices with their start and end apart: 27 -> 27, of which waited for: 11 -> 11; matrix products, arithmetic and copies ran while one was open for 1% -> 0% of each run, Pallas kernels for 13% -> 14%
where the time goes in v5:
time: 138 us; the launch traced here: 137 us
  starting transfers between devices  56.6 us (41%)
  waiting for transfers between devices  49 us (36%)
  Pallas kernels  24.5 us (18%)
  local copies, waits for them, and re-layouts  5.45 us (4%)
    all_to_all x3, waiting for transfers between devices, spread(): return lax.all_to_all(v, 'doc', split_axis=0, concat_axis=0, tiled=True)  19 us
    ppermute x12, starting transfers between devices, shift_x(): return lax.ppermute(v, 'doc', pairs)  16.9 us
    all_to_all x3, starting transfers between devices, spread(): return lax.all_to_all(v, 'doc', split_axis=0, concat_axis=0, tiled=True)  16.3 us
    ppermute x1, waiting for transfers between devices, swap_halves(): return lax.ppermute(v, 'head', pairs)  13 us
    all_to_all x1, waiting for transfers between devices, per_device(): lax.all_to_all(terms, 'head', split_axis=0, concat_axis=0, tiled=True, ax...  9.33 us
    ppermute x6, starting transfers between devices, shift_z(): return lax.ppermute(v, 'doc', pairs)  7.78 us
    unnamed x16, local copies, waits for them, and re-layouts  5.45 us
    pallas_call x1, Pallas kernels, project(): pl.pallas_call(_project_body, in_specs=[ANY] * 5, out_specs=[VMEM] * (1 +...  5.45 us
  transfers between devices with their start and end apart: 27, of which 11 were waited for; matrix products, arithmetic and copies ran while one was open for 0% of the time, Pallas kernels for 14%

profile of v5, /device:TPU:72, one launch (start us, length us, event | category | flops | bytes accessed | tf_op | source)
XLA Modules:
  0.0 137.2 jit_solution(504860475894203545)
XLA Ops:
  0.6 0.9 copy-done.5
  1.5 5.5 %project.1 = (bf16[256,1024]{1,0:T(8,128)(2,1)}, bf16[256,1024]{1,0:T(8,128)(2,1)S(1)}, bf16[64,1024]{1,0:T(8,128)(2,1)S(1)}, bf16[64,1024]{1,0:T(8,128)(2,1)S(1)}, bf16[64,1024]{1,0:T(8,128)(2,1)S(1)}) custom-call(bf16[256,4096]{1,0:T(8,128)(2,1)} %bitcast.21, bf16[4096,256]{1,0:T(8,128)(2,1)} %wq_ref.3, bf16[4096,256]{1,0:T(8,128)(2,1)} %wk_ref.3, ...), custom_call_target="tpu_custom_call" | custom-call | flops 1610612736 | bytes 8388608 | tf_op jit(solution)/shard_map/project/pallas_call | solution.py:93
  7.0 1.6 %collective-permute-start = (bf16[64,1024]{1,0:T(8,128)(2,1)S(1)}, bf16[64,1024]{1,0:T(8,128)(2,1)S(1)}, u32[]{:S(2)}, u32[]{:S(2)}) collective-permute-start(bf16[64,1024]{1,0:T(8,128)(2,1)S(1)} %get-tuple-element.27), channel_id=1, source_target_pairs={{0,16},{16,32},{32,48},{48,0},{64,80},{80,96},{96,112},{112,64},{1... | collective-permute-start | bytes 393224 | tf_op jit(solution)/shard_map/ppermute | solution.py:443
  8.6 2.7 %collective-permute-start.1 = (bf16[64,1024]{1,0:T(8,128)(2,1)S(1)}, bf16[64,1024]{1,0:T(8,128)(2,1)S(1)}, u32[]{:S(2)}, u32[]{:S(2)}) collective-permute-start(bf16[64,1024]{1,0:T(8,128)(2,1)S(1)} %get-tuple-element.28), channel_id=1, source_target_pairs={{0,32},{16,48},{32,0},{48,16},{64,96},{80,112},{96,64},{112,80},{1... | collective-permute-start | bytes 393224 | tf_op jit(solution)/shard_map/ppermute | solution.py:443
  11.3 1.4 %collective-permute-start.2 = (bf16[64,1024]{1,0:T(8,128)(2,1)S(1)}, bf16[64,1024]{1,0:T(8,128)(2,1)S(1)}, u32[]{:S(2)}, u32[]{:S(2)}) collective-permute-start(bf16[64,1024]{1,0:T(8,128)(2,1)S(1)} %get-tuple-element.29), channel_id=1, source_target_pairs={{0,48},{16,0},{32,16},{48,32},{64,112},{80,64},{96,80},{112,96},{1... | collective-permute-start | bytes 393224 | tf_op jit(solution)/shard_map/ppermute | solution.py:443
  12.7 5.6 %all-to-all-start = ((bf16[16,16,1024]{2,1,0:T(8,128)(2,1)}), bf16[16,16,1024]{2,1,0:T(8,128)(2,1)S(1)}, u32[]{:S(2)}, u32[]{:S(2)}) async-start(bf16[16,16,1024]{2,1,0:T(8,128)(2,1)} %bitcast.4), calls=%async_computation | async-start | bytes 1048576 | tf_op jit(solution)/shard_map/all_to_all | solution.py:480
  18.4 0.5 collective-permute-start.5
  18.9 2.6 %collective-permute-start.4 = (bf16[3,64,1024]{2,1,0:T(8,128)(2,1)S(1)}, bf16[3,64,1024]{2,1,0:T(8,128)(2,1)S(1)}, u32[]{:S(2)}, u32[]{:S(2)}) collective-permute-start(bf16[3,64,1024]{2,1,0:T(8,128)(2,1)S(1)} %stack.21.refs_0_.rest_0_), channel_id=1, source_target_pairs={{0,4},{2,6},{4,0},{6,2},{8,12},{10,14},{12,8},{14,10},{1,5},{3,7},... | collective-permute-start | bytes 1179656 | tf_op jit(solution)/shard_map/ppermute | solution.py:453
  21.5 1.9 %collective-permute-start.3 = (bf16[3,64,1024]{2,1,0:T(8,128)(2,1)S(1)}, bf16[3,64,1024]{2,1,0:T(8,128)(2,1)S(1)}, u32[]{:S(2)}, u32[]{:S(2)}) collective-permute-start(bf16[3,64,1024]{2,1,0:T(8,128)(2,1)S(1)} %stack.21.refs_0_.rest_0_), channel_id=1, source_target_pairs={{0,2},{2,4},{4,6},{6,0},{8,10},{10,12},{12,14},{14,8},{1,3},{3,5},... | collective-permute-start | bytes 1179656 | tf_op jit(solution)/shard_map/ppermute | solution.py:453
  23.4 8.6 %all-to-all-done.all_ref = bf16[16,16,1024]{2,1,0:T(8,128)(2,1)S(1)} async-done(((bf16[16,16,1024]{2,1,0:T(8,128)(2,1)}), bf16[16,16,1024]{2,1,0:T(8,128)(2,1)S(1)}, u32[]{:S(2)}, u32[]{:S(2)}) %all-to-all-start) | async-done | bytes 524320 | tf_op jit(solution)/shard_map/all_to_all | solution.py:480
  32.1 1.5 %pick.3 = bf16[16,2,16,512]{3,2,1,0:T(8,128)(2,1)} custom-call(s32[16]{0:T(128)S(1)} %bitcast.15, s32[16]{0:T(128)S(1)} %bitcast.18, bf16[16,16,1024]{2,1,0:T(8,128)(2,1)S(1)} %all-to-all-done.all_ref, bf16[3,64,1024]{2,1,0:T(8,128)(2,1)S(1)} %stack.21.refs_0_.rest_0_), custom_call_target="tpu_custom_call" | custom-call | bytes 1048576 | tf_op jit(solution)/shard_map/pick/pallas_call | solution.py:182
  33.5 5.4 %all-to-all-start.2 = ((bf16[16,2,16,512]{3,2,1,0:T(8,128)(2,1)}), bf16[16,2,16,512]{3,2,1,0:T(8,128)(2,1)S(1)}, u32[]{:S(2)}, u32[]{:S(2)}) async-start(bf16[16,2,16,512]{3,2,1,0:T(8,128)(2,1)} %pick.3), calls=%async_computation.2 | async-start | bytes 1048576 | tf_op jit(solution)/shard_map/all_to_all | solution.py:480
  39.1 1.5 %pick.2 = bf16[16,2,16,512]{3,2,1,0:T(8,128)(2,1)} custom-call(s32[16]{0:T(128)S(1)} %bitcast.16, s32[16]{0:T(128)S(1)} %bitcast.19, bf16[16,16,1024]{2,1,0:T(8,128)(2,1)S(1)} %all-to-all-done.all_ref, bf16[4,256,1024]{2,1,0:T(8,128)(2,1)S(1)} %merge.1.rest_0_.x_ref), custom_call_target="tpu_custom_call" | custom-call | bytes 1048576 | tf_op jit(solution)/shard_map/pick/pallas_call | solution.py:182
  40.5 1.4 copy-done.3
  41.9 10.3 %all-to-all-done.2.kv_ref = bf16[16,2,16,512]{3,2,1,0:T(8,128)(2,1)S(1)} async-done(((bf16[16,2,16,512]{3,2,1,0:T(8,128)(2,1)}), bf16[16,2,16,512]{3,2,1,0:T(8,128)(2,1)S(1)}, u32[]{:S(2)}, u32[]{:S(2)}) %all-to-all-start.2) | async-done | bytes 524320 | tf_op jit(solution)/shard_map/all_to_all | solution.py:480
  52.2 5.4 %all-to-all-start.1 = ((bf16[16,2,16,512]{3,2,1,0:T(8,128)(2,1)}), bf16[16,2,16,512]{3,2,1,0:T(8,128)(2,1)S(1)}, u32[]{:S(2)}, u32[]{:S(2)}) async-start(bf16[16,2,16,512]{3,2,1,0:T(8,128)(2,1)} %pick.2), calls=%async_computation.1 | async-start | bytes 1048576 | tf_op jit(solution)/shard_map/all_to_all | solution.py:480
  57.6 2.7 %attend.1 = (bf16[256,256]{1,0:T(8,128)(2,1)S(1)}, f32[8,256]{1,0:T(8,128)S(1)}) custom-call(bf16[256,1024]{1,0:T(8,128)(2,1)} %get-tuple-element.25.qkv_ref, bf16[16,2,16,512]{3,2,1,0:T(8,128)(2,1)S(1)} %all-to-all-done.2.kv_ref), custom_call_target="tpu_custom_call" | custom-call | flops 369098752 | bytes 2621440 | tf_op jit(solution)/shard_map/attend/pallas_call | solution.py:231
  60.3 2.8 %collective-permute-start.8 = (f32[8,256]{1,0:T(8,128)S(1)}, f32[8,256]{1,0:T(8,128)S(1)}, u32[]{:S(2)}, u32[]{:S(2)}) collective-permute-start(f32[8,256]{1,0:T(8,128)S(1)} %get-tuple-element.30), channel_id=1, source_target_pairs={{0,48},{16,0},{32,16},{48,32},{64,112},{80,64},{96,80},{112,96},{1... | collective-permute-start | bytes 24584 | tf_op jit(solution)/shard_map/ppermute | solution.py:443
  63.1 0.9 collective-permute-start.7
  63.9 0.9 collective-permute-start.6
  64.8 2.4 %collective-permute-start.14 = (bf16[256,256]{1,0:T(8,128)(2,1)S(1)}, bf16[256,256]{1,0:T(8,128)(2,1)S(1)}, u32[]{:S(2)}, u32[]{:S(2)}) collective-permute-start(bf16[256,256]{1,0:T(8,128)(2,1)S(1)} %get-tuple-element.33.refs_0_.gq_ref), channel_id=1, source_target_pairs={{0,48},{16,0},{32,16},{48,32},{64,112},{80,64},{96,80},{112,96},{1... | collective-permute-start | bytes 393224 | tf_op jit(solution)/shard_map/ppermute | solution.py:443
  67.2 1.1 collective-permute-done.7
  68.3 0.5 collective-permute-done.6
  68.8 0.5 collective-permute-start.11
  69.4 3.3 %collective-permute-start.10 = (f32[4,8,256]{2,1,0:T(8,128)S(1)}, f32[4,8,256]{2,1,0:T(8,128)S(1)}, u32[]{:S(2)}, u32[]{:S(2)}) collective-permute-start(f32[4,8,256]{2,1,0:T(8,128)S(1)} %pad_maximum_fusion.rest_0_), channel_id=1, source_target_pairs={{0,128},{16,144},{32,160},{48,176},{64,192},{80,208},{96,224},{112... | collective-permute-start | bytes 98312 | tf_op jit(solution)/shard_map/ppermute | solution.py:448
  72.6 1.5 %collective-permute-start.13 = (bf16[256,256]{1,0:T(8,128)(2,1)S(1)}, bf16[256,256]{1,0:T(8,128)(2,1)S(1)}, u32[]{:S(2)}, u32[]{:S(2)}) collective-permute-start(bf16[256,256]{1,0:T(8,128)(2,1)S(1)} %get-tuple-element.33.refs_0_.gq_ref), channel_id=1, source_target_pairs={{0,32},{16,48},{32,0},{48,16},{64,96},{80,112},{96,64},{112,80},{1... | collective-permute-start | bytes 393224 | tf_op jit(solution)/shard_map/ppermute | solution.py:443
  74.1 0.8 collective-permute-done.10.rest_2_
  74.9 1.6 %collective-permute-done.9.rest_1_ = f32[4,8,256]{2,1,0:T(8,128)S(1)} collective-permute-done((f32[4,8,256]{2,1,0:T(8,128)S(1)}, f32[4,8,256]{2,1,0:T(8,128)S(1)}, u32[]{:S(2)}, u32[]{:S(2)}) %collective-permute-start.9) | collective-permute-done | bytes 32800 | tf_op jit(solution)/shard_map/ppermute | solution.py:448
  76.5 3.2 %settle.1 = (bf16[256,256]{1,0:T(8,128)(2,1)}, bf16[256,256]{1,0:T(8,128)(2,1)}, bf16[256,512]{1,0:T(8,128)(2,1)S(1)}) custom-call(s32[16]{0:T(128)S(1)} %bitcast.17, s32[16]{0:T(128)S(1)} %bitcast.20, bf16[256,1024]{1,0:T(8,128)(2,1)} %get-tuple-element.25.qkv_ref, bf16[16,2,16,512]{3,2,1,0:T(8,128)(2,1)S(1)} %all-to-all-done.1.qdo_ref, ...), custom_call_target="tpu_custom_call" | custom-call | flops 402653184 | bytes 2097152 | tf_op jit(solution)/shard_map/settle/pallas_call | solution.py:292
  79.7 0.8 collective-permute-start.17
  80.5 0.9 collective-permute-start.16
  81.4 1.2 collective-permute-start.15
  82.6 1.5 %collective-permute-done.12.refs_1_.rest_0_ = bf16[256,256]{1,0:T(8,128)(2,1)S(1)} collective-permute-done((bf16[256,256]{1,0:T(8,128)(2,1)S(1)}, bf16[256,256]{1,0:T(8,128)(2,1)S(1)}, u32[]{:S(2)}, u32[]{:S(2)}) %collective-permute-start.12) | collective-permute-done | bytes 131104 | tf_op jit(solution)/shard_map/ppermute | solution.py:443
  84.1 1.6 %copy-done.1 = bf16[4096,256]{1,0:T(8,128)(2,1)S(1)} copy-done((bf16[4096,256]{1,0:T(8,128)(2,1)S(1)}, bf16[4096,256]{1,0:T(8,128)(2,1)}, u32[]{:S(2)}) %copy-start.1) | copy-done | bytes 2097176
  85.7 1.6 %copy-done.2 = bf16[4096,256]{1,0:T(8,128)(2,1)S(1)} copy-done((bf16[4096,256]{1,0:T(8,128)(2,1)S(1)}, bf16[4096,256]{1,0:T(8,128)(2,1)}, u32[]{:S(2)}) %copy-start.2) | copy-done | bytes 2097176
  87.3 3.2 %xgrad.1 = bf16[4,2,512,256]{3,2,1,0:T(8,128)(2,1)} custom-call(bf16[4096,256]{1,0:T(8,128)(2,1)S(1)} %copy-done, bf16[4096,256]{1,0:T(8,128)(2,1)S(1)} %copy-done.1, bf16[4096,256]{1,0:T(8,128)(2,1)S(1)} %copy-done.2, bf16[256,256]{1,0:T(8,128)(2,1)S(1)} %get-tuple-element.33.refs_0_.gq_ref, bf16[256,512]{1,0:T(8,128)(2,1)S(1)} %get-tuple-element.34.refs_4_.gkv_ref, ...), custom_call_target="tpu_custom_call" | custom-call | flops 1610612736 | bytes 8912896 | tf_op jit(solution)/shard_map/xgrad/pallas_call | solution.py:385
  90.5 5.1 %all-to-all-start.3 = ((bf16[4,2,512,256]{3,2,1,0:T(8,128)(2,1)}), bf16[4,2,512,256]{3,2,1,0:T(8,128)(2,1)}, u32[]{:S(2)}, u32[]{:S(2)}) async-start(bf16[4,2,512,256]{3,2,1,0:T(8,128)(2,1)} %xgrad.1), calls=%async_computation.3 | async-start | bytes 4194304 | tf_op jit(solution)/shard_map/all_to_all | solution.py:500
  95.6 2.0 %wgrad.3 = bf16[4,128,768]{2,1,0:T(8,128)(2,1)S(1)} custom-call(bf16[4,256,1024]{2,1,0:T(8,128)(2,1)S(1)} %copy-done.4, bf16[256,256]{1,0:T(8,128)(2,1)S(1)} %get-tuple-element.33.refs_0_.gq_ref, bf16[256,256]{1,0:T(8,128)(2,1)S(1)} %collective-permute-done.12.refs_1_.rest_0_, bf16[256,256]{1,0:T(8,128)(2,1)S(1)} %collective-permute-done.13.refs_2_.rest_2_, ...), custom_call_target="tpu_custom_call" | custom-call | flops 2415919104 | bytes 4456448 | tf_op jit(solution)/shard_map/wgrad/pallas_call | solution.py:331
  97.8 2.0 %wgrad.2.keep_ref = bf16[4,128,768]{2,1,0:T(8,128)(2,1)S(1)} custom-call(bf16[4,256,1024]{2,1,0:T(8,128)(2,1)S(1)} %copy-done.4, bf16[256,256]{1,0:T(8,128)(2,1)S(1)} %get-tuple-element.33.refs_0_.gq_ref, bf16[256,256]{1,0:T(8,128)(2,1)S(1)} %collective-permute-done.12.refs_1_.rest_0_, bf16[256,256]{1,0:T(8,128)(2,1)S(1)} %collective-permute-done.13.refs_2_.rest_2_, ...), custom_call_target="tpu_custom_call" | custom-call | flops 2415919104 | bytes 4456448 | tf_op jit(solution)/shard_map/wgrad/pallas_call | solution.py:331
  100.2 2.0 %collective-permute-start.19 = (bf16[128,768]{1,0:T(8,128)(2,1)S(1)}, bf16[128,768]{1,0:T(8,128)(2,1)S(1)}, u32[]{:S(2)}, u32[]{:S(2)}) collective-permute-start(bf16[128,768]{1,0:T(8,128)(2,1)S(1)} %get-tuple-element.36), channel_id=1, source_target_pairs={{0,64},{16,80},{32,96},{48,112},{64,128},{80,144},{96,160},{112,17... | collective-permute-start | bytes 589832 | tf_op jit(solution)/shard_map/ppermute | solution.py:448
  102.2 2.0 %collective-permute-start.20 = (bf16[128,768]{1,0:T(8,128)(2,1)S(1)}, bf16[128,768]{1,0:T(8,128)(2,1)S(1)}, u32[]{:S(2)}, u32[]{:S(2)}) collective-permute-start(bf16[128,768]{1,0:T(8,128)(2,1)S(1)} %get-tuple-element.37), channel_id=1, source_target_pairs={{0,128},{16,144},{32,160},{48,176},{64,192},{80,208},{96,224},{112... | collective-permute-start | bytes 589832 | tf_op jit(solution)/shard_map/ppermute | solution.py:448
  104.2 9.3 %all-to-all-done.3.terms_ref = bf16[4,2,512,256]{3,2,1,0:T(8,128)(2,1)} async-done(((bf16[4,2,512,256]{3,2,1,0:T(8,128)(2,1)}), bf16[4,2,512,256]{3,2,1,0:T(8,128)(2,1)}, u32[]{:S(2)}, u32[]{:S(2)}) %all-to-all-start.3) | async-done | bytes 2097184 | tf_op jit(solution)/shard_map/all_to_all | solution.py:500
  113.5 1.8 %join.1 = (f32[512,256]{1,0:T(8,128)S(1)}, bf16[512,256]{1,0:T(8,128)(2,1)S(1)}) custom-call(bf16[4,2,512,256]{3,2,1,0:T(8,128)(2,1)} %all-to-all-done.3.terms_ref), custom_call_target="tpu_custom_call" | custom-call | flops 4000000000 | bytes 2097152 | tf_op jit(solution)/shard_map/join/pallas_call | solution.py:407
  115.4 5.4 %collective-permute-start.22 = (bf16[512,256]{1,0:T(8,128)(2,1)S(1)}, bf16[512,256]{1,0:T(8,128)(2,1)S(1)}, u32[]{:S(2)}, u32[]{:S(2)}) collective-permute-start(bf16[512,256]{1,0:T(8,128)(2,1)S(1)} %get-tuple-element.43), channel_id=1, source_target_pairs={{0,8},{2,10},{4,12},{6,14},{8,0},{10,2},{12,4},{14,6},{1,9},{3,11}... | collective-permute-start | bytes 786440 | tf_op jit(solution)/shard_map/ppermute | solution.py:458
  120.8 1.8 %collective-permute-done.21.c_ref = bf16[128,768]{1,0:T(8,128)(2,1)S(1)} collective-permute-done((bf16[128,768]{1,0:T(8,128)(2,1)S(1)}, bf16[128,768]{1,0:T(8,128)(2,1)S(1)}, u32[]{:S(2)}, u32[]{:S(2)}) %collective-permute-start.21) | collective-permute-done | bytes 196640 | tf_op jit(solution)/shard_map/ppermute | solution.py:448
  122.6 0.8 finish.1
  123.4 13.0 %collective-permute-done.22 = bf16[512,256]{1,0:T(8,128)(2,1)S(1)} collective-permute-done((bf16[512,256]{1,0:T(8,128)(2,1)S(1)}, bf16[512,256]{1,0:T(8,128)(2,1)S(1)}, u32[]{:S(2)}, u32[]{:S(2)}) %collective-permute-start.22) | collective-permute-done | bytes 262176 | tf_op jit(solution)/shard_map/ppermute | solution.py:458
  136.4 0.8 fusion
  (37 shorter events, 0.8 us)
Async XLA Ops:
  0.6 0.9 copy-start.5
  7.0 11.4 %collective-permute-start = (bf16[64,1024]{1,0:T(8,128)(2,1)S(1)}, bf16[64,1024]{1,0:T(8,128)(2,1)S(1)}, u32[]{:S(2)}, u32[]{:S(2)}) collective-permute-start(bf16[64,1024]{1,0:T(8,128)(2,1)S(1)} %get-tuple-element.27), channel_id=1, source_target_pairs={{0,16},{16,32},{32,48},{48,0},{64,80},{80,96},{96,112},{112,64},{1... | collective-permute-start | bytes 393224 | tf_op jit(solution)/shard_map/ppermute | solution.py:443
  8.6 9.8 %collective-permute-start.1 = (bf16[64,1024]{1,0:T(8,128)(2,1)S(1)}, bf16[64,1024]{1,0:T(8,128)(2,1)S(1)}, u32[]{:S(2)}, u32[]{:S(2)}) collective-permute-start(bf16[64,1024]{1,0:T(8,128)(2,1)S(1)} %get-tuple-element.28), channel_id=1, source_target_pairs={{0,32},{16,48},{32,0},{48,16},{64,96},{80,112},{96,64},{112,80},{1... | collective-permute-start | bytes 393224 | tf_op jit(solution)/shard_map/ppermute | solution.py:443
  11.3 7.1 %collective-permute-start.2 = (bf16[64,1024]{1,0:T(8,128)(2,1)S(1)}, bf16[64,1024]{1,0:T(8,128)(2,1)S(1)}, u32[]{:S(2)}, u32[]{:S(2)}) collective-permute-start(bf16[64,1024]{1,0:T(8,128)(2,1)S(1)} %get-tuple-element.29), channel_id=1, source_target_pairs={{0,48},{16,0},{32,16},{48,32},{64,112},{80,64},{96,80},{112,96},{1... | collective-permute-start | bytes 393224 | tf_op jit(solution)/shard_map/ppermute | solution.py:443
  12.7 19.3 %all-to-all-start = ((bf16[16,16,1024]{2,1,0:T(8,128)(2,1)}), bf16[16,16,1024]{2,1,0:T(8,128)(2,1)S(1)}, u32[]{:S(2)}, u32[]{:S(2)}) async-start(bf16[16,16,1024]{2,1,0:T(8,128)(2,1)} %bitcast.4), calls=%async_computation | async-start | bytes 1048576 | tf_op jit(solution)/shard_map/all_to_all | solution.py:480
  18.3 13.7 %copy-start.6 = (s32[1,16]{1,0:T(1,128)S(1)}, s32[1,16]{1,0:T(1,128)}, u32[]{:S(2)}) copy-start(s32[1,16]{1,0:T(1,128)} %param.12) | copy-start | bytes 196
  18.3 13.7 %copy-start.7 = (s32[1,16]{1,0:T(1,128)S(1)}, s32[1,16]{1,0:T(1,128)}, u32[]{:S(2)}) copy-start(s32[1,16]{1,0:T(1,128)} %param.13) | copy-start | bytes 196
  18.4 20.5 %collective-permute-start.5 = (bf16[3,64,1024]{2,1,0:T(8,128)(2,1)S(1)}, bf16[3,64,1024]{2,1,0:T(8,128)(2,1)S(1)}, u32[]{:S(2)}, u32[]{:S(2)}) collective-permute-start(bf16[3,64,1024]{2,1,0:T(8,128)(2,1)S(1)} %stack.21.refs_0_.rest_0_), channel_id=1, source_target_pairs={{0,6},{2,0},{4,2},{6,4},{8,14},{10,8},{12,10},{14,12},{1,7},{3,1},... | collective-permute-start | bytes 1179656 | tf_op jit(solution)/shard_map/ppermute | solution.py:453
  18.9 20.0 %collective-permute-start.4 = (bf16[3,64,1024]{2,1,0:T(8,128)(2,1)S(1)}, bf16[3,64,1024]{2,1,0:T(8,128)(2,1)S(1)}, u32[]{:S(2)}, u32[]{:S(2)}) collective-permute-start(bf16[3,64,1024]{2,1,0:T(8,128)(2,1)S(1)} %stack.21.refs_0_.rest_0_), channel_id=1, source_target_pairs={{0,4},{2,6},{4,0},{6,2},{8,12},{10,14},{12,8},{14,10},{1,5},{3,7},... | collective-permute-start | bytes 1179656 | tf_op jit(solution)/shard_map/ppermute | solution.py:453
  21.5 17.4 %collective-permute-start.3 = (bf16[3,64,1024]{2,1,0:T(8,128)(2,1)S(1)}, bf16[3,64,1024]{2,1,0:T(8,128)(2,1)S(1)}, u32[]{:S(2)}, u32[]{:S(2)}) collective-permute-start(bf16[3,64,1024]{2,1,0:T(8,128)(2,1)S(1)} %stack.21.refs_0_.rest_0_), channel_id=1, source_target_pairs={{0,2},{2,4},{4,6},{6,0},{8,10},{10,12},{12,14},{14,8},{1,3},{3,5},... | collective-permute-start | bytes 1179656 | tf_op jit(solution)/shard_map/ppermute | solution.py:453
  33.5 18.7 %all-to-all-start.2 = ((bf16[16,2,16,512]{3,2,1,0:T(8,128)(2,1)}), bf16[16,2,16,512]{3,2,1,0:T(8,128)(2,1)S(1)}, u32[]{:S(2)}, u32[]{:S(2)}) async-start(bf16[16,2,16,512]{3,2,1,0:T(8,128)(2,1)} %pick.3), calls=%async_computation.2 | async-start | bytes 1048576 | tf_op jit(solution)/shard_map/all_to_all | solution.py:480
  40.5 1.4 copy-start.3
  41.9 42.2 %copy-start = (bf16[4096,256]{1,0:T(8,128)(2,1)S(1)}, bf16[4096,256]{1,0:T(8,128)(2,1)}, u32[]{:S(2)}) copy-start(bf16[4096,256]{1,0:T(8,128)(2,1)} %wq_ref.3) | copy-start | bytes 6291460
  52.2 21.9 %all-to-all-start.1 = ((bf16[16,2,16,512]{3,2,1,0:T(8,128)(2,1)}), bf16[16,2,16,512]{3,2,1,0:T(8,128)(2,1)S(1)}, u32[]{:S(2)}, u32[]{:S(2)}) async-start(bf16[16,2,16,512]{3,2,1,0:T(8,128)(2,1)} %pick.2), calls=%async_computation.1 | async-start | bytes 1048576 | tf_op jit(solution)/shard_map/all_to_all | solution.py:480
  60.3 6.8 %collective-permute-start.8 = (f32[8,256]{1,0:T(8,128)S(1)}, f32[8,256]{1,0:T(8,128)S(1)}, u32[]{:S(2)}, u32[]{:S(2)}) collective-permute-start(f32[8,256]{1,0:T(8,128)S(1)} %get-tuple-element.30), channel_id=1, source_target_pairs={{0,48},{16,0},{32,16},{48,32},{64,112},{80,64},{96,80},{112,96},{1... | collective-permute-start | bytes 24584 | tf_op jit(solution)/shard_map/ppermute | solution.py:443
  63.1 5.2 %collective-permute-start.7 = (f32[8,256]{1,0:T(8,128)S(1)}, f32[8,256]{1,0:T(8,128)S(1)}, u32[]{:S(2)}, u32[]{:S(2)}) collective-permute-start(f32[8,256]{1,0:T(8,128)S(1)} %get-tuple-element.30), channel_id=1, source_target_pairs={{0,32},{16,48},{32,0},{48,16},{64,96},{80,112},{96,64},{112,80},{1... | collective-permute-start | bytes 24584 | tf_op jit(solution)/shard_map/ppermute | solution.py:443
  63.9 4.9 %collective-permute-start.6 = (f32[8,256]{1,0:T(8,128)S(1)}, f32[8,256]{1,0:T(8,128)S(1)}, u32[]{:S(2)}, u32[]{:S(2)}) collective-permute-start(f32[8,256]{1,0:T(8,128)S(1)} %get-tuple-element.30), channel_id=1, source_target_pairs={{0,16},{16,32},{32,48},{48,0},{64,80},{80,96},{96,112},{112,64},{1... | collective-permute-start | bytes 24584 | tf_op jit(solution)/shard_map/ppermute | solution.py:443
  64.8 16.7 %collective-permute-start.14 = (bf16[256,256]{1,0:T(8,128)(2,1)S(1)}, bf16[256,256]{1,0:T(8,128)(2,1)S(1)}, u32[]{:S(2)}, u32[]{:S(2)}) collective-permute-start(bf16[256,256]{1,0:T(8,128)(2,1)S(1)} %get-tuple-element.33.refs_0_.gq_ref), channel_id=1, source_target_pairs={{0,48},{16,0},{32,16},{48,32},{64,112},{80,64},{96,80},{112,96},{1... | collective-permute-start | bytes 393224 | tf_op jit(solution)/shard_map/ppermute | solution.py:443
  68.8 5.3 %collective-permute-start.11 = (f32[4,8,256]{2,1,0:T(8,128)S(1)}, f32[4,8,256]{2,1,0:T(8,128)S(1)}, u32[]{:S(2)}, u32[]{:S(2)}) collective-permute-start(f32[4,8,256]{2,1,0:T(8,128)S(1)} %pad_maximum_fusion.rest_0_), channel_id=1, source_target_pairs={{0,192},{16,208},{32,224},{48,240},{64,0},{80,16},{96,32},{112,48}... | collective-permute-start | bytes 98312 | tf_op jit(solution)/shard_map/ppermute | solution.py:448
  69.4 5.5 %collective-permute-start.10 = (f32[4,8,256]{2,1,0:T(8,128)S(1)}, f32[4,8,256]{2,1,0:T(8,128)S(1)}, u32[]{:S(2)}, u32[]{:S(2)}) collective-permute-start(f32[4,8,256]{2,1,0:T(8,128)S(1)} %pad_maximum_fusion.rest_0_), channel_id=1, source_target_pairs={{0,128},{16,144},{32,160},{48,176},{64,192},{80,208},{96,224},{112... | collective-permute-start | bytes 98312 | tf_op jit(solution)/shard_map/ppermute | solution.py:448
  72.6 3.9 %collective-permute-start.9 = (f32[4,8,256]{2,1,0:T(8,128)S(1)}, f32[4,8,256]{2,1,0:T(8,128)S(1)}, u32[]{:S(2)}, u32[]{:S(2)}) collective-permute-start(f32[4,8,256]{2,1,0:T(8,128)S(1)} %pad_maximum_fusion.rest_0_), channel_id=1, source_target_pairs={{0,64},{16,80},{32,96},{48,112},{64,128},{80,144},{96,160},{112,17... | collective-permute-start | bytes 98312 | tf_op jit(solution)/shard_map/ppermute | solution.py:448
  72.6 10.0 %collective-permute-start.13 = (bf16[256,256]{1,0:T(8,128)(2,1)S(1)}, bf16[256,256]{1,0:T(8,128)(2,1)S(1)}, u32[]{:S(2)}, u32[]{:S(2)}) collective-permute-start(bf16[256,256]{1,0:T(8,128)(2,1)S(1)} %get-tuple-element.33.refs_0_.gq_ref), channel_id=1, source_target_pairs={{0,32},{16,48},{32,0},{48,16},{64,96},{80,112},{96,64},{112,80},{1... | collective-permute-start | bytes 393224 | tf_op jit(solution)/shard_map/ppermute | solution.py:443
  74.1 10.0 %collective-permute-start.12 = (bf16[256,256]{1,0:T(8,128)(2,1)S(1)}, bf16[256,256]{1,0:T(8,128)(2,1)S(1)}, u32[]{:S(2)}, u32[]{:S(2)}) collective-permute-start(bf16[256,256]{1,0:T(8,128)(2,1)S(1)} %get-tuple-element.33.refs_0_.gq_ref), channel_id=1, source_target_pairs={{0,16},{16,32},{32,48},{48,0},{64,80},{80,96},{96,112},{112,64},{1... | collective-permute-start | bytes 393224 | tf_op jit(solution)/shard_map/ppermute | solution.py:443
  79.7 15.9 %collective-permute-start.17 = (bf16[256,512]{1,0:T(8,128)(2,1)S(1)}, bf16[256,512]{1,0:T(8,128)(2,1)S(1)}, u32[]{:S(2)}, u32[]{:S(2)}) collective-permute-start(bf16[256,512]{1,0:T(8,128)(2,1)S(1)} %get-tuple-element.34.refs_4_.gkv_ref), channel_id=1, source_target_pairs={{0,48},{16,0},{32,16},{48,32},{64,112},{80,64},{96,80},{112,96},{1... | collective-permute-start | bytes 786440 | tf_op jit(solution)/shard_map/ppermute | solution.py:443
  80.5 15.1 %collective-permute-start.16 = (bf16[256,512]{1,0:T(8,128)(2,1)S(1)}, bf16[256,512]{1,0:T(8,128)(2,1)S(1)}, u32[]{:S(2)}, u32[]{:S(2)}) collective-permute-start(bf16[256,512]{1,0:T(8,128)(2,1)S(1)} %get-tuple-element.34.refs_4_.gkv_ref), channel_id=1, source_target_pairs={{0,32},{16,48},{32,0},{48,16},{64,96},{80,112},{96,64},{112,80},{1... | collective-permute-start | bytes 786440 | tf_op jit(solution)/shard_map/ppermute | solution.py:443
  81.4 14.2 %collective-permute-start.15 = (bf16[256,512]{1,0:T(8,128)(2,1)S(1)}, bf16[256,512]{1,0:T(8,128)(2,1)}, u32[]{:S(2)}, u32[]{:S(2)}) collective-permute-start(bf16[256,512]{1,0:T(8,128)(2,1)S(1)} %get-tuple-element.34.refs_4_.gkv_ref), channel_id=1, source_target_pairs={{0,16},{16,32},{32,48},{48,0},{64,80},{80,96},{96,112},{112,64},{1... | collective-permute-start | bytes 786440 | tf_op jit(solution)/shard_map/ppermute | solution.py:443
  84.1 1.6 %copy-start.1 = (bf16[4096,256]{1,0:T(8,128)(2,1)S(1)}, bf16[4096,256]{1,0:T(8,128)(2,1)}, u32[]{:S(2)}) copy-start(bf16[4096,256]{1,0:T(8,128)(2,1)} %wk_ref.3) | copy-start | bytes 6291460
  85.7 1.6 %copy-start.2 = (bf16[4096,256]{1,0:T(8,128)(2,1)S(1)}, bf16[4096,256]{1,0:T(8,128)(2,1)}, u32[]{:S(2)}) copy-start(bf16[4096,256]{1,0:T(8,128)(2,1)} %wv_ref.3) | copy-start | bytes 6291460
  90.5 5.1 %copy-start.4 = (bf16[4,256,1024]{2,1,0:T(8,128)(2,1)S(1)}, bf16[4,256,1024]{2,1,0:T(8,128)(2,1)}, u32[]{:S(2)}) copy-start(bf16[4,256,1024]{2,1,0:T(8,128)(2,1)} %copy-done.3) | copy-start | bytes 6291460
  90.5 23.0 %all-to-all-start.3 = ((bf16[4,2,512,256]{3,2,1,0:T(8,128)(2,1)}), bf16[4,2,512,256]{3,2,1,0:T(8,128)(2,1)}, u32[]{:S(2)}, u32[]{:S(2)}) async-start(bf16[4,2,512,256]{3,2,1,0:T(8,128)(2,1)} %xgrad.1), calls=%async_computation.3 | async-start | bytes 4194304 | tf_op jit(solution)/shard_map/all_to_all | solution.py:500
  97.7 2.4 %collective-permute-start.18 = (bf16[4,128,768]{2,1,0:T(8,128)(2,1)S(1)}, bf16[4,128,768]{2,1,0:T(8,128)(2,1)S(1)}, u32[]{:S(2)}, u32[]{:S(2)}) collective-permute-start(bf16[4,128,768]{2,1,0:T(8,128)(2,1)S(1)} %wgrad.3), channel_id=1, source_target_pairs={{0,1},{1,0},{2,3},{3,2},{4,5},{5,4},{6,7},{7,6},{8,9},{9,8},{10,11... | collective-permute-start | bytes 2359304 | tf_op jit(solution)/shard_map/ppermute | solution.py:462
  100.2 20.5 %collective-permute-start.19 = (bf16[128,768]{1,0:T(8,128)(2,1)S(1)}, bf16[128,768]{1,0:T(8,128)(2,1)S(1)}, u32[]{:S(2)}, u32[]{:S(2)}) collective-permute-start(bf16[128,768]{1,0:T(8,128)(2,1)S(1)} %get-tuple-element.36), channel_id=1, source_target_pairs={{0,64},{16,80},{32,96},{48,112},{64,128},{80,144},{96,160},{112,17... | collective-permute-start | bytes 589832 | tf_op jit(solution)/shard_map/ppermute | solution.py:448
  102.2 18.5 %collective-permute-start.20 = (bf16[128,768]{1,0:T(8,128)(2,1)S(1)}, bf16[128,768]{1,0:T(8,128)(2,1)S(1)}, u32[]{:S(2)}, u32[]{:S(2)}) collective-permute-start(bf16[128,768]{1,0:T(8,128)(2,1)S(1)} %get-tuple-element.37), channel_id=1, source_target_pairs={{0,128},{16,144},{32,160},{48,176},{64,192},{80,208},{96,224},{112... | collective-permute-start | bytes 589832 | tf_op jit(solution)/shard_map/ppermute | solution.py:448
  104.2 18.4 %collective-permute-start.21 = (bf16[128,768]{1,0:T(8,128)(2,1)S(1)}, bf16[128,768]{1,0:T(8,128)(2,1)S(1)}, u32[]{:S(2)}, u32[]{:S(2)}) collective-permute-start(bf16[128,768]{1,0:T(8,128)(2,1)S(1)} %get-tuple-element.38), channel_id=1, source_target_pairs={{0,192},{16,208},{32,224},{48,240},{64,0},{80,16},{96,32},{112,48}... | collective-permute-start | bytes 589832 | tf_op jit(solution)/shard_map/ppermute | solution.py:448
  115.4 21.0 %collective-permute-start.22 = (bf16[512,256]{1,0:T(8,128)(2,1)S(1)}, bf16[512,256]{1,0:T(8,128)(2,1)S(1)}, u32[]{:S(2)}, u32[]{:S(2)}) collective-permute-start(bf16[512,256]{1,0:T(8,128)(2,1)S(1)} %get-tuple-element.43), channel_id=1, source_target_pairs={{0,8},{2,10},{4,12},{6,14},{8,0},{10,2},{12,4},{14,6},{1,9},{3,11}... | collective-permute-start | bytes 786440 | tf_op jit(solution)/shard_map/ppermute | solution.py:458
